TPU v7x, 32 devices: a whole 2x2x4 slice. The times are simulated.
32 devices in a mesh: dp: 4 (over z), row: 2 (over x), col: 4 (over y, core).
Axes of the slice: x: 2, y: 2, z: 4, core: 2. Of those that a mesh axis runs over, the one named last changes fastest.
Arguments:
- residual_in: bfloat16 [8192, 2048], P(('dp', 'col'), 'row'), may hold values from -6 to 6
- attn_gain: float32 [2048], P('row'), may hold values from 0.5 to 1.5
- attn_shift: float32 [2048], P('row'), may hold values from -1.75 to 1.75
- mlp_gain: float32 [2048], P('row'), may hold values from 0.5 to 1.5
- mlp_shift: float32 [2048], P('row'), may hold values from -1.75 to 1.75
- qkv_weight: bfloat16 [2048, 8, 768], P('row', 'col'), may hold values from -0.125 to 0.125
- qkv_bias: float32 [8, 768], P('col'), may hold values from -1.75 to 1.75
- dense_weight: bfloat16 [8, 256, 2048], P('col', None, 'row'), may hold values from -1 to 1
- dense_bias: float32 [2048], P('row'), may hold values from -1.75 to 1.75
- in_weight: bfloat16 [2048, 8192], P('row', 'col'), may hold values from -1 to 1
- in_bias: float32 [8192], P('col'), may hold values from -1.75 to 1.75
- out_weight: bfloat16 [8192, 2048], P('col', 'row'), may hold values from -0.0625 to 0.0625
- out_bias: float32 [2048], P('row'), may hold values from -1.75 to 1.75
- cotangent: bfloat16 [8192, 2048], P(('dp', 'col'), 'row'), may hold values from -6 to 6
Outputs:
- block_out: bfloat16 [8192, 2048], P(('dp', 'col'), 'row')
- input_grad: float32 [8192, 2048], P(('dp', 'col'), 'row')
- attn_gain_grad: float32 [2048], P('row')
- attn_shift_grad: float32 [2048], P('row')
- mlp_gain_grad: float32 [2048], P('row')
- mlp_shift_grad: float32 [2048], P('row')
- qkv_weight_grad: float32 [2048, 8, 768], P('row', 'col')
- qkv_bias_grad: float32 [8, 768], P('col')
- dense_weight_grad: float32 [8, 256, 2048], P('col', None, 'row')
- dense_bias_grad: float32 [2048], P('row')
- in_weight_grad: float32 [2048, 8192], P('row', 'col')
- in_bias_grad: float32 [8192], P('col')
- out_weight_grad: float32 [8192, 2048], P('col', 'row')
- out_bias_grad: float32 [2048], P('row')
All inputs are finite; a program needn't handle non-finite values.
Results may differ from a plain program's by a relative error of at most 0.011.
Values may be sent and summed in bfloat16 or wider, within the bound.
No kernel may reach another device: no remote copies, remote signals or barrier semaphores. Data moves between devices by JAX's collectives and lax.ppermute only.
A program may use at most 256 MiB of HBM per device.

v0:
```python
import math

import jax
import jax.numpy as jnp
from jax import lax
from jax.sharding import PartitionSpec as P

HS = 256
ROT = 64
LENGTH = 2048
QBLOCK = 512


EPSILON = 1e-05
ROPE_BASE = 10000.0
NEGATIVE = -1e30


def angle_tables(count):
    half_rot = ROT // 2
    position = (jnp.arange(count) % LENGTH).astype(jnp.float32)
    frequency = ROPE_BASE ** (-(2.0 * jnp.arange(half_rot).astype(jnp.float32)) / ROT)
    angles = position[:, None] * frequency[None, :]
    return (jnp.cos(angles)[:, None, :], jnp.sin(angles)[:, None, :])


def rotate(values, cos_table, sin_table):
    half_rot = ROT // 2
    lower_half = values[..., :half_rot]
    upper_half = values[..., half_rot:ROT]
    return jnp.concatenate(
        [
            lower_half * cos_table - upper_half * sin_table,
            upper_half * cos_table + lower_half * sin_table,
            values[..., ROT:],
        ],
        -1,
    )


def unrotate(grad_rows, cos_table, sin_table):
    half_rot = ROT // 2
    lower_half = grad_rows[..., :half_rot]
    upper_half = grad_rows[..., half_rot:ROT]
    return jnp.concatenate(
        [
            lower_half * cos_table + upper_half * sin_table,
            upper_half * cos_table - lower_half * sin_table,
            grad_rows[..., ROT:],
        ],
        -1,
    )


def gelu_slope(values):
    return 0.5 * (1.0 + lax.erf(values * 2.0 ** (-0.5))) + values * jnp.exp(
        -0.5 * values * values
    ) * (2.0 * math.pi) ** (-0.5)


def block_scores(query_blk, key_seq, start):
    raw_scores = jnp.einsum(
        "qhe,khe->hqk", query_blk, key_seq, preferred_element_type=jnp.float32
    ) * HS ** (-0.5)
    query_pos = start + jnp.arange(query_blk.shape[0])
    key_pos = jnp.arange(key_seq.shape[0])
    causal_mask = key_pos[None, :] <= query_pos[:, None]
    return jnp.where(causal_mask[None], raw_scores, NEGATIVE)


def attend_forward(query_rows, key_rows, value_rows):
    total_rows, heads_here, _ = query_rows.shape
    seq_count = total_rows // LENGTH
    blocks = LENGTH // QBLOCK
    query_split = query_rows.reshape(seq_count, blocks, QBLOCK, heads_here, HS)
    key_split = key_rows.reshape(seq_count, LENGTH, heads_here, HS)
    value_split = value_rows.reshape(seq_count, LENGTH, heads_here, HS)

    def one_sequence(pieces):
        query_seq, key_seq, value_seq = pieces

        def one_block(inputs):
            query_blk, block_index = inputs
            scores = block_scores(query_blk, key_seq, block_index * QBLOCK)
            row_max = jnp.max(scores, -1, keepdims=True)
            exp_scores = jnp.exp(scores - row_max)
            exp_total = jnp.sum(exp_scores, -1, keepdims=True)
            prob_rows = (exp_scores / exp_total).astype(jnp.bfloat16)
            output = jnp.einsum(
                "hqk,khe->qhe", prob_rows, value_seq, preferred_element_type=jnp.float32
            )
            return (output, (row_max + jnp.log(exp_total))[..., 0])

        return lax.map(one_block, (query_seq, jnp.arange(blocks)))

    output, logsum = lax.map(one_sequence, (query_split, key_split, value_split))
    return (output.reshape(total_rows, heads_here, HS), logsum)


def attend_backward(query_rows, key_rows, value_rows, out_grad, logsum):
    total_rows, heads_here, _ = query_rows.shape
    seq_count = total_rows // LENGTH
    blocks = LENGTH // QBLOCK
    query_split = query_rows.reshape(seq_count, blocks, QBLOCK, heads_here, HS)
    grad_split = out_grad.reshape(seq_count, blocks, QBLOCK, heads_here, HS)
    key_split = key_rows.reshape(seq_count, LENGTH, heads_here, HS)
    value_split = value_rows.reshape(seq_count, LENGTH, heads_here, HS)

    def one_sequence(pieces):
        query_seq, key_seq, value_seq, grad_seq, logsum_seq = pieces

        def one_block(carry, inputs):
            key_acc, value_acc = carry
            query_blk, grad_blk, logsum_blk, block_index = inputs
            scores = block_scores(query_blk, key_seq, block_index * QBLOCK)
            prob_rows = jnp.exp(scores - logsum_blk[..., None])
            prob_grad = jnp.einsum(
                "qhe,khe->hqk", grad_blk, value_seq, preferred_element_type=jnp.float32
            )
            center = jnp.sum(prob_rows * prob_grad, -1, keepdims=True)
            score_grad = (prob_rows * (prob_grad - center)).astype(jnp.bfloat16)
            query_grad = jnp.einsum(
                "hqk,khe->qhe", score_grad, key_seq, preferred_element_type=jnp.float32
            ) * HS ** (-0.5)
            key_acc = key_acc + jnp.einsum(
                "hqk,qhe->khe", score_grad, query_blk, preferred_element_type=jnp.float32
            ) * HS ** (-0.5)
            value_acc = value_acc + jnp.einsum(
                "hqk,qhe->khe",
                prob_rows.astype(jnp.bfloat16),
                grad_blk,
                preferred_element_type=jnp.float32,
            )
            return ((key_acc, value_acc), query_grad)

        zero_acc = jnp.zeros((LENGTH, heads_here, HS), jnp.float32)
        (key_grad, value_grad), query_grad = lax.scan(
            one_block, (zero_acc, zero_acc), (query_seq, grad_seq, logsum_seq, jnp.arange(blocks))
        )
        return (query_grad, key_grad, value_grad)

    query_grad, key_grad, value_grad = lax.map(
        one_sequence, (query_split, key_split, value_split, grad_split, logsum)
    )
    return (
        query_grad.reshape(total_rows, heads_here, HS),
        key_grad.reshape(total_rows, heads_here, HS),
        value_grad.reshape(total_rows, heads_here, HS),
    )


def per_device(
    residual_in,
    attn_gain,
    attn_shift,
    mlp_gain,
    mlp_shift,
    qkv_weight,
    qkv_bias,
    dense_weight,
    dense_bias,
    in_weight,
    in_bias,
    out_weight,
    out_bias,
    cotangent,
):
    full_width = residual_in.shape[1] * lax.axis_size("row")
    row_place = lax.axis_index("row")
    heads_here = qkv_weight.shape[1] // lax.axis_size("row")
    units_here = in_weight.shape[1] // lax.axis_size("row")
    inputs = residual_in.astype(jnp.float32)
    first_sum, square_sum = lax.psum((jnp.sum(inputs, 1), jnp.sum(inputs * inputs, 1)), "row")
    average = first_sum / full_width
    inv_scale = lax.rsqrt(square_sum / full_width - average * average + EPSILON)
    normed = (inputs - average[:, None]) * inv_scale[:, None]
    attn_input = (normed * attn_gain + attn_shift).astype(jnp.bfloat16)
    mlp_input = (normed * mlp_gain + mlp_shift).astype(jnp.bfloat16)
    attn_all, mlp_all = (
        lax.all_gather(attn_input, "col", axis=0, tiled=True),
        lax.all_gather(mlp_input, "col", axis=0, tiled=True),
    )
    packed, pre_act = (
        lax.psum_scatter(
            jnp.einsum("td,dhe->the", attn_all, qkv_weight, preferred_element_type=jnp.float32),
            "row",
            scatter_dimension=1,
            tiled=True,
        ),
        lax.psum_scatter(
            jnp.dot(mlp_all, in_weight, preferred_element_type=jnp.float32),
            "row",
            scatter_dimension=1,
            tiled=True,
        ),
    )
    packed = (
        packed + lax.dynamic_slice_in_dim(qkv_bias, row_place * heads_here, heads_here, 0)[None]
    )
    pre_act = pre_act + lax.dynamic_slice_in_dim(in_bias, row_place * units_here, units_here, 0)
    active = jax.nn.gelu(pre_act, approximate=False).astype(jnp.bfloat16)
    cos_table, sin_table = angle_tables(packed.shape[0])
    query_rows = rotate(packed[..., :HS], cos_table, sin_table).astype(jnp.bfloat16)
    key_rows = rotate(packed[..., HS : 2 * HS], cos_table, sin_table).astype(jnp.bfloat16)
    value_rows = packed[..., 2 * HS :].astype(jnp.bfloat16)
    attended, logsum = attend_forward(query_rows, key_rows, value_rows)
    attended_all, active_all = (
        lax.all_gather(attended.astype(jnp.bfloat16), "row", axis=1, tiled=True),
        lax.all_gather(active, "row", axis=1, tiled=True),
    )
    partial_value = jnp.einsum(
        "the,hed->td", attended_all, dense_weight, preferred_element_type=jnp.float32
    ) + jnp.dot(active_all, out_weight, preferred_element_type=jnp.float32)
    mixed_sum = lax.psum_scatter(partial_value, "col", scatter_dimension=0, tiled=True)
    block_out = (inputs + mixed_sum + dense_bias + out_bias).astype(jnp.bfloat16)
    grad_all = lax.all_gather(cotangent, "col", axis=0, tiled=True)
    shift_out_grad = jnp.sum(grad_all, 0, dtype=jnp.float32)
    dense_grad = jnp.einsum(
        "the,td->hed", attended_all, grad_all, preferred_element_type=jnp.float32
    )
    out_grad_local = jnp.einsum(
        "tf,td->fd", active_all, grad_all, preferred_element_type=jnp.float32
    )
    attended_grad, active_grad = (
        lax.psum_scatter(
            jnp.einsum("td,hed->the", grad_all, dense_weight, preferred_element_type=jnp.float32),
            "row",
            scatter_dimension=1,
            tiled=True,
        ),
        lax.psum_scatter(
            jnp.einsum("td,fd->tf", grad_all, out_weight, preferred_element_type=jnp.float32),
            "row",
            scatter_dimension=1,
            tiled=True,
        ),
    )
    pre_grad = (active_grad * gelu_slope(pre_act)).astype(jnp.bfloat16)
    query_grad, key_grad, value_grad = attend_backward(
        query_rows, key_rows, value_rows, attended_grad.astype(jnp.bfloat16), logsum
    )
    packed_grad = jnp.concatenate(
        [
            unrotate(query_grad, cos_table, sin_table),
            unrotate(key_grad, cos_table, sin_table),
            value_grad,
        ],
        -1,
    ).astype(jnp.bfloat16)
    packed_all, pre_all = (
        lax.all_gather(packed_grad, "row", axis=1, tiled=True),
        lax.all_gather(pre_grad, "row", axis=1, tiled=True),
    )
    qkv_grad_local = jnp.einsum(
        "td,the->dhe", attn_all, packed_all, preferred_element_type=jnp.float32
    )
    qkv_shift_grad = jnp.sum(packed_all, 0, dtype=jnp.float32)
    in_grad_local = jnp.einsum("td,tf->df", mlp_all, pre_all, preferred_element_type=jnp.float32)
    in_shift_grad = jnp.sum(pre_all, 0, dtype=jnp.float32)
    totals = lax.psum(
        (
            qkv_grad_local,
            qkv_shift_grad,
            dense_grad,
            shift_out_grad,
            in_grad_local,
            in_shift_grad,
            out_grad_local,
        ),
        "dp",
    )
    attn_in_grad, mlp_in_grad = (
        lax.psum_scatter(
            jnp.einsum("the,dhe->td", packed_all, qkv_weight, preferred_element_type=jnp.float32),
            "col",
            scatter_dimension=0,
            tiled=True,
        ),
        lax.psum_scatter(
            jnp.einsum("tf,df->td", pre_all, in_weight, preferred_element_type=jnp.float32),
            "col",
            scatter_dimension=0,
            tiled=True,
        ),
    )
    norm_totals = lax.psum(
        (
            jnp.sum(attn_in_grad * normed, 0),
            jnp.sum(attn_in_grad, 0),
            jnp.sum(mlp_in_grad * normed, 0),
            jnp.sum(mlp_in_grad, 0),
        ),
        ("dp", "col"),
    )
    normed_grad = attn_in_grad * attn_gain + mlp_in_grad * mlp_gain
    grad_sum, grad_dot = lax.psum(
        (jnp.sum(normed_grad, 1), jnp.sum(normed_grad * normed, 1)), "row"
    )
    input_grad = cotangent.astype(jnp.float32) + inv_scale[:, None] * (
        normed_grad - grad_sum[:, None] / full_width - normed * (grad_dot[:, None] / full_width)
    )
    return (
        block_out,
        input_grad,
        norm_totals[0],
        norm_totals[1],
        norm_totals[2],
        norm_totals[3],
        totals[0],
        totals[1],
        totals[2],
        totals[3],
        totals[4],
        totals[5],
        totals[6],
        totals[3],
    )


def solution(mesh):
    in_specs = (
        P(("dp", "col"), "row"),
        P("row"),
        P("row"),
        P("row"),
        P("row"),
        P("row", "col", None),
        P("col", None),
        P("col", None, "row"),
        P("row"),
        P("row", "col"),
        P("col"),
        P("col", "row"),
        P("row"),
        P(("dp", "col"), "row"),
    )
    out_specs = (
        P(("dp", "col"), "row"),
        P(("dp", "col"), "row"),
        P("row"),
        P("row"),
        P("row"),
        P("row"),
        P("row", "col", None),
        P("col", None),
        P("col", None, "row"),
        P("row"),
        P("row", "col"),
        P("col"),
        P("col", "row"),
        P("row"),
    )
    return jax.shard_map(
        per_device, mesh=mesh, in_specs=in_specs, out_specs=out_specs, check_vma=False
    )
```

profile of v0, /device:TPU:0, one launch (start us, length us, event | category | flops | bytes accessed | tf_op | source)
XLA Modules:
  0.0 2133.2 jit_solution(17255416018816586509)
XLA Ops:
  20.2 26.6 %all-gather.16.cloned.1.call-done = bf16[2048,1024]{1,0:T(8,128)(2,1)} async-done(((bf16[512,1024]{1,0:T(8,128)(2,1)}), bf16[2048,1024]{1,0:T(8,128)(2,1)}) %all-gather.16.cloned.1.call-update) | async-done | bytes 4194320 | tf_op jit(solution)/shard_map/all_gather | solution.py:216
  53.8 29.7 %all-gather.8.cloned.1.call-done = bf16[2048,1024]{1,0:T(8,128)(2,1)} async-done(((bf16[512,1024]{1,0:T(8,128)(2,1)}), bf16[2048,1024]{1,0:T(8,128)(2,1)}) %all-gather.8.cloned.1.call-update) | async-done | bytes 4194320 | tf_op jit(solution)/shard_map/all_gather | solution.py:180
  95.1 25.1 %all-gather.12.cloned.1.call-done = bf16[2048,1024]{1,0:T(8,128)(2,1)} async-done(((bf16[512,1024]{1,0:T(8,128)(2,1)}), bf16[2048,1024]{1,0:T(8,128)(2,1)}) %all-gather.12.cloned.1.call-update) | async-done | bytes 4194320 | tf_op jit(solution)/shard_map/all_gather | solution.py:181
  120.1 15.2 fusion.121
  135.6 15.4 fusion.123
  153.3 23.8 %reduce-scatter.14.cloned.1.call-done = f32[2048,1,256]{2,0,1:T(8,128)} async-done(((f32[2048,2,256]{2,0,1:T(8,128)}), f32[2048,1,256]{2,0,1:T(8,128)}) %reduce-scatter.14.cloned.1.call-update) | async-done | bytes 2097168 | tf_op jit(solution)/shard_map/reduce_scatter | solution.py:225
  179.9 144.1 %reduce-scatter.8.cloned.1.call-done = f32[2048,1,768]{0,2,1:T(8,128)} async-done(((f32[2048,2,768]{0,2,1:T(8,128)}), f32[2048,1,768]{0,2,1:T(8,128)}) %reduce-scatter.8.cloned.1.call-update) | async-done | bytes 6291472 | tf_op jit(solution)/shard_map/reduce_scatter | solution.py:184
  350.0 25.4 %while.49 = (s32[]{:T(128)}, bf16[4,512,1,256]{3,1,2,0:T(8,128)(2,1)}, f32[4,1,512]{2,1,0:T(1,128)S(1)}, s32[4]{0:T(128)S(1)}, bf16[4,512,1,256]{3,1,2,0:T(8,128...) while((s32[]{:T(128)}, ...), condition=%wide.region_8.9_spmd.clone, body=%wide.region_5.8_spmd.sunk.clone | while | flops 1083179008 | bytes 28074200 | solution.py:94
  375.3 46.7 %while.50 = (s32[]{:T(128)}, f32[2048,1,256]{0,2,1:T(8,128)}, f32[2048,1,256]{0,2,1:T(8,128)}, f32[4,512,1,256]{3,1,2,0:T(8,128)}, bf16[4,512,1,256]{3,1,2,0:T(8...) while((s32[]{:T(128)}, f32[2048,1,256]{0,2,1:T(8,128)}, ...), condition=%wide.region_14.15_spmd.clone.clone, body=%wide.region_12.14_spmd.clone.sunk.clone | while | flops 2697592832 | bytes 86522208 | solution.py:137
  461.8 53.5 %reduce-scatter.10.cloned.1.call-done = f32[2048,1024]{1,0:T(8,128)} async-done(((f32[2048,2048]{1,0:T(8,128)}), f32[2048,1024]{1,0:T(8,128)}) %reduce-scatter.10.cloned.1.call-update) | async-done | bytes 8388624 | tf_op jit(solution)/shard_map/reduce_scatter | solution.py:190
  515.3 191.5 %reduce-scatter.18.cloned.1.call-done = f32[2048,1024]{1,0:T(8,128)} async-done(((f32[2048,2048]{1,0:T(8,128)}), f32[2048,1024]{1,0:T(8,128)}) %reduce-scatter.18.cloned.1.call-update) | async-done | bytes 8388624 | tf_op jit(solution)/shard_map/reduce_scatter | solution.py:231
  706.8 24.3 %fusion.39 = (bf16[2048,1024]{1,0:T(8,128)(2,1)}, bf16[2048,1024]{1,0:T(8,128)(2,1)}) fusion(f32[2048,1024]{1,0:T(8,128)} %reduce-scatter.18.cloned.1.call-done, f32[2048,1024]{1,0:T(8,128)} %reduce-scatter.10.cloned.1.call-done, f32[1024]{0:T(1024)S(1)} %dynamic_slice.47), kind=kLoop, calls=%fused_computation.59 | loop fusion | flops 159383552 | bytes 25169920 | tf_op jit(solution)/shard_map/convert_element_type | solution.py:238
  732.5 56.9 %all-gather.18.cloned.1.call-done = bf16[2048,2,768]{2,0,1:T(8,128)(2,1)} async-done(((bf16[2048,1,768]{2,0,1:T(8,128)(2,1)}), bf16[2048,2,768]{2,0,1:T(8,128)(2,1)}) %all-gather.18.cloned.1.call-update) | async-done | bytes 6291472 | tf_op jit(solution)/shard_map/all_gather | solution.py:251
  800.4 95.2 %all-gather.14.cloned.1.call-done = bf16[2048,2048]{1,0:T(8,128)(2,1)} async-done(((bf16[2048,1024]{1,0:T(8,128)(2,1)}), bf16[2048,2048]{1,0:T(8,128)(2,1)}) %all-gather.14.cloned.1.call-update) | async-done | bytes 8388624 | tf_op jit(solution)/shard_map/all_gather | solution.py:209
  895.7 14.5 fusion.122
  910.1 20.7 all-gather.10.cloned.1.call-done
  941.7 95.4 %all-gather.20.cloned.1.call-done = bf16[2048,2048]{1,0:T(8,128)(2,1)} async-done(((bf16[2048,1024]{1,0:T(8,128)(2,1)}), bf16[2048,2048]{1,0:T(8,128)(2,1)}) %all-gather.20.cloned.1.call-update) | async-done | bytes 8388624 | tf_op jit(solution)/shard_map/all_gather | solution.py:252
  1037.1 15.0 fusion.124
  1082.6 11.8 fusion.125
  1105.9 19.5 all-reduce.1
  1125.5 60.9 %reduce-scatter.12.cloned.1.call-done = f32[512,1024]{1,0:T(8,128)} async-done(((f32[2048,1024]{1,0:T(8,128)}), f32[512,1024]{1,0:T(8,128)}) %reduce-scatter.12.cloned.1.call-update) | async-done | bytes 2097168 | tf_op jit(solution)/shard_map/reduce_scatter | solution.py:214
  1186.4 75.0 %reduce-scatter.20.cloned.1.call-done = f32[512,1024]{1,0:T(8,128)} async-done(((f32[2048,1024]{1,0:T(8,128)}), f32[512,1024]{1,0:T(8,128)}) %reduce-scatter.20.cloned.1.call-update) | async-done | bytes 2097168 | tf_op jit(solution)/shard_map/reduce_scatter | solution.py:279
  1271.4 62.8 %all-reduce = (f32[1024]{0:T(1024)}, f32[1024]{0:T(1024)}, f32[1024]{0:T(1024)}, f32[1024]{0:T(1024)}) all-reduce(f32[1024]{0:T(1024)S(1)} %get-tuple-element.372, f32[1024]{0:T(1024)S(1)} %get-tuple-element.373, f32[1024]{0:T(1024)S(1)} %get-tuple-element.300, ...), channel_id=1, replica_groups=mesh['dp'=4,'row'=2,'col'=4] {'dp','col'}, use_global_device_ids=true, to_apply=%region_23.24 | all-reduce | flops 4096 | bytes 32768 | tf_op jit(solution)/shard_map/psum | solution.py:286
  1338.4 763.6 %all-reduce.7.cloned.1.call-done = (f32[1024,2,768]{2,0,1:T(8,128)}, f32[2,256,1024]{2,1,0:T(8,128)}, f32[1024,2048]{1,0:T(8,128)}, f32[2048,1024]{1,0:T(8,128)}) async-done(((f32[1024,2,768]{2,0,1:T(8,128)}, f32[2,256,1024]{2,1,0:T(8,128)}, f32[1024,2048]{1,0:T(8,128)}, f32[2048,1024]{1,0:T(8,128)}), (f32[1024,2,768]{2,0,1:T(8,128)}, f32[2,256,1024]{2,1,0:T(8,128)}, f32[1024,2048]{1,0:T(8,128)}, ...) | async-done | bytes 25165840 | tf_op jit(solution)/shard_map/psum | solution.py:260
  (279 shorter events, 272.2 us)
Async XLA Ops:
  7.2 76.3 %copy-start = (bf16[1024,2,768]{2,1,0:T(2,128)(2,1)S(1)}, bf16[1024,2,768]{2,1,0:T(2,128)(2,1)}, u32[]{:S(2)}) copy-start(bf16[1024,2,768]{2,1,0:T(2,128)(2,1)} %param.23) | copy-start | bytes 9437188
  7.2 39.6 %all-gather.16.cloned.1.call-start = ((), (), s32[]{:S(2)}) async-start(), calls=%async_computation.14 | async-start | bytes 5242880 | tf_op jit(solution)/shard_map/all_gather | solution.py:216
  7.9 75.5 %all-gather.8.cloned.1.call-start = ((), (), s32[]{:S(2)}) async-start(), calls=%async_computation.7 | async-start | bytes 5242880 | tf_op jit(solution)/shard_map/all_gather | solution.py:180
  19.4 100.7 %all-gather.12.cloned.1.call-start = ((), (), s32[]{:S(2)}) async-start(), calls=%async_computation.10 | async-start | bytes 5242880 | tf_op jit(solution)/shard_map/all_gather | solution.py:181
  20.2 157.0 %reduce-scatter.14.cloned.1.call-start = ((), (), s32[]{:S(2)}) async-start(), calls=%async_computation.15 | async-start | bytes 6291456 | tf_op jit(solution)/shard_map/reduce_scatter | solution.py:225
  53.7 270.2 %reduce-scatter.8.cloned.1.call-start = ((), (), s32[]{:S(2)}) async-start(), calls=%async_computation.8 | async-start | bytes 18874368 | tf_op jit(solution)/shard_map/reduce_scatter | solution.py:184
  95.0 420.3 %reduce-scatter.10.cloned.1.call-start = ((), (), s32[]{:S(2)}) async-start(), calls=%async_computation.11 | async-start | bytes 25165824 | tf_op jit(solution)/shard_map/reduce_scatter | solution.py:190
  135.4 571.4 %reduce-scatter.18.cloned.1.call-start = ((), (), s32[]{:S(2)}) async-start(), calls=%async_computation.18 | async-start | bytes 25165824 | tf_op jit(solution)/shard_map/reduce_scatter | solution.py:231
  151.1 638.3 %all-gather.18.cloned.1.call-start = ((), (), s32[]{:S(2)}) async-start(), calls=%async_computation.16 | async-start | bytes 9437184 | tf_op jit(solution)/shard_map/all_gather | solution.py:251
  461.8 433.9 %all-gather.14.cloned.1.call-start = ((), (), s32[]{:S(2)}) async-start(), calls=%async_computation.12 | async-start | bytes 12582912 | tf_op jit(solution)/shard_map/all_gather | solution.py:209
  731.1 199.7 %all-gather.10.cloned.1.call-start = ((), (), s32[]{:S(2)}) async-start(), calls=%async_computation.9 | async-start | bytes 3145728 | tf_op jit(solution)/shard_map/all_gather | solution.py:208
  731.7 305.4 %all-gather.20.cloned.1.call-start = ((), (), s32[]{:S(2)}) async-start(), calls=%async_computation.19 | async-start | bytes 12582912 | tf_op jit(solution)/shard_map/all_gather | solution.py:252
  732.5 393.0 %reduce-scatter.16.cloned.1.call-start = ((), (), s32[]{:S(2)}) async-start(), calls=%async_computation.17 | async-start | bytes 10485760 | tf_op jit(solution)/shard_map/reduce_scatter | solution.py:273
  800.4 386.0 %reduce-scatter.12.cloned.1.call-start = ((), (), s32[]{:S(2)}) async-start(), calls=%async_computation.13 | async-start | bytes 10485760 | tf_op jit(solution)/shard_map/reduce_scatter | solution.py:214
  941.7 319.7 %reduce-scatter.20.cloned.1.call-start = ((), (), s32[]{:S(2)}) async-start(), calls=%async_computation.20 | async-start | bytes 10485760 | tf_op jit(solution)/shard_map/reduce_scatter | solution.py:279
  1052.1 1049.9 %all-reduce.7.cloned.1.call-start = ((), (), s32[]{:S(2)}) async-start(), calls=%async_computation.21 | async-start | bytes 50331648 | tf_op jit(solution)/shard_map/psum | solution.py:260
  1059.9 22.8 %slice-start = ((s8[8388608]{0:T(1024)(128)(4,1)}), s8[4194304]{0:T(1024)(128)(4,1)S(1)}, s32[]{:S(2)}) async-start(s8[8388608]{0:T(1024)(128)(4,1)} %bitcast.175), calls=%async_computation.22 | async-start | bytes 8388608
  1101.1 160.3 %copy-start.13 = (f32[512]{0:T(512)S(1)}, f32[512]{0:T(512)}, u32[]{:S(2)}) copy-start(f32[512]{0:T(512)} %copy-done.12) | copy-start | bytes 6148
  1101.1 160.3 %copy-start.15 = (f32[512]{0:T(512)S(1)}, f32[512]{0:T(512)}, u32[]{:S(2)}) copy-start(f32[512]{0:T(512)} %copy-done.14) | copy-start | bytes 6148
  1101.1 160.2 %copy-start.16 = (f32[1024]{0:T(1024)S(1)}, f32[1024]{0:T(1024)}, u32[]{:S(2)}) copy-start(f32[1024]{0:T(1024)} %param.19) | copy-start | bytes 12292
  1101.1 160.2 %copy-start.17 = (f32[1024]{0:T(1024)S(1)}, f32[1024]{0:T(1024)}, u32[]{:S(2)}) copy-start(f32[1024]{0:T(1024)} %param.21) | copy-start | bytes 12292
  1101.1 160.2 %copy-start.18 = (f32[1024]{0:T(1024)S(1)}, f32[1024]{0:T(1024)}, u32[]{:S(2)}) copy-start(f32[1024]{0:T(1024)} %param.30) | copy-start | bytes 12292
  1101.1 160.2 %copy-start.19 = (f32[1024]{0:T(1024)S(1)}, f32[1024]{0:T(1024)}, u32[]{:S(2)}) copy-start(f32[1024]{0:T(1024)} %param.26) | copy-start | bytes 12292
  1125.5 987.0 %copy-start.20 = (f32[1024]{0:T(1024)}, f32[1024]{0:T(1024)S(1)}, u32[]{:S(2)}) copy-start(f32[1024]{0:T(1024)S(1)} %get-tuple-element.646) | copy-start | bytes 12292
  (51 other events, 217.2 us)
Sparse Core Ops, SparseCore 0:
  9.6 37.1 all-gather.15
  48.9 34.4 all-gather.7
  85.6 34.4 all-gather.11
  122.8 54.2 reduce-scatter.13
  179.4 144.4 reduce-scatter.7
  326.2 189.1 reduce-scatter.9
  517.6 189.1 reduce-scatter.17
  709.0 80.3 all-gather.17
  791.6 103.9 all-gather.13
  897.7 33.1 all-gather.9
  933.0 103.9 all-gather.19
  1040.3 71.7 reduce-scatter.15
  1114.6 71.6 reduce-scatter.11
  1189.5 71.7 reduce-scatter.19
  1264.7 837.2 all-reduce.6
where the time goes:
time: 2140 us; the launch traced here: 2130 us
  waiting for transfers between devices  1660 us (78%)
  matrix products  190 us (9%)
  blocking collectives  93.1 us (4%)
  local copies, waits for them, and re-layouts  89.8 us (4%)
  other arithmetic  73.8 us (3%)
    psum x1, waiting for transfers between devices, per_device(): lax.psum((qkv_grad_local, qkv_shift_grad, dense_grad, shift_out_grad, in_...  764 us
    reduce_scatter x1, waiting for transfers between devices, per_device(): lax.psum_scatter(jnp.einsum('td,fd->tf', grad_all, out_weight, preferred_...  191 us
    reduce_scatter x1, waiting for transfers between devices, per_device(): lax.psum_scatter(jnp.einsum('td,dhe->the', attn_all, qkv_weight, preferre...  144 us
    all_gather x1, waiting for transfers between devices, per_device(): lax.all_gather(pre_grad, 'row', axis=1, tiled=True)  95.4 us
    all_gather x1, waiting for transfers between devices, per_device(): lax.all_gather(active, 'row', axis=1, tiled=True)  95.2 us
    reduce_scatter x1, waiting for transfers between devices, per_device(): lax.psum_scatter(jnp.einsum('tf,df->td', pre_all, in_weight, preferred_el...  75 us
    psum x1, blocking collectives, per_device(): lax.psum((jnp.sum(attn_in_grad * normed, 0), jnp.sum(attn_in_grad, 0), jn...  62.8 us
    reduce_scatter x1, waiting for transfers between devices, per_device(): lax.psum_scatter(partial_value, 'col', scatter_dimension=0, tiled=True)  60.9 us
  transfers between devices with their start and end apart: 15, of which 14 were waited for; matrix products, arithmetic and copies ran while one was open for 15% of the time, Pallas kernels for 0%

commit v1 on v0

v1 whole, which is shorter than its diff:
```python
import math

import jax
import jax.numpy as jnp
from jax import lax
from jax.experimental import pallas as pl
from jax.experimental.pallas import tpu as pltpu
from jax.sharding import PartitionSpec as P

HS = 256
ROT = 64
LENGTH = 2048
LANES = 128
EPSILON = 1e-05
ROPE_BASE = 10000.0
NEGATIVE = -1e30
BF = jnp.bfloat16
F32 = jnp.float32
NN, NT, TN = ((1,), (0,)), ((1,), (1,)), ((0,), (0,))
MIB = 2**20
COST = pl.CostEstimate(flops=0, bytes_accessed=0, transcendentals=0)


def tie(value, *others):
    return lax.optimization_barrier((value,) + others)[0]


def swap_row(value):
    return lax.ppermute(value, "row", [(0, 1), (1, 0)])


def swap_col(value, bit):
    return lax.ppermute(value, "col", [(i, i ^ bit) for i in range(lax.axis_size("col"))])


def swap_y(value):
    return swap_col(value, 2)


def swap_core(value):
    return swap_col(value, 1)


def half(array, axis, index):
    size = array.shape[axis] // 2
    return lax.dynamic_slice_in_dim(array, index * size, size, axis)


def dot(a, b, dims):
    return lax.dot_general(a, b, (dims, ((), ())), preferred_element_type=F32)


def rotary_tables(tokens):
    position = (jnp.arange(tokens) % LENGTH).astype(F32)
    lane = jnp.arange(LANES)
    index = (lane % (ROT // 2)).astype(F32)
    frequency = ROPE_BASE ** (-(2.0 * index) / ROT)
    angle = position[:, None] * frequency[None, :]
    cos = jnp.where(lane < ROT, jnp.cos(angle), 1.0)
    sin = jnp.sin(angle)
    low = jnp.where(lane < ROT // 2, -sin, 0.0)
    high = jnp.where((lane >= ROT // 2) & (lane < ROT), sin, 0.0)
    return cos, low, high


def rotate(values, cos, low, high):
    first = values[:, :LANES]
    up = pltpu.roll(first, LANES - ROT // 2, 1)
    down = pltpu.roll(first, ROT // 2, 1)
    first = first * cos + up * low + down * high
    return jnp.concatenate([first, values[:, LANES:]], 1)


def tiled(i, *_):
    return (i, 0)


def fixed(*_):
    return (0, 0)


def call(kernel, name, steps, ins, outs, col=None, vmem=40, tile=None):
    def block(shape, index, rows=None):
        rows = rows or (shape[0] if index is fixed else tile or shape[0] // steps)
        return pl.BlockSpec((rows, shape[1]), index)

    spec = pltpu.PrefetchScalarGridSpec(
        num_scalar_prefetch=0 if col is None else 1,
        grid=(steps,),
        in_specs=[block(a.shape, index) for a, index in ins],
        out_specs=tuple(block(shape, index, rows) for shape, _, rows, index in outs),
    )
    return pl.pallas_call(
        kernel if col is None else lambda _, *refs: kernel(*refs),
        grid_spec=spec,
        out_shape=tuple(jax.ShapeDtypeStruct(shape, dtype) for shape, dtype, _, _ in outs),
        compiler_params=pltpu.CompilerParams(vmem_limit_bytes=vmem * MIB),
        cost_estimate=COST,
        name=name,
    )(*([] if col is None else [col.reshape(1)]), *[a for a, _ in ins])


def normed_halves(x_ref, y_ref):
    x, y = x_ref[...].astype(F32), y_ref[...].astype(F32)
    width = x.shape[1] + y.shape[1]
    average = (jnp.sum(x, 1, keepdims=True) + jnp.sum(y, 1, keepdims=True)) / width
    squares = (jnp.sum(x * x, 1, keepdims=True) + jnp.sum(y * y, 1, keepdims=True)) / width
    scale = lax.rsqrt(squares - average * average + EPSILON)
    return (x - average) * scale, (y - average) * scale


def norm_kernel(x_ref, y_ref, gx_ref, gy_ref, ax_ref, ay_ref, mx_ref, my_ref):
    x, y = normed_halves(x_ref, y_ref)
    ax_ref[...] = (x * gx_ref[0:1] + gx_ref[1:2]).astype(BF)
    ay_ref[...] = (y * gy_ref[0:1] + gy_ref[1:2]).astype(BF)
    mx_ref[...] = (x * gx_ref[2:3] + gx_ref[3:4]).astype(BF)
    my_ref[...] = (y * gy_ref[2:3] + gy_ref[3:4]).astype(BF)


def norm_call(col, flip, x, y, gx, gy, *before):
    (rows, feats), tile, slots = x.shape, 256, 4
    steps = rows // tile

    def index(i, col_ref):
        return ((col_ref[0] ^ flip) * steps + i, 0)

    rest = [pl.BlockSpec(memory_space=pl.ANY)] * len(before)
    block = pl.BlockSpec((tile, feats), tiled)
    whole = pl.BlockSpec(gx.shape, fixed)
    return pl.pallas_call(
        lambda _, x, y, gx, gy, *refs: norm_kernel(x, y, gx, gy, *refs[len(before) :]),
        grid_spec=pltpu.PrefetchScalarGridSpec(
            num_scalar_prefetch=1,
            grid=(steps,),
            in_specs=[block, block, whole, whole] + rest,
            out_specs=(pl.BlockSpec((tile, feats), index),) * 4,
        ),
        out_shape=(jax.ShapeDtypeStruct((slots * rows, feats), BF),) * 4,
        input_output_aliases={5 + i: i for i in range(len(before))},
        compiler_params=pltpu.CompilerParams(vmem_limit_bytes=56 * MIB),
        cost_estimate=COST,
        name="norm",
    )(col.reshape(1), x, y, gx, gy, *before)


def pre_kernel(x_ref, y_ref, wx_ref, wy0_ref, wy1_ref, bias_ref, active_ref, slope_ref):
    mid, part = wy0_ref.shape[0], wx_ref.shape[1]
    for start in range(0, wx_ref.shape[1], part):
        at = slice(start, start + part)
        u = dot(x_ref[...], wx_ref[:, at], NN) + bias_ref[:, at]
        u = u + dot(y_ref[:, :mid], wy0_ref[:, at], NN) + dot(y_ref[:, mid:], wy1_ref[:, at], NN)
        phi = 0.5 * (1.0 + lax.erf(u * 2.0**-0.5))
        bell = jnp.exp(-0.5 * u * u)
        active_ref[:, at] = (u * phi).astype(BF)
        slope_ref[:, at] = (phi + u * bell * (2.0 * math.pi) ** (-0.5)).astype(BF)


def pre_call(x, y, wx, wy0, wy1, bias):
    tokens, tile, units = x.shape[0], 256, wx.shape[1]
    return call(
        pre_kernel,
        "pre_act",
        tokens // tile,
        [(x, tiled), (y, tiled), (wx, fixed), (wy0, fixed), (wy1, fixed), (bias.reshape(1, -1), fixed)],
        [((tokens, units), BF, tile, tiled)] * 2,
        vmem=56,
    )


def rowwise(fn, rows, outs, *ins, flag=None):
    tile = 256
    ins = [i if isinstance(i, tuple) else (i, 0) for i in ins]
    flags = [] if flag is None else [flag.astype(jnp.int32).reshape(1)]

    def at(first):
        return fixed if first is None else lambda i, *_: (i + first // tile, 0)

    def kernel(*refs):
        values = [ref[0] != 0 for ref in refs[: len(flags)]]
        refs = refs[len(flags) :]
        results = fn(*values, *[ref[...] for ref in refs[: len(ins)]])
        for ref, result in zip(refs[len(ins) :], results, strict=True):
            ref[...] = result

    return pl.pallas_call(
        kernel,
        grid_spec=pltpu.PrefetchScalarGridSpec(
            num_scalar_prefetch=len(flags),
            grid=(rows // tile,),
            in_specs=[pl.BlockSpec((tile, a.shape[1]), at(first)) for a, first in ins],
            out_specs=tuple(pl.BlockSpec((tile, cols), tiled) for cols, _ in outs),
        ),
        out_shape=tuple(jax.ShapeDtypeStruct((rows, cols), dtype) for cols, dtype in outs),
        compiler_params=pltpu.CompilerParams(vmem_limit_bytes=32 * MIB),
        cost_estimate=COST,
        name="rowwise",
    )(*flags, *[a for a, _ in ins])


def plain_add(a, b):
    return [(a.astype(F32) + b.astype(F32)).astype(BF)]


def add_low(a, b):
    return (a.astype(F32) + b.astype(F32)).astype(a.dtype)


def choose(flag):
    def fn(held, arrived):
        if held.ndim == 1:
            return jnp.where(flag, arrived, held)
        outs = [(held.shape[1], BF)]
        return rowwise(lambda f, h, a: [jnp.where(f, a, h)], held.shape[0], outs, held, arrived, flag=flag)[0]

    return fn


def choose_or_add(flag):
    return lambda value, a, b: jnp.where(flag, value, add_low(a, b))


def weight_grad(cuts, a, b, last_a=None, last_b=None):
    tokens, cols, tile = b.shape[0], b.shape[1], 256
    own = sum(cuts) // tile if last_a is None else a.shape[1] // tile
    skip = 0
    if isinstance(a, tuple):
        a, skip = a[0], a[1] // tile
    first = [sum(cuts[:i]) // tile for i in range(len(cuts) + 1)]

    def kernel(*refs):
        step = pl.program_id(0)

        def store(out):
            for start, end, ref in zip(first[:-1], first[1:], refs[-len(cuts) :], strict=True):

                @pl.when((step >= start) & (step < end))
                def _():
                    ref[...] = out

        if last_a is None:
            store(dot(refs[0][...], refs[1][...], TN).astype(BF))
            return

        @pl.when(step < own)
        def _():
            store(dot(refs[0][...], refs[1][...], TN).astype(BF))

        @pl.when(step >= own)
        def _():
            store(dot(refs[2][...], refs[3][...], TN).astype(BF))

    def index(start, end):
        return lambda i: (jnp.clip(i - start, 0, end - start - 1), 0)

    ins = [a, b] if last_a is None else [a, b, last_a, last_b]
    specs = [
        pl.BlockSpec((tokens, tile), lambda i: (0, jnp.minimum(i, own - 1) + skip)),
        pl.BlockSpec(b.shape, fixed),
        pl.BlockSpec((tokens, tile), fixed),
        pl.BlockSpec(b.shape, fixed),
    ]
    return pl.pallas_call(
        kernel,
        grid=(first[-1],),
        out_shape=tuple(jax.ShapeDtypeStruct((size, cols), BF) for size in cuts),
        in_specs=specs[: len(ins)],
        out_specs=tuple(
            pl.BlockSpec((tile, cols), index(s, e)) for s, e in zip(first[:-1], first[1:], strict=True)
        ),
        compiler_params=pltpu.CompilerParams(vmem_limit_bytes=40 * MIB),
        cost_estimate=COST,
        name="weight_grad",
    )(*ins)


def pre_grad_kernel(gx_ref, gy_ref, wx_ref, wy0_ref, wy1_ref, slope_ref, out_ref, sum_ref):
    @pl.when(pl.program_id(0) == 0)
    def _():
        sum_ref[...] = jnp.zeros_like(sum_ref)

    mid = wy0_ref.shape[0]
    for i, wy_ref in enumerate((wy0_ref, wy1_ref)):
        at = slice(i * mid, (i + 1) * mid)
        u = dot(gx_ref[...], wx_ref[at, :], NT) + dot(gy_ref[...], wy_ref[...], NT)
        low = (u * slope_ref[:, at].astype(F32)).astype(BF)
        out_ref[:, at] = low
        sum_ref[:, at] += jnp.sum(low.astype(F32), 0, keepdims=True)


def pre_grad_call(gx, gy, wx, wy0, wy1, slope):
    tokens, tile, units = gx.shape[0], 512, wx.shape[0]
    return call(
        pre_grad_kernel,
        "pre_grad",
        tokens // tile,
        [(gx, tiled), (gy, tiled), (wx, fixed), (wy0, fixed), (wy1, fixed), (slope, tiled)],
        [((tokens, units), BF, tile, tiled), ((1, units), F32, 1, fixed)],
    )


def packed_kernel(x_ref, y_ref, wx_ref, wy_ref, bias_ref, cos_ref, low_ref, high_ref, q_ref, k_ref, v_ref):
    out = dot(x_ref[...], wx_ref[...], NN) + dot(y_ref[...], wy_ref[...], NN) + bias_ref[...]
    tables = cos_ref[...], low_ref[...], high_ref[...]
    q_ref[...] = rotate(out[:, :HS], *tables).astype(BF)
    k_ref[...] = rotate(out[:, HS : 2 * HS], *tables).astype(BF)
    v_ref[...] = out[:, 2 * HS :].astype(BF)


def packed_call(x, y, wx, wy, bias, *tables):
    tokens, tile = x.shape[0], 512
    return call(
        packed_kernel,
        "packed",
        tokens // tile,
        [(x, tiled), (y, tiled), (wx, fixed), (wy, fixed), (bias.reshape(1, -1), fixed)]
        + [(t, tiled) for t in tables],
        [((tokens, HS), BF, tile, tiled)] * 3,
    )


def attention_kernel(
    q_ref, k_ref, v_ref, g_ref, cos_ref, low_ref, high_ref, o_ref, out_ref, sum_ref, dk_acc, dv_acc
):
    slots, rows, _ = q_ref.shape
    scale = HS ** (-0.5)
    mask = lax.broadcasted_iota(jnp.int32, (rows, rows), 1) <= lax.broadcasted_iota(
        jnp.int32, (rows, rows), 0
    )
    total_sum = [jnp.zeros((1, HS), F32) for _ in range(3)]

    def unrotate(values, at):
        return rotate(values, cos_ref[at], -low_ref[at], -high_ref[at]).astype(BF)

    for i in range(slots):
        q, g = q_ref[i], g_ref[i]
        scores = []
        for j in range(i + 1):
            s = dot(q, k_ref[j], NT) * scale
            scores.append(jnp.where(mask, s, NEGATIVE) if j == i else s)
        top = scores[0].max(-1, keepdims=True)
        for s in scores[1:]:
            top = jnp.maximum(top, s.max(-1, keepdims=True))
        exps = [jnp.exp(s - top) for s in scores]
        inv = 1.0 / sum(e.sum(-1, keepdims=True) for e in exps)
        probs = [e * inv for e in exps]
        out = jnp.zeros((rows, HS), F32)
        center = jnp.zeros((rows, 1), F32)
        prob_grads = []
        for j in range(i + 1):
            low = probs[j].astype(BF)
            v = v_ref[j]
            out = out + dot(low, v, NN)
            pg = dot(g, v, NT)
            center = center + (probs[j] * pg).sum(-1, keepdims=True)
            prob_grads.append(pg)
            dv = dot(low, g, TN)
            if j == i:
                dv_acc[j] = dv
            else:
                dv_acc[j] += dv
        o_ref[i] = out.astype(BF)
        dq = jnp.zeros((rows, HS), F32)
        for j in range(i + 1):
            sg = (probs[j] * (prob_grads[j] - center)).astype(BF)
            dq = dq + dot(sg, k_ref[j], NN)
            dk = dot(sg, q, TN)
            if j == i:
                dk_acc[j] = dk
            else:
                dk_acc[j] += dk
        dq = unrotate(dq * scale, i)
        out_ref[i, :, 0:HS] = dq
        total_sum[0] = total_sum[0] + jnp.sum(dq.astype(F32), 0, keepdims=True)
    for j in range(slots):
        dk = unrotate(dk_acc[j] * scale, j)
        dv = dv_acc[j].astype(BF)
        out_ref[j, :, HS : 2 * HS] = dk
        out_ref[j, :, 2 * HS :] = dv
        total_sum[1] = total_sum[1] + jnp.sum(dk.astype(F32), 0, keepdims=True)
        total_sum[2] = total_sum[2] + jnp.sum(dv.astype(F32), 0, keepdims=True)
    for i in range(3):
        sum_ref[:, i * HS : (i + 1) * HS] = total_sum[i]


def attention(slots, q, k, v, g, cos, low, high):
    tokens = q.shape[0]
    rows = tokens // slots
    vmem = pl.BlockSpec(memory_space=pltpu.VMEM)
    attended, packed_grad, sums = pl.pallas_call(
        attention_kernel,
        out_shape=(
            jax.ShapeDtypeStruct((slots, rows, HS), BF),
            jax.ShapeDtypeStruct((slots, rows, 3 * HS), BF),
            jax.ShapeDtypeStruct((1, 3 * HS), F32),
        ),
        in_specs=[vmem] * 7,
        out_specs=(vmem,) * 3,
        scratch_shapes=[pltpu.VMEM((slots, rows, HS), F32)] * 2,
        compiler_params=pltpu.CompilerParams(vmem_limit_bytes=56 * MIB),
        cost_estimate=COST,
        name="attention",
    )(*[a.reshape(slots, rows, a.shape[1]) for a in (q, k, v, g, cos, low, high)])
    return packed_grad.reshape(tokens, 3 * HS), attended.reshape(tokens, HS), sums


def mixed_kernel(a_ref, b_ref, dx_ref, dy_ref, wx_ref, wy0_ref, wy1_ref, out_ref):
    feats, mid = dx_ref.shape[1], wy0_ref.shape[0]
    a, b = a_ref[...], b_ref[...]
    out_ref[:, :feats] = (dot(a, dx_ref[...], NN) + dot(b, wx_ref[...], NN)).astype(BF)
    y = dot(a, dy_ref[...], NN) + dot(b[:, :mid], wy0_ref[...], NN) + dot(b[:, mid:], wy1_ref[...], NN)
    out_ref[:, feats:] = y.astype(BF)


def mixed_call(col, part, attended, active, dx, dy, *weights):
    tokens, tile, width = attended.shape[0] // 2, 256, dx.shape[1] + dy.shape[1]
    steps = tokens // tile
    each = steps // 2

    def order(i, col_ref):
        return ((col_ref[0] ^ part ^ (2 * (i // each))) * each + i % each, 0)

    ins = [(attended, order), (active, order)] + [(w, fixed) for w in (dx, dy, *weights)]
    outs = [((tokens, width), BF, tile, tiled)]
    return call(mixed_kernel, "mixed", steps, ins, outs, col, tile=tile)[0]


def norm_grad_kernel(
    x_ref, y_ref, gx_ref, gy_ref, p_ref, u_ref, qx_ref, qy_ref, wx_ref, wy0_ref, wy1_ref, out_ref, sum_ref
):
    feats, mid = x_ref.shape[1], wy0_ref.shape[0]

    @pl.when(pl.program_id(0) == 0)
    def _():
        sum_ref[...] = jnp.zeros_like(sum_ref)

    normed = normed_halves(x_ref, y_ref)
    p, u = p_ref[...], u_ref[...]
    for start in range(0, 2 * feats, mid):
        side, lo = divmod(start, feats)
        at, part = slice(start, start + mid), slice(lo, lo + mid)
        q = (qx_ref, qy_ref)[side][part, :]
        w = wx_ref[part, :] if side == 0 else (wy0_ref, wy1_ref)[lo // mid][...]
        gains = (gx_ref, gy_ref)[side][:, part]
        n = normed[side][:, part]
        a, m = dot(p, q, NT), dot(u, w, NT)
        out_ref[:, at] = (a * gains[0:1] + m * gains[2:3]).astype(BF)
        sum_ref[0:1, at] += jnp.sum(a * n, 0, keepdims=True)
        sum_ref[1:2, at] += jnp.sum(a, 0, keepdims=True)
        sum_ref[2:3, at] += jnp.sum(m * n, 0, keepdims=True)
        sum_ref[3:4, at] += jnp.sum(m, 0, keepdims=True)


def norm_grad_call(col, part, x, y, gx, gy, packed_grad, pre_grad, *weights):
    tokens, tile, width = x.shape[0], 256, x.shape[1] + y.shape[1]
    steps = tokens // tile
    each = steps // 2

    def order(i, col_ref):
        return ((col_ref[0] ^ part ^ (2 * (i // each))) * each + i % each, 0)

    ins = [(x, tiled), (y, tiled), (gx, fixed), (gy, fixed), (packed_grad, order), (pre_grad, order)]
    return call(
        norm_grad_kernel,
        "norm_grad",
        steps,
        ins + [(w, fixed) for w in weights],
        [((tokens, width), BF, tile, tiled), ((4, width), F32, 4, fixed)],
        col,
        tile=tile,
    )


def assemble(name, meta, arrays, steps, out, fill):
    flat = [a for _, _, part in arrays for a in part]
    shape, block, index = out

    def kernel(meta_ref, *refs):
        at = iter(refs[:-1])
        parts = [[next(at) for _ in part] for _, _, part in arrays]

        def read(i):
            values = [ref[...] for ref in parts[i]]
            value = values[0] if len(values) == 1 else jnp.where(meta_ref[1] != 0, *values)
            return value.astype(F32)

        fill(read, meta_ref[0], refs[-1])

    return pl.pallas_call(
        kernel,
        grid_spec=pltpu.PrefetchScalarGridSpec(
            num_scalar_prefetch=1,
            grid=(steps,),
            in_specs=[pl.BlockSpec(block, index) for block, index, part in arrays for _ in part],
            out_specs=pl.BlockSpec(block, index),
        ),
        out_shape=jax.ShapeDtypeStruct(shape, F32),
        compiler_params=pltpu.CompilerParams(vmem_limit_bytes=48 * MIB),
        cost_estimate=COST,
        name=name,
    )(meta, *flat)


def rows_of(part, tiles):
    return lambda i, *_: (jnp.clip(i - part * tiles, 0, tiles - 1), 0)


def finish_out(meta, parts):
    rows, cols = parts[0][0].shape
    tile, tiles = 256, rows // 256
    block = (tile, cols)

    def index(i, meta_ref):
        return ((i // (2 * tiles) ^ meta_ref[0]) * 2 * tiles + i % (2 * tiles), 0)

    def fill(read, row, out_ref):
        for k in range(4):

            @pl.when(pl.program_id(0) // tiles == k)
            def _():
                out_ref[...] = read(k)

    arrays = [(block, rows_of(k, tiles), part) for k, part in enumerate(parts)]
    return assemble("out_grad", meta, arrays, 4 * tiles, ((4 * rows, cols), block, index), fill)


def finish_in(meta, parts):
    rows, cols = parts[0][0].shape
    tile, tiles = 256, rows // 256

    def fill(read, row, out_ref):
        for k in range(2):

            @pl.when(pl.program_id(0) // tiles == k)
            def _():
                mine, other = read(k), read(2 + k)
                out_ref[:, :cols] = jnp.where(row == 0, mine, other)
                out_ref[:, cols:] = jnp.where(row == 0, other, mine)

    arrays = [((tile, cols), rows_of(k % 2, tiles), part) for k, part in enumerate(parts)]
    out = ((2 * rows, 2 * cols), (tile, 2 * cols), tiled)
    return assemble("in_grad", meta, arrays, 2 * tiles, out, fill)


def finish_qkv(meta, parts):
    feats, tile = parts[0][0].shape[1], 256
    blocks = [(2 * HS, tile), (HS, tile)] * 2

    def fill(read, row, out_ref):
        mine, other = (jnp.concatenate([read(k), read(k + 1)], 0).T for k in (0, 2))
        out_ref[:, 0, :] = jnp.where(row == 0, mine, other)
        out_ref[:, 1, :] = jnp.where(row == 0, other, mine)

    arrays = [(block, lambda i, *_: (0, i), part) for block, part in zip(blocks, parts, strict=True)]
    out = ((feats, 2, 3 * HS), (tile, 2, 3 * HS), lambda i, *_: (i, 0, 0))
    return assemble("qkv_grad", meta, arrays, feats // tile, out, fill)


def finish_dense(meta, parts):
    feats = parts[0][0].shape[1]

    def fill(read, row, out_ref):
        out_ref[row] = read(0)
        out_ref[1 - row] = read(1)

    arrays = [((HS, feats), lambda *_: (1, 0), part) for part in parts]
    out = ((2, HS, feats), (2, HS, feats), lambda *_: (0, 0, 0))
    return assemble("dense_grad", meta, arrays, 1, out, fill)


class Names:
    def __getattr__(self, name):
        return name


def is_name(value):
    return isinstance(value, (str, tuple))


class Beats:
    def __init__(self):
        self.env, self.tasks, self.flying = {}, [], []
        self.now, self.token = 0, jnp.zeros((8, LANES), F32)
        self.last, self.new = self.token, []
        self.line = Line()

    def compute(self, beat, names, fn, *inputs, top=False):
        self.tasks.append((beat, inputs, names, (fn, None) if top else fn))

    def send(self, beat, name, fn, source, beats=1):
        self.tasks.append((beat, (source,), name, (fn, beats)))

    def put(self, name, value):
        self.env[name] = value
        self.new.append(name)

    def run(self):
        while self.tasks or self.flying or self.line.busy:
            if self.now > 20 + 8 * self.line.count:
                raise ValueError([task[:3] for task in self.tasks])
            self.line.beat(self)
            for task in [t for t in self.tasks if isinstance(t[3], tuple)] + self.tasks[:]:
                beat, inputs, names, fn = task
                if not any(task is t for t in self.tasks):
                    continue
                if beat > self.now or any(is_name(i) and i not in self.env for i in inputs):
                    continue
                self.tasks = [t for t in self.tasks if t is not task]
                values = [self.env[i] if is_name(i) else i for i in inputs]
                if isinstance(fn, tuple) and fn[1] is None:
                    self.do(names, fn[0], *values)
                elif isinstance(fn, tuple):
                    fn, beats = fn
                    value = fn(tie(values[0], self.token))
                    if beats:
                        self.flying.append((self.now + beats, names, value))
                    else:
                        self.env[names] = value
                else:
                    self.do(names, fn, *values)
            self.tick()

    def do(self, names, fn, first, *rest):
        outs = fn(tie(first, self.last), *rest)
        for name, value in [(names, outs)] if is_name(names) else zip(names, outs, strict=True):
            self.put(name, value)
        self.last = jax.tree.leaves(outs)[0]
        return outs

    def tick(self):
        self.now += 1
        for due, name, value in self.flying:
            if due <= self.now:
                self.put(name, value)
        self.flying = [f for f in self.flying if f[0] > self.now]
        names = list(dict.fromkeys(n for n in self.new if n in self.env))
        values = lax.optimization_barrier((self.token, *[self.env[n] for n in names]))
        self.token = self.last = values[0]
        self.env.update(zip(names, values[1:], strict=True))
        self.new = []


class Line:
    def __init__(self):
        self.count, self.place = lax.axis_size("dp"), lax.axis_index("dp")
        self.mid = self.count // 2
        self.queue, self.going = [], []

    @property
    def busy(self):
        return bool(self.queue or self.going)

    def enter(self, *names):
        self.queue += names

    def on(self, *places):
        return (self.place == places[0]) | (self.place == places[1])

    def pairs(self, step):
        n, mid = self.count, self.mid
        if step < mid - 1:
            return [(step, step + 1), (n - 1 - step, n - 2 - step)]
        if step == mid - 1:
            return [(mid - 1, mid), (mid, mid - 1)]
        step -= mid
        return [(mid - 1 - step, mid - 2 - step), (mid + step, mid + 1 + step)]

    def beat(self, beats):
        env, mid, steps = beats.env, self.mid, 2 * self.mid - 1
        later, outward = [], {}
        for name, step in self.going:
            got, value = (name, step), (name, "held")
            if step + 1 == steps:
                src = self.pairs(step)
                held, arrived = env[value], env[got]
                env[name, "sum"] = jnp.where(self.on(src[0][1], src[1][1]), arrived, held)
                env[name, "parts"] = self.on(src[0][1], src[1][1]), arrived, held
            else:
                later.append((name, step + 1))
        starting = []
        if self.queue and self.queue[0] in env and self.queue[0] != "small":
            starting = [self.queue.pop(0)]
            env[starting[0], "held"] = env[starting[0]]
        small = [n for n in self.queue if n == "small" and n in env]
        for n in small:
            self.queue.remove(n)
            env[n, "held"] = env[n]
            starting.append(n)
        moving = [(n, 0) for n in starting] + later

        def update(name, step):
            if step == 0:
                return (lambda v: v), [(name, "held")]
            inputs = [(name, "held"), (name, step - 1)]
            if step <= mid:
                return add_low, inputs
            src = self.pairs(step - 1)
            return choose(self.on(src[0][1], src[1][1])), inputs

        for name, step in sorted(moving, key=lambda m: (m[1] != mid - 1, m[1] < mid)):
            fn, inputs = update(name, step)
            values = [env[i] for i in inputs]
            if step >= mid:
                match = [
                    m
                    for m in moving
                    if m[1] == 2 * mid - 2 - step and env[m[0]].shape == env[name].shape and m not in outward
                ]
                if match:
                    inner = match[0]
                    outward[inner] = (name, step)
                    continue
            if step < mid - 1 and (name, step) in outward:
                continue
            if step:
                beats.do((name, "held"), fn, *values)
            self.send(beats, self.pairs(step), (name, "held"), [(name, step)])
        for (name, step), (far, far_step) in outward.items():
            fn, inputs = update(name, step)
            if step:
                beats.do((name, "held"), fn, *[env[i] for i in inputs])
            inputs = update(far, far_step)[1]
            outer = self.on(step, self.count - 1 - step)
            if far_step > mid:
                gets = self.on(*[pair[1] for pair in self.pairs(far_step - 1)])
                beats.do((far, "held"), choose(gets), *[env[i] for i in inputs])
                beats.do((far, "held"), choose(outer), env[far, "held"], env[name, "held"])
            else:
                add = choose_or_add(outer)
                beats.do((far, "held"), add, env[name, "held"], *[env[i] for i in inputs])
            self.send(
                beats,
                self.pairs(step) + self.pairs(far_step),
                (far, "held"),
                [(name, step), (far, far_step)],
            )
        self.going = moving

    def send(self, beats, pairs, source, gets):
        value = lax.ppermute(tie(beats.env[source], beats.token), "dp", pairs)
        for name, step in gets:
            beats.flying.append((beats.now + 1, (name, step), value))


def per_device(
    residual_in,
    attn_gain,
    attn_shift,
    mlp_gain,
    mlp_shift,
    qkv_weight,
    qkv_bias,
    dense_weight,
    dense_bias,
    in_weight,
    in_bias,
    out_weight,
    out_bias,
    cotangent,
):
    row, col = lax.axis_index("row"), lax.axis_index("col")
    rows, feats = residual_in.shape
    slots, width = lax.axis_size("col"), 2 * feats
    units = in_weight.shape[1] // 2
    other = 1 - row
    plan = Beats()
    env, compute, send, n = plan.env, plan.compute, plan.send, Names()

    def summed(name):
        return name, n.sum


    def below(*parts):
        return jnp.concatenate(parts, 0)

    def part(lo, hi):
        return lambda v: lax.slice_in_dim(v, lo, hi)

    def share(beat, name, fn, source, *needs):
        compute_free = (beat, (source, *needs), name, (fn, 0))
        plan.tasks.append(compute_free)

    env.update(res=residual_in, cot=cotangent)
    env[n.gx] = jnp.stack([attn_gain, attn_shift, mlp_gain, mlp_shift])

    send(0, n.gy, swap_row, n.gx)
    send(0, n.res_x, swap_row, n.res)
    send(0, n.res_y, swap_y, n.res)
    send(0, n.res_c, swap_core, n.res)
    mid = feats // 2
    pick = lax.dynamic_slice
    compute(0, n.in_sent0, lambda w: pick(w, (0, other * units), (mid, units)), in_weight)
    compute(0, n.wx, lambda w: half(w, 1, row), in_weight)
    compute(0, n.ox, lambda w: half(w, 0, row), out_weight)
    compute(0, n.in_sent1, lambda w: pick(w, (mid, other * units), (mid, units)), in_weight)

    compute(0, [n.cos, n.low, n.high], lambda _: rotary_tables(slots * rows), n.gx)

    send(1, n.wy0, swap_row, n.in_sent0)
    send(1, n.res_xy, swap_y, n.res_x)
    send(1, n.res_xc, swap_core, n.res_x)
    send(1, n.res_yc, swap_core, n.res_y)
    compute(1, n.norm0, lambda *a: norm_call(col, 0, *a), n.res, n.res_x, n.gx, n.gy)
    for i in range(2):
        at = other * units + i * (units // 2)
        compute(1, (n.oy_sent, i), lambda w, at=at: pick(w, (at, 0), (units // 2, feats)), out_weight)
    compute(1, n.qx, lambda w: lax.dynamic_index_in_dim(w, row, 1, False), qkv_weight)
    compute(1, n.dense_sent, lambda w: lax.dynamic_index_in_dim(w, other, 0, False), dense_weight)
    compute(1, n.dx, lambda w: lax.dynamic_index_in_dim(w, row, 0, False), dense_weight)

    send(2, n.wy1, swap_row, n.in_sent1)
    send(2, n.res_xyc, swap_core, n.res_xy, 0)

    def gather_col(value):
        return lax.all_gather(value, "col", axis=0, tiled=True)

    share(2, n.g, gather_col, n.cot)

    def norm_rest(res_c, res_xc, res_y, res_xy, res_yc, res_xyc, gx, gy, before):
        before = norm_call(col, 1, res_c, res_xc, gx, gy, *before)
        before = norm_call(col, 2, res_y, res_xy, gx, gy, *before)
        return norm_call(col, 3, res_yc, res_xyc, gx, gy, *before)

    compute(
        2,
        [n.ax, n.ay, n.mx, n.my],
        norm_rest,
        *[n.res_c, n.res_xc, n.res_y, n.res_xy, n.res_yc, n.res_xyc, n.gx, n.gy, n.norm0],
    )

    send(3, n.cot_x, swap_row, n.cot)
    in_bias_mine = lax.dynamic_slice_in_dim(in_bias, row * units, units, 0)
    compute(3, [n.active, n.slope], pre_call, n.mx, n.my, n.wx, n.wy0, n.wy1, in_bias_mine)

    def grads(beat, names, cuts, *inputs):
        compute(beat, names, lambda *a: weight_grad(cuts, *a), *inputs)

    two = [units // 2] * 2
    half_units = [units // 2]
    grads(3, [n.out_own0], half_units, n.active, n.g)
    z = 4
    for i in range(2):
        send(z + i, (n.oy, i), swap_row, (n.oy_sent, i))
    oy = [(n.oy, 0), (n.oy, 1)]
    compute(z, [n.out_own1], lambda a, g: weight_grad(half_units, (a, units // 2), g), n.active, n.g)
    share(z, n.h, gather_col, n.cot_x)
    compute(z, n.x_near, below, n.res, n.res_y)
    compute(z, n.y_near, below, n.res_x, n.res_xy)
    compute(z, n.x_far, below, n.res_c, n.res_yc)
    compute(z, n.y_far, below, n.res_xc, n.res_xyc)
    grads(z + 1, [n.out_oth0, n.out_oth1], two, n.active, n.h)
    compute(z + 2, [n.pre_grad, n.in_bias_sum], pre_grad_call, n.g, n.h, n.ox, *oy, n.slope)
    two = [feats // 2] * 2
    grads(z + 3, [n.in_own0, n.in_own1], two, n.mx, n.pre_grad)
    grads(z + 3, [n.in_oth0, n.in_oth1], two, n.my, n.pre_grad)
    cut = 5 * feats // 8
    for i, (lo, hi) in enumerate(((0, cut), (cut, feats))):
        sent = (n.qy_sent, i)
        compute(2, sent, lambda w, lo=lo, hi=hi: lax.dynamic_index_in_dim(w[lo:hi], other, 1, False), qkv_weight)
        send(z + 2 + i, (n.qy, i), swap_row, sent)
    send(z + 3, n.dy, swap_row, n.dense_sent)
    compute(z + 4, n.qy, below, (n.qy, 0), (n.qy, 1))
    qkv_bias_mine = lax.dynamic_index_in_dim(qkv_bias, row, 0, False)
    compute(
        z + 4,
        [n.query, n.key, n.value],
        packed_call,
        *[n.ax, n.ay, n.qx, n.qy, qkv_bias_mine, n.cos, n.low, n.high],
    )
    compute(
        z + 4,
        n.attended_grad,
        lambda g, h, dx, dy: (dot(g, dx, NT) + dot(h, dy, NT)).astype(BF),
        *[n.g, n.h, n.dx, n.dy],
    )
    compute(
        z + 5,
        [n.packed_grad, n.attended, n.qkv_bias_sum],
        lambda *a: attention(slots, *a),
        *[n.query, n.key, n.value, n.attended_grad, n.cos, n.low, n.high],
    )
    cuts = [2 * HS, 2 * HS]
    grads(z + 6, [n.att_own0, n.att_own1], cuts, n.packed_grad, n.ax, n.attended, n.g)
    grads(z + 6, [n.att_oth0, n.att_oth1], cuts, n.packed_grad, n.ay, n.attended, n.h)

    send(z + 4, n.in_oth0_x, swap_row, n.in_oth0)
    send(z + 5, n.in_oth1_x, swap_row, n.in_oth1)
    send(z + 7, n.att_oth0_x, swap_row, n.att_oth0)
    send(z + 8, n.att_oth1_x, swap_row, n.att_oth1)
    plan.line.enter(
        *(n.out_own0, n.out_own1, n.out_oth0, n.out_oth1, n.in_own0, n.in_own1, n.in_oth0_x),
        *(n.att_own0, n.att_own1, n.att_oth0_x, n.att_oth1_x, n.in_oth1_x, n.small),
    )

    def choose_part(parts):
        return choose(parts[0])(parts[2], parts[1])

    compute(z + 5, n.out_oth0_s, choose_part, (n.out_oth0, n.parts))
    compute(z + 6, n.out_oth1_s, choose_part, (n.out_oth1, n.parts))
    send(z + 6, n.out_oth0_y, swap_row, n.out_oth0_s)
    send(z + 9, n.out_oth1_y, swap_row, n.out_oth1_s)

    for beat, part, name, sums, x, y in (
        (z + 7, 1, (n.ng, n.far), n.sums_far, n.x_far, n.y_far),
        (z + 8, 0, (n.ng, n.near), n.sums_near, n.x_near, n.y_near),
    ):
        compute(
            beat,
            [name, sums],
            lambda *a, part=part: norm_grad_call(col, part, *a),
            *[x, y, n.gx, n.gy, n.packed_grad, n.pre_grad, n.qx, n.qy, n.wx, n.wy0, n.wy1],
        )
    for beat, part, name in ((z + 9, 1, (n.mixed, n.far)), (z + 10, 0, (n.mixed, n.near))):
        compute(
            beat,
            name,
            lambda *a, part=part: mixed_call(col, part, *a),
            *[n.attended, n.active, n.dx, n.dy, n.ox, *oy],
        )

    part_rows = rows // 2

    def near(a, b, *c):
        def fn(a, b, c0, c1):
            c = jnp.where(pl.program_id(0) == 0, c0, c1)
            out = a.astype(F32) + b.astype(F32) + c.astype(F32)
            return [out[:, feats:].astype(BF), out[:, :feats]]

        return rowwise(fn, rows, [(feats, BF), (feats, F32)], a, b, *[(v, None) for v in c])

    def far_sum(i):
        at, outs = rows + i * part_rows, [(width, BF)]
        return lambda a, b: rowwise(plain_add, part_rows, outs, (a, at), (b, at))[0]

    def scatter(beat, name):
        far, mine, got = [(name, i) for i in (n.far, n.near, n.core)]
        send(beat, got, swap_core, far)
        got_y = [(name, n.near, i) for i in range(2)]
        for i in range(2):
            far_y = (name, n.far, i)
            compute(beat + 1, far_y, far_sum(i), mine, got, top=i == 0)
            send(beat + 1 + i, got_y[i], swap_y, far_y)
        compute(beat + 3, [(name, n.sent), (name, n.keep)], near, mine, got, *got_y, top=True)
        send(beat + 3, (name, n.got), swap_row, (name, n.sent))

    scatter(z + 8, n.ng)
    scatter(z + 10, n.mixed)
    compute(
        z + 14,
        n.block_out,
        lambda a, xg, res, b, c: (res.astype(F32) + a + xg.astype(F32) + b + c).astype(BF),
        *[(n.mixed, n.keep), (n.mixed, n.got), n.res, dense_bias, out_bias],
    )

    def own_norm(res, res_x):
        x, y = res.astype(F32), res_x.astype(F32)
        average = (jnp.sum(x, 1, keepdims=True) + jnp.sum(y, 1, keepdims=True)) / width
        squares = (jnp.sum(x * x, 1, keepdims=True) + jnp.sum(y * y, 1, keepdims=True)) / width
        scale = lax.rsqrt(squares - average * average + EPSILON)
        return (x - average) * scale, scale

    def token_sums(keep, xg, res, res_x):
        normed, scale = own_norm(res, res_x)
        grad = keep + xg.astype(F32)
        return jnp.stack([jnp.sum(grad, 1), jnp.sum(grad * normed, 1)])

    compute(z + 12, n.tok, token_sums, (n.ng, n.keep), (n.ng, n.got), n.res, n.res_x)
    send(z + 12, n.tok_x, swap_row, n.tok)

    def finish_input(keep, xg, res, res_x, cot, tok, tok_x):
        normed, scale = own_norm(res, res_x)
        tok = (tok + tok_x) / width
        grad = keep + xg.astype(F32)
        return cot.astype(F32) + scale * (grad - tok[0][:, None] - normed * tok[1][:, None])

    rest = [n.res, n.res_x, n.cot, n.tok, n.tok_x]
    compute(
        z + 13, n.input_grad, finish_input, (n.ng, n.keep), (n.ng, n.got), *rest
    )

    def small_all(near, far, cot, qkv_bias_sum, in_bias_sum):
        bias_sum = jnp.pad(jnp.sum(cot, 0, dtype=F32), (0, feats))
        parts = [(near + far).reshape(-1), bias_sum, qkv_bias_sum.reshape(-1), in_bias_sum.reshape(-1)]
        return jnp.concatenate(parts)

    def take(parts):
        return jnp.where(parts[0], parts[1], parts[2])

    compute(z + 8, n.small, small_all, n.sums_near, n.sums_far, n.cot, n.qkv_bias_sum, n.in_bias_sum)
    compute(z + 12, n.small_s, take, (n.small, n.parts), top=True)
    send(z + 12, n.small_x, swap_row, n.small_s)

    def by_feature(mine, got):
        mine, got = (v[: 5 * width].reshape(5, width) for v in (mine, got))
        return mine[:, :feats] + got[:, feats:]

    compute(z + 13, n.small0, by_feature, n.small_s, n.small_x)
    send(z + 13, n.small0_c, swap_core, n.small0, 0)
    compute(z + 13, n.small1, jnp.add, n.small0, n.small0_c)
    send(z + 13, n.small1_y, swap_y, n.small1, 0)
    compute(z + 13, n.small2, jnp.add, n.small1, n.small1_y)

    def finish(beat, name, fn, *sources):
        def step(*sources):
            flag = next(v[0] for v in sources if isinstance(v, tuple))
            arrays = [v[1:] if isinstance(v, tuple) else (v,) for v in sources]
            return fn(jnp.stack([row, flag.astype(jnp.int32)]), arrays)

        compute(beat, name, step, *sources)

    def done(*names):
        return [(v, n.parts) for v in names]

    finish(z + 12, n.out_weight_grad, finish_out, *done(n.out_own0, n.out_own1), n.out_oth0_y, n.out_oth1_y)
    att = done(n.att_own0, n.att_own1, n.att_oth0_x, n.att_oth1_x)
    finish(z + 13, n.qkv_weight_grad, finish_qkv, *att)
    finish(z + 13, n.dense_weight_grad, finish_dense, att[1], att[3])
    finish(
        z + 14, n.in_weight_grad, finish_in, *done(n.in_own0, n.in_own1, n.in_oth0_x, n.in_oth1_x)
    )
    plan.run()
    def in_order(mine, got):
        return jnp.where(row == 0, jnp.concatenate([mine, got]), jnp.concatenate([got, mine]))

    by_feature = env[n.small2]
    by_col, by_col_got = (env[name][5 * width :] for name in (n.small_s, n.small_x))
    qkv_bias_grad = in_order(by_col[: 3 * HS], by_col_got[: 3 * HS]).reshape(2, 3 * HS)
    in_bias_grad = in_order(by_col[3 * HS :], by_col_got[3 * HS :])
    return (
        env[n.block_out],
        env[n.input_grad],
        by_feature[0],
        by_feature[1],
        by_feature[2],
        by_feature[3],
        env[n.qkv_weight_grad],
        qkv_bias_grad,
        env[n.dense_weight_grad],
        by_feature[4],
        env[n.in_weight_grad],
        in_bias_grad,
        env[n.out_weight_grad],
        by_feature[4],
    )


def solution(mesh):
    in_specs = (
        P(("dp", "col"), "row"),
        P("row"),
        P("row"),
        P("row"),
        P("row"),
        P("row", "col", None),
        P("col", None),
        P("col", None, "row"),
        P("row"),
        P("row", "col"),
        P("col"),
        P("col", "row"),
        P("row"),
        P(("dp", "col"), "row"),
    )
    out_specs = (
        P(("dp", "col"), "row"),
        P(("dp", "col"), "row"),
        P("row"),
        P("row"),
        P("row"),
        P("row"),
        P("row", "col", None),
        P("col", None),
        P("col", None, "row"),
        P("row"),
        P("row", "col"),
        P("col"),
        P("col", "row"),
        P("row"),
    )
    return jax.shard_map(
        per_device, mesh=mesh, in_specs=in_specs, out_specs=out_specs, check_vma=False
    )
```

time: 2140 us -> 582 us (0.27)
  waiting for transfers between devices: 1660 us -> 109 us
  Pallas kernels: 0 us -> 196 us
  matrix products: 190 us -> 3.59 us
  starting transfers between devices: 0.79 us -> 101 us
  blocking collectives: 93.1 us -> 0 us
    psum x1 -> x0, waiting for transfers between devices: 764 us -> none  [per_device(): lax.psum((qkv_grad_local, qkv_shift_grad, dense_grad, shift_out_grad, in_...]
    reduce_scatter x7 -> x0, waiting for transfers between devices: 549 us -> none  [the longest x1 191 us: per_device(): lax.psum_scatter(jnp.einsum('td,fd->tf', grad_all, out_weight, preferred_...]
    all_gather x7 -> x2, waiting for transfers between devices: 350 us -> 0.01 us  [gather_col(): return lax.all_gather(value, 'col', axis=0, tiled=True)]
    pallas_call x0 -> x31, Pallas kernels: none -> 196 us  [the longest x7 78.6 us: call(): pl.pallas_call(kernel if col is None else lambda _, *refs: kernel(*refs),...]
    dot_general x40 -> x2, matrix products: 190 us -> 3.59 us  [dot(): return lax.dot_general(a, b, (dims, ((), ())), preferred_element_type=F32)]
    ppermute x0 -> x63, waiting for transfers between devices: none -> 109 us  [the longest x20 45.8 us: swap_row(): return lax.ppermute(value, 'row', [(0, 1), (1, 0)])]
    ppermute x0 -> x63, starting transfers between devices: none -> 100 us  [the longest x29 68.4 us: send(): value = lax.ppermute(tie(beats.env[source], beats.token), 'dp', pairs)]
    psum x4 -> x0, blocking collectives: 93.1 us -> none  [the longest x1 62.8 us: per_device(): lax.psum((jnp.sum(attn_in_grad * normed, 0), jnp.sum(attn_in_grad, 0), jn...]
  transfers between devices with their start and end apart: 15 -> 65, of which waited for: 14 -> 26; matrix products, arithmetic and copies ran while one was open for 15% -> 11% of each run, Pallas kernels for 0% -> 31%
where the time goes in v1:
time: 582 us; the launch traced here: 578 us
  Pallas kernels  196 us (34%)
  waiting for transfers between devices  109 us (19%)
  starting transfers between devices  101 us (17%)
  other arithmetic  79.9 us (14%)
  local copies, waits for them, and re-layouts  73.3 us (13%)
  between operations  15.7 us (3%)
    pallas_call x7, Pallas kernels, call(): pl.pallas_call(kernel if col is None else lambda _, *refs: kernel(*refs),...  78.6 us
    ppermute x29, starting transfers between devices, send(): value = lax.ppermute(tie(beats.env[source], beats.token), 'dp', pairs)  68.4 us
    unnamed x266, local copies, waits for them, and re-layouts  47.2 us
    ppermute x20, waiting for transfers between devices, swap_row(): return lax.ppermute(value, 'row', [(0, 1), (1, 0)])  45.8 us
    ppermute x29, waiting for transfers between devices, send(): value = lax.ppermute(tie(beats.env[source], beats.token), 'dp', pairs)  44.7 us
    pallas_call x7, Pallas kernels, weight_grad(): pl.pallas_call(kernel, grid=(first[-1],), out_shape=tuple((jax.ShapeDtype...  42.7 us
    convert_element_type x14, other arithmetic, add_low(): return (a.astype(F32) + b.astype(F32)).astype(a.dtype)  31 us
    pallas_call x4, Pallas kernels, assemble(): pl.pallas_call(kernel, grid_spec=pltpu.PrefetchScalarGridSpec(num_scalar_...  24.6 us
  transfers between devices with their start and end apart: 65, of which 26 were waited for; matrix products, arithmetic and copies ran while one was open for 11% of the time, Pallas kernels for 31%

profile of v1, /device:TPU:0, one launch (start us, length us, event | category | flops | bytes accessed | tf_op | source)
XLA Modules:
  0.0 577.5 jit_solution(7220352366439271598)
XLA Ops:
  28.4 7.8 %collective-permute-done.gy.refs_3_ = f32[4,1024]{1,0:T(4,128)S(1)} collective-permute-done((f32[4,1024]{1,0:T(4,128)S(1)}, f32[4,1024]{1,0:T(4,128)S(1)}, u32[]{:S(2)}, u32[]{:S(2)}) %collective-permute-start) | collective-permute-done | bytes 16416 | tf_op jit(solution)/shard_map/ppermute | solution.py:29
  50.0 12.1 %collective-permute-done.5.y = bf16[512,1024]{1,0:T(8,128)(2,1)} collective-permute-done((bf16[512,1024]{1,0:T(8,128)(2,1)}, bf16[512,1024]{1,0:T(8,128)(2,1)}, u32[]{:S(2)}, u32[]{:S(2)}) %collective-permute-start.5) | collective-permute-done | bytes 1048608 | tf_op jit(solution)/shard_map/ppermute | solution.py:33
  81.1 7.3 %collective-permute-done.9.wy1_ref.refs_10_ = bf16[512,1024]{1,0:T(8,128)(2,1)S(1)} collective-permute-done((bf16[512,1024]{1,0:T(8,128)(2,1)}, bf16[512,1024]{1,0:T(8,128)(2,1)S(1)}, u32[]{:S(2)}, u32[]{:S(2)}) %collective-permute-start.9) | collective-permute-done | bytes 1048608 | tf_op jit(solution)/shard_map/ppermute | solution.py:29
  90.7 16.3 %pre_act.1 = (bf16[2048,1024]{1,0:T(8,128)(2,1)}, bf16[2048,1024]{1,0:T(8,128)(2,1)}) custom-call(bf16[2048,1024]{1,0:T(8,128)(2,1)} %get-tuple-element.511.x_ref.refs_0_, bf16[2048,1024]{1,0:T(8,128)(2,1)} %get-tuple-element.515.y_ref.refs_0_, bf16[1024,1024]{1,0:T(8,128)(2,1)} %constant_dynamic-slice_fusion.4.wx_ref.refs_8_, ...), custom_call_target="tpu_custom_call" | custom-call | tf_op jit(solution)/shard_map/pre_act/pallas_call | solution.py:93
  146.0 7.2 %collective-permute-start.14 = (bf16[512,1024]{1,0:T(8,128)(2,1)}, bf16[512,1024]{1,0:T(8,128)(2,1)}, u32[]{:S(2)}, u32[]{:S(2)}) collective-permute-start(bf16[512,1024]{1,0:T(8,128)(2,1)} %weight_grad.8), channel_id=1, source_target_pairs={{0,8},{24,16},{1,9},{25,17},{2,10},{26,18},{3,11},{27,19},{4,12},{... | collective-permute-start | bytes 3145736 | tf_op jit(solution)/shard_map/ppermute | solution.py:739
  182.7 11.5 %pre_grad.1 = (bf16[2048,1024]{1,0:T(8,128)(2,1)S(1)}, f32[1,1024]{1,0:T(1,128)S(1)}) custom-call(bf16[2048,1024]{1,0:T(8,128)(2,1)S(1)} %copy-done.15, bf16[2048,1024]{1,0:T(8,128)(2,1)} %all-gather.5.cloned.1.call-done.refs_1_.gy_ref.refs_3_, bf16[1024,1024]{1,0:T(8,128)(2,1)S(1)} %copy-done.24, bf16[512,1024]{1,0:T(8,128)(2,1)S(1)} %copy-done.36, ...), custom_call_target="tpu_custom_call" | custom-call | tf_op jit(solution)/shard_map/pre_grad/pallas_call | solution.py:93
  194.1 6.9 %collective-permute-done.18 = bf16[640,768]{1,0:T(8,128)(2,1)S(1)} collective-permute-done((bf16[640,768]{1,0:T(8,128)(2,1)S(1)}, bf16[640,768]{1,0:T(8,128)(2,1)S(1)}, u32[]{:S(2)}, u32[]{:S(2)}) %collective-permute-start.18) | collective-permute-done | bytes 983072 | tf_op jit(solution)/shard_map/ppermute | solution.py:29
  216.6 7.1 %weight_grad.11 = (bf16[512,1024]{1,0:T(8,128)(2,1)}, bf16[512,1024]{1,0:T(8,128)(2,1)}) custom-call(bf16[2048,1024]{1,0:T(8,128)(2,1)S(1)} %copy-done.9, bf16[2048,1024]{1,0:T(8,128)(2,1)S(1)} %get-tuple-element.512.refs_1_.refs_5_), custom_call_target="tpu_custom_call" | custom-call | tf_op jit(solution)/shard_map/weight_grad/pallas_call | solution.py:262
  223.7 6.1 %collective-permute-done.22.refs_3_ = bf16[256,1024]{1,0:T(8,128)(2,1)S(1)} collective-permute-done((bf16[256,1024]{1,0:T(8,128)(2,1)}, bf16[256,1024]{1,0:T(8,128)(2,1)S(1)}, u32[]{:S(2)}, u32[]{:S(2)}) %collective-permute-start.22) | collective-permute-done | bytes 524320 | tf_op jit(solution)/shard_map/ppermute | solution.py:29
  235.6 13.4 %collective-permute-start.23 = (bf16[512,1024]{1,0:T(8,128)(2,1)}, bf16[512,1024]{1,0:T(8,128)(2,1)}, u32[]{:S(2)}, u32[]{:S(2)}) collective-permute-start(bf16[512,1024]{1,0:T(8,128)(2,1)} %add_convert_fusion.18), channel_id=1, source_target_pairs={{8,16},{16,8},{9,17},{17,9},{10,18},{18,10},{11,19},{19,11},{12,20... | collective-permute-start | bytes 3145736 | tf_op jit(solution)/shard_map/ppermute | solution.py:739
  251.2 9.3 %packed.1 = (bf16[2048,256]{1,0:T(8,128)(2,1)S(1)}, bf16[2048,256]{1,0:T(8,128)(2,1)S(1)}, bf16[2048,256]{1,0:T(8,128)(2,1)S(1)}) custom-call(bf16[2048,1024]{1,0:T(8,128)(2,1)S(1)} %copy-done.5, bf16[2048,1024]{1,0:T(8,128)(2,1)} %get-tuple-element.536.y_ref.refs_1_, bf16[1024,768]{1,0:T(8,128)(2,1)S(1)} %dynamic-slice_bitcast_fusion.wx_ref.refs_6_, ...), custom_call_target="tpu_custom_call" | custom-call | tf_op jit(solution)/shard_map/packed/pallas_call | solution.py:93
  278.8 16.4 %attention.1 = (bf16[4,512,256]{2,1,0:T(8,128)(2,1)}, bf16[4,512,768]{2,1,0:T(8,128)(2,1)}, f32[1,768]{1,0:T(1,128)}) custom-call(bf16[4,512,256]{2,1,0:T(8,128)(2,1)} %bitcast.60, bf16[4,512,256]{2,1,0:T(8,128)(2,1)} %bitcast.61, bf16[4,512,256]{2,1,0:T(8,128)(2,1)} %bitcast.62, bf16[4,512,256]{2,1,0:T(8,128)(2,1)} %bitcast.64, f32[4,512,128]{2,1,0:T(8,128)} %bitcast.59, ...), custom_call_target="tpu_custom_call" | custom-call | tf_op jit(solution)/shard_map/attention/pallas_call | solution.py:389
  308.7 7.9 %weight_grad.12 = (bf16[512,1024]{1,0:T(8,128)(2,1)S(1)}, bf16[512,1024]{1,0:T(8,128)(2,1)S(1)}) custom-call(bf16[2048,768]{1,0:T(8,128)(2,1)S(1)} %bitcast.51, bf16[2048,1024]{1,0:T(8,128)(2,1)S(1)} %copy-done.6, bf16[2048,256]{1,0:T(8,128)(2,1)S(1)} %bitcast.53, bf16[2048,1024]{1,0:T(8,128)(2,1)} %all-gather.3.cloned.1.call-done.refs_1_.gx_ref.refs_3_), custom_call_target="tpu_custom_call" | custom-call | tf_op jit(solution)/shard_map/weight_grad/pallas_call | solution.py:262
  316.7 9.2 %weight_grad.13 = (bf16[512,1024]{1,0:T(8,128)(2,1)S(1)}, bf16[512,1024]{1,0:T(8,128)(2,1)}) custom-call(bf16[2048,768]{1,0:T(8,128)(2,1)S(1)} %bitcast.52, bf16[2048,1024]{1,0:T(8,128)(2,1)S(1)} %copy-done.7, bf16[2048,256]{1,0:T(8,128)(2,1)S(1)} %bitcast.54, bf16[2048,1024]{1,0:T(8,128)(2,1)} %all-gather.5.cloned.1.call-done.refs_1_.gy_ref.refs_3_), custom_call_target="tpu_custom_call" | custom-call | tf_op jit(solution)/shard_map/weight_grad/pallas_call | solution.py:262
  338.7 12.9 %norm_grad.2 = (bf16[1024,2048]{1,0:T(8,128)(2,1)}, f32[4,2048]{1,0:T(4,128)S(1)}) custom-call(s32[1]{0:T(128)} %bitcast.4._, bf16[1024,1024]{1,0:T(8,128)(2,1)S(1)} %copy-done.53, bf16[1024,1024]{1,0:T(8,128)(2,1)S(1)} %copy-done.49, f32[4,1024]{1,0:T(4,128)S(1)} %copy-done.102, f32[4,1024]{1,0:T(4,128)S(1)} %copy-done.104, bf16[2048,768]{1,0:T(8,128)(2,1)} %bitcast.49, ...), custom_call_target="tpu_custom_call" | custom-call | tf_op jit(solution)/shard_map/norm_grad/pallas_call | solution.py:93
  370.6 13.1 %norm_grad.3 = (bf16[1024,2048]{1,0:T(8,128)(2,1)}, f32[4,2048]{1,0:T(4,128)S(1)}) custom-call(s32[1]{0:T(128)} %bitcast.4._, bf16[1024,1024]{1,0:T(8,128)(2,1)S(1)} %copy-done.55, bf16[1024,1024]{1,0:T(8,128)(2,1)S(1)} %copy-done.57, f32[4,1024]{1,0:T(4,128)S(1)} %copy-done.102, f32[4,1024]{1,0:T(4,128)S(1)} %copy-done.104, bf16[2048,768]{1,0:T(8,128)(2,1)} %bitcast.50, ...), custom_call_target="tpu_custom_call" | custom-call | tf_op jit(solution)/shard_map/norm_grad/pallas_call | solution.py:93
  403.7 8.2 %mixed.2 = bf16[1024,2048]{1,0:T(8,128)(2,1)} custom-call(s32[1]{0:T(128)} %bitcast.4._, bf16[2048,256]{1,0:T(8,128)(2,1)S(1)} %bitcast.55, bf16[2048,1024]{1,0:T(8,128)(2,1)} %get-tuple-element.476.refs_0_.refs_1_, bf16[256,1024]{1,0:T(8,128)(2,1)S(1)} %copy-done.51, bf16[256,1024]{1,0:T(8,128)(2,1)S(1)} %copy-done.91, bf16[1024,1024]{1,0:T(8,128)(2,1)S(1)} %copy-done.25, ...), custom_call_target="tpu_custom_call" | custom-call | tf_op jit(solution)/shard_map/mixed/pallas_call | solution.py:93
  413.4 6.3 %collective-permute-done.40 = f32[12032]{0:T(1024)S(1)} collective-permute-done((f32[12032]{0:T(1024)S(1)}, f32[12032]{0:T(1024)S(1)}, u32[]{:S(2)}, u32[]{:S(2)}) %collective-permute-start.40) | collective-permute-done | bytes 48160 | tf_op jit(solution)/shard_map/ppermute | solution.py:739
  430.6 7.3 %mixed.3.refs_0_ = bf16[1024,2048]{1,0:T(8,128)(2,1)S(1)} custom-call(s32[1]{0:T(128)} %bitcast.4._, bf16[2048,256]{1,0:T(8,128)(2,1)S(1)} %bitcast.56, bf16[2048,1024]{1,0:T(8,128)(2,1)} %get-tuple-element.476.refs_0_.refs_1_, bf16[256,1024]{1,0:T(8,128)(2,1)S(1)} %copy-done.51, bf16[256,1024]{1,0:T(8,128)(2,1)S(1)} %copy-done.91, ...), custom_call_target="tpu_custom_call" | custom-call | tf_op jit(solution)/shard_map/mixed/pallas_call | solution.py:93
  437.9 13.9 %collective-permute-done.46.refs_2_.refs_0_ = bf16[512,1024]{1,0:T(8,128)(2,1)S(1)} collective-permute-done((bf16[512,1024]{1,0:T(8,128)(2,1)S(1)}, bf16[512,1024]{1,0:T(8,128)(2,1)S(1)}, u32[]{:S(2)}, u32[]{:S(2)}) %collective-permute-start.46) | collective-permute-done | bytes 1048608 | tf_op jit(solution)/shard_map/ppermute | solution.py:739
  481.2 11.6 %collective-permute-done.50 = f32[12032]{0:T(1024)S(1)} collective-permute-done((f32[12032]{0:T(1024)S(1)}, f32[12032]{0:T(1024)S(1)}, u32[]{:S(2)}, u32[]{:S(2)}) %collective-permute-start.50) | collective-permute-done | bytes 48160 | tf_op jit(solution)/shard_map/ppermute | solution.py:739
  514.2 7.3 %out_grad.1 = f32[2048,1024]{1,0:T(8,128)} custom-call(s32[2]{0:T(128)S(1)} %pad_add_fusion.meta_ref, bf16[512,1024]{1,0:T(8,128)(2,1)S(1)} %copy-done.61, bf16[512,1024]{1,0:T(8,128)(2,1)S(1)} %copy-done.59, bf16[512,1024]{1,0:T(8,128)(2,1)S(1)} %copy-done.65, bf16[512,1024]{1,0:T(8,128)(2,1)S(1)} %copy-done.63, bf16[512,1024]{1,0:T(8,128)(2,1)S(1)} %copy-done.93, ...), custom_call_target="tpu_custom_call" | custom-call | tf_op jit(solution)/shard_map/out_grad/pallas_call | solution.py:488
  546.1 6.7 %qkv_grad.1 = f32[1024,2,768]{2,1,0:T(2,128)} custom-call(s32[2]{0:T(128)S(1)} %pad_add_fusion.1.meta_ref, bf16[512,1024]{1,0:T(8,128)(2,1)S(1)} %copy-done.73, bf16[512,1024]{1,0:T(8,128)(2,1)S(1)} %copy-done.71, bf16[512,1024]{1,0:T(8,128)(2,1)S(1)} %collective-permute-done.46.refs_2_.refs_0_, bf16[512,1024]{1,0:T(8,128)(2,1)S(1)} %fusion.27.refs_3_.refs_1_, ...), custom_call_target="tpu_custom_call" | custom-call | tf_op jit(solution)/shard_map/qkv_grad/pallas_call | solution.py:488
  562.1 7.1 %in_grad.1 = f32[1024,2048]{1,0:T(8,128)} custom-call(s32[2]{0:T(128)S(1)} %pad_add_fusion.3.meta_ref, bf16[512,1024]{1,0:T(8,128)(2,1)} %collective-permute-done.30.refs_0_, bf16[512,1024]{1,0:T(8,128)(2,1)} %fusion.23.refs_1_, bf16[512,1024]{1,0:T(8,128)(2,1)S(1)} %copy-done.69, bf16[512,1024]{1,0:T(8,128)(2,1)S(1)} %copy-done.67, ...), custom_call_target="tpu_custom_call" | custom-call | tf_op jit(solution)/shard_map/in_grad/pallas_call | solution.py:488
  (497 shorter events, 328.9 us)
Async XLA Ops:
  7.2 99.8 %all-gather.3.cloned.1.call-start = ((), (), s32[]{:S(2)}) async-start(), calls=%async_computation | async-start | bytes 5242880 | tf_op jit(solution)/shard_map/all_gather | solution.py:814
  7.2 28.9 %collective-permute-start.3 = (bf16[512,1024]{1,0:T(8,128)(2,1)}, bf16[512,1024]{1,0:T(8,128)(2,1)S(1)}, u32[]{:S(2)}, u32[]{:S(2)}) collective-permute-start(bf16[512,1024]{1,0:T(8,128)(2,1)} %x.2), channel_id=1, source_target_pairs={{0,1},{1,0},{2,3},{3,2},{4,5},{5,4},{6,7},{7,6},{8,9},{9,8},{10,11... | collective-permute-start | bytes 3145736 | tf_op jit(solution)/shard_map/ppermute | solution.py:33
  7.8 28.4 %collective-permute-start.2 = (bf16[512,1024]{1,0:T(8,128)(2,1)}, bf16[512,1024]{1,0:T(8,128)(2,1)}, u32[]{:S(2)}, u32[]{:S(2)}) collective-permute-start(bf16[512,1024]{1,0:T(8,128)(2,1)} %x.2), channel_id=1, source_target_pairs={{0,2},{1,3},{2,0},{3,1},{4,6},{5,7},{6,4},{7,5},{8,10},{9,11},{10,... | collective-permute-start | bytes 3145736 | tf_op jit(solution)/shard_map/ppermute | solution.py:33
  10.4 25.8 %collective-permute-start.1 = (bf16[512,1024]{1,0:T(8,128)(2,1)}, bf16[512,1024]{1,0:T(8,128)(2,1)}, u32[]{:S(2)}, u32[]{:S(2)}) collective-permute-start(bf16[512,1024]{1,0:T(8,128)(2,1)} %x.2), channel_id=1, source_target_pairs={{0,4},{4,0},{1,5},{5,1},{2,6},{6,2},{3,7},{7,3},{8,12},{12,8},{9,1... | collective-permute-start | bytes 3145736 | tf_op jit(solution)/shard_map/ppermute | solution.py:29
  36.3 25.9 %collective-permute-start.5 = (bf16[512,1024]{1,0:T(8,128)(2,1)}, bf16[512,1024]{1,0:T(8,128)(2,1)}, u32[]{:S(2)}, u32[]{:S(2)}) collective-permute-start(bf16[512,1024]{1,0:T(8,128)(2,1)} %collective-permute-done.1.y), channel_id=1, source_target_pairs={{0,2},{1,3},{2,0},{3,1},{4,6},{5,7},{6,4},{7,5},{8,10},{9,11},{10,... | collective-permute-start | bytes 3145736 | tf_op jit(solution)/shard_map/ppermute | solution.py:33
  36.6 25.5 %collective-permute-start.7 = (bf16[512,1024]{1,0:T(8,128)(2,1)}, bf16[512,1024]{1,0:T(8,128)(2,1)}, u32[]{:S(2)}, u32[]{:S(2)}) collective-permute-start(bf16[512,1024]{1,0:T(8,128)(2,1)} %collective-permute-done.2.x), channel_id=1, source_target_pairs={{0,1},{1,0},{2,3},{3,2},{4,5},{5,4},{6,7},{7,6},{8,9},{9,8},{10,11... | collective-permute-start | bytes 3145736 | tf_op jit(solution)/shard_map/ppermute | solution.py:33
  36.8 25.7 %collective-permute-start.4 = (bf16[512,1024]{1,0:T(8,128)(2,1)}, bf16[512,1024]{1,0:T(8,128)(2,1)}, u32[]{:S(2)}, u32[]{:S(2)}) collective-permute-start(bf16[512,1024]{1,0:T(8,128)(2,1)} %constant_dynamic-slice_fusion.5), channel_id=1, source_target_pairs={{0,4},{4,0},{1,5},{5,1},{2,6},{6,2},{3,7},{7,3},{8,12},{12,8},{9,1... | collective-permute-start | bytes 3145736 | tf_op jit(solution)/shard_map/ppermute | solution.py:29
  62.5 90.7 %all-gather.5.cloned.1.call-start = ((), (), s32[]{:S(2)}) async-start(), calls=%async_computation.1 | async-start | bytes 5242880 | tf_op jit(solution)/shard_map/all_gather | solution.py:814
  62.6 25.8 %collective-permute-start.9 = (bf16[512,1024]{1,0:T(8,128)(2,1)}, bf16[512,1024]{1,0:T(8,128)(2,1)S(1)}, u32[]{:S(2)}, u32[]{:S(2)}) collective-permute-start(bf16[512,1024]{1,0:T(8,128)(2,1)} %constant_dynamic-slice_fusion.6), channel_id=1, source_target_pairs={{0,4},{4,0},{1,5},{5,1},{2,6},{6,2},{3,7},{7,3},{8,12},{12,8},{9,1... | collective-permute-start | bytes 3145736 | tf_op jit(solution)/shard_map/ppermute | solution.py:29
  88.4 25.9 %collective-permute-start.10 = (bf16[512,1024]{1,0:T(8,128)(2,1)}, bf16[512,1024]{1,0:T(8,128)(2,1)}, u32[]{:S(2)}, u32[]{:S(2)}) collective-permute-start(bf16[512,1024]{1,0:T(8,128)(2,1)} %param.27), channel_id=1, source_target_pairs={{0,4},{4,0},{1,5},{5,1},{2,6},{6,2},{3,7},{7,3},{8,12},{12,8},{9,1... | collective-permute-start | bytes 3145736 | tf_op jit(solution)/shard_map/ppermute | solution.py:29
  115.7 25.9 %collective-permute-start.11 = (bf16[512,1024]{1,0:T(8,128)(2,1)}, bf16[512,1024]{1,0:T(8,128)(2,1)S(1)}, u32[]{:S(2)}, u32[]{:S(2)}) collective-permute-start(bf16[512,1024]{1,0:T(8,128)(2,1)} %copy-done.86), channel_id=1, source_target_pairs={{0,8},{24,16},{1,9},{25,17},{2,10},{26,18},{3,11},{27,19},{4,12},{... | collective-permute-start | bytes 3145736 | tf_op jit(solution)/shard_map/ppermute | solution.py:739
  146.0 26.9 %collective-permute-start.14 = (bf16[512,1024]{1,0:T(8,128)(2,1)}, bf16[512,1024]{1,0:T(8,128)(2,1)}, u32[]{:S(2)}, u32[]{:S(2)}) collective-permute-start(bf16[512,1024]{1,0:T(8,128)(2,1)} %weight_grad.8), channel_id=1, source_target_pairs={{0,8},{24,16},{1,9},{25,17},{2,10},{26,18},{3,11},{27,19},{4,12},{... | collective-permute-start | bytes 3145736 | tf_op jit(solution)/shard_map/ppermute | solution.py:739
  203.3 26.5 %collective-permute-start.20 = (bf16[512,1024]{1,0:T(8,128)(2,1)S(1)}, bf16[512,1024]{1,0:T(8,128)(2,1)S(1)}, u32[]{:S(2)}, u32[]{:S(2)}) collective-permute-start(bf16[512,1024]{1,0:T(8,128)(2,1)S(1)} %fusion.20.refs_3_), channel_id=1, source_target_pairs={{0,8},{24,16},{8,0},{16,24},{1,9},{25,17},{9,1},{17,25},{2,10},{26... | collective-permute-start | bytes 3145736 | tf_op jit(solution)/shard_map/ppermute | solution.py:739
  234.5 30.8 %collective-permute-start.24 = (bf16[512,1024]{1,0:T(8,128)(2,1)}, bf16[512,1024]{1,0:T(8,128)(2,1)}, u32[]{:S(2)}, u32[]{:S(2)}) collective-permute-start(bf16[512,1024]{1,0:T(8,128)(2,1)} %fusion.21.refs_1_), channel_id=1, source_target_pairs={{0,8},{24,16},{8,0},{16,24},{1,9},{25,17},{9,1},{17,25},{2,10},{26... | collective-permute-start | bytes 3145736 | tf_op jit(solution)/shard_map/ppermute | solution.py:739
  235.6 29.7 %collective-permute-start.23 = (bf16[512,1024]{1,0:T(8,128)(2,1)}, bf16[512,1024]{1,0:T(8,128)(2,1)}, u32[]{:S(2)}, u32[]{:S(2)}) collective-permute-start(bf16[512,1024]{1,0:T(8,128)(2,1)} %add_convert_fusion.18), channel_id=1, source_target_pairs={{8,16},{16,8},{9,17},{17,9},{10,18},{18,10},{11,19},{19,11},{12,20... | collective-permute-start | bytes 3145736 | tf_op jit(solution)/shard_map/ppermute | solution.py:739
  354.8 33.0 %collective-permute-start.38 = (bf16[1024,2048]{1,0:T(8,128)(2,1)}, bf16[1024,2048]{1,0:T(8,128)(2,1)}, u32[]{:S(2)}, u32[]{:S(2)}) collective-permute-start(bf16[1024,2048]{1,0:T(8,128)(2,1)} %get-tuple-element.637), channel_id=1, source_target_pairs={{0,1},{1,0},{2,3},{3,2},{4,5},{5,4},{6,7},{7,6},{8,9},{9,8},{10,11... | collective-permute-start | bytes 12582920 | tf_op jit(solution)/shard_map/ppermute | solution.py:33
  357.8 26.8 %collective-permute-start.36 = (bf16[512,1024]{1,0:T(8,128)(2,1)}, bf16[512,1024]{1,0:T(8,128)(2,1)}, u32[]{:S(2)}, u32[]{:S(2)}) collective-permute-start(bf16[512,1024]{1,0:T(8,128)(2,1)} %fusion.25.refs_5_), channel_id=1, source_target_pairs={{0,8},{24,16},{8,0},{16,24},{1,9},{25,17},{9,1},{17,25},{2,10},{26... | collective-permute-start | bytes 3145736 | tf_op jit(solution)/shard_map/ppermute | solution.py:739
  362.1 25.6 %collective-permute-start.37 = (bf16[512,1024]{1,0:T(8,128)(2,1)}, bf16[512,1024]{1,0:T(8,128)(2,1)}, u32[]{:S(2)}, u32[]{:S(2)}) collective-permute-start(bf16[512,1024]{1,0:T(8,128)(2,1)} %get-tuple-element.635), channel_id=1, source_target_pairs={{0,4},{4,0},{1,5},{5,1},{2,6},{6,2},{3,7},{7,3},{8,12},{12,8},{9,1... | collective-permute-start | bytes 3145736 | tf_op jit(solution)/shard_map/ppermute | solution.py:29
  394.1 25.6 %collective-permute-start.43 = (bf16[256,2048]{1,0:T(8,128)(2,1)S(1)}, bf16[256,2048]{1,0:T(8,128)(2,1)S(1)}, u32[]{:S(2)}, u32[]{:S(2)}) collective-permute-start(bf16[256,2048]{1,0:T(8,128)(2,1)S(1)} %rowwise.10), channel_id=1, source_target_pairs={{0,2},{1,3},{2,0},{3,1},{4,6},{5,7},{6,4},{7,5},{8,10},{9,11},{10,... | collective-permute-start | bytes 3145736 | tf_op jit(solution)/shard_map/ppermute | solution.py:33
  422.5 32.0 %collective-permute-start.48 = (bf16[1024,2048]{1,0:T(8,128)(2,1)}, bf16[1024,2048]{1,0:T(8,128)(2,1)S(1)}, u32[]{:S(2)}, u32[]{:S(2)}) collective-permute-start(bf16[1024,2048]{1,0:T(8,128)(2,1)} %mixed.2), channel_id=1, source_target_pairs={{0,1},{1,0},{2,3},{3,2},{4,5},{5,4},{6,7},{7,6},{8,9},{9,8},{10,11... | collective-permute-start | bytes 12582920 | tf_op jit(solution)/shard_map/ppermute | solution.py:33
  426.1 25.6 %collective-permute-start.46 = (bf16[512,1024]{1,0:T(8,128)(2,1)S(1)}, bf16[512,1024]{1,0:T(8,128)(2,1)S(1)}, u32[]{:S(2)}, u32[]{:S(2)}) collective-permute-start(bf16[512,1024]{1,0:T(8,128)(2,1)S(1)} %fusion.27.refs_3_.refs_1_), channel_id=1, source_target_pairs={{0,8},{24,16},{8,0},{16,24},{1,9},{25,17},{9,1},{17,25},{2,10},{26... | collective-permute-start | bytes 3145736 | tf_op jit(solution)/shard_map/ppermute | solution.py:739
  465.9 26.9 %collective-permute-start.53 = (bf16[256,2048]{1,0:T(8,128)(2,1)}, bf16[256,2048]{1,0:T(8,128)(2,1)S(1)}, u32[]{:S(2)}, u32[]{:S(2)}) collective-permute-start(bf16[256,2048]{1,0:T(8,128)(2,1)} %rowwise.13), channel_id=1, source_target_pairs={{0,2},{1,3},{2,0},{3,1},{4,6},{5,7},{6,4},{7,5},{8,10},{9,11},{10,... | collective-permute-start | bytes 3145736 | tf_op jit(solution)/shard_map/ppermute | solution.py:33
  466.5 26.2 %collective-permute-start.52 = (bf16[512,1024]{1,0:T(8,128)(2,1)}, bf16[512,1024]{1,0:T(8,128)(2,1)}, u32[]{:S(2)}, u32[]{:S(2)}) collective-permute-start(bf16[512,1024]{1,0:T(8,128)(2,1)} %get-tuple-element.696), channel_id=1, source_target_pairs={{0,4},{4,0},{1,5},{5,1},{2,6},{6,2},{3,7},{7,3},{8,12},{12,8},{9,1... | collective-permute-start | bytes 3145736 | tf_op jit(solution)/shard_map/ppermute | solution.py:29
  533.3 25.7 %collective-permute-start.61 = (bf16[512,1024]{1,0:T(8,128)(2,1)}, bf16[512,1024]{1,0:T(8,128)(2,1)}, u32[]{:S(2)}, u32[]{:S(2)}) collective-permute-start(bf16[512,1024]{1,0:T(8,128)(2,1)} %add_convert_fusion.refs_7_), channel_id=1, source_target_pairs={{8,0},{16,24},{9,1},{17,25},{10,2},{18,26},{11,3},{19,27},{12,4},{... | collective-permute-start | bytes 3145736 | tf_op jit(solution)/shard_map/ppermute | solution.py:739
  (173 other events, 2085.4 us)
Sparse Core Ops, SparseCore 0:
  62.6 35.9 all-gather.2
  115.5 34.7 all-gather.4

commit v2 on v1

--- a/solution.py
+++ b/solution.py
@@ -79,7 +79,7 @@
     return (0, 0)
 
 
-def call(kernel, name, steps, ins, outs, col=None, vmem=40, tile=None):
+def call(kernel, name, steps, ins, outs, col=None, vmem=28, tile=None):
     def block(shape, index, rows=None):
         rows = rows or (shape[0] if index is fixed else tile or shape[0] // steps)
         return pl.BlockSpec((rows, shape[1]), index)
@@ -137,7 +137,7 @@
         ),
         out_shape=(jax.ShapeDtypeStruct((slots * rows, feats), BF),) * 4,
         input_output_aliases={5 + i: i for i in range(len(before))},
-        compiler_params=pltpu.CompilerParams(vmem_limit_bytes=56 * MIB),
+        compiler_params=pltpu.CompilerParams(vmem_limit_bytes=58 * MIB),
         cost_estimate=COST,
         name="norm",
     )(col.reshape(1), x, y, gx, gy, *before)
@@ -163,11 +163,11 @@
         tokens // tile,
         [(x, tiled), (y, tiled), (wx, fixed), (wy0, fixed), (wy1, fixed), (bias.reshape(1, -1), fixed)],
         [((tokens, units), BF, tile, tiled)] * 2,
-        vmem=56,
-    )
-
-
-def rowwise(fn, rows, outs, *ins, flag=None):
+        vmem=58,
+    )
+
+
+def rowwise(fn, rows, outs, *ins, flag=None, vmem=20, whole=None, skip=0, before=()):
     tile = 256
     ins = [i if isinstance(i, tuple) else (i, 0) for i in ins]
     flags = [] if flag is None else [flag.astype(jnp.int32).reshape(1)]
@@ -179,22 +179,25 @@
         values = [ref[0] != 0 for ref in refs[: len(flags)]]
         refs = refs[len(flags) :]
         results = fn(*values, *[ref[...] for ref in refs[: len(ins)]])
-        for ref, result in zip(refs[len(ins) :], results, strict=True):
+        for ref, result in zip(refs[len(ins) + len(before) :], results, strict=True):
             ref[...] = result
 
+    first_in = len(flags) + len(ins)
     return pl.pallas_call(
         kernel,
         grid_spec=pltpu.PrefetchScalarGridSpec(
             num_scalar_prefetch=len(flags),
             grid=(rows // tile,),
-            in_specs=[pl.BlockSpec((tile, a.shape[1]), at(first)) for a, first in ins],
-            out_specs=tuple(pl.BlockSpec((tile, cols), tiled) for cols, _ in outs),
+            in_specs=[pl.BlockSpec((tile, a.shape[1]), at(first)) for a, first in ins]
+            + [pl.BlockSpec(memory_space=pl.ANY)] * len(before),
+            out_specs=tuple(pl.BlockSpec((tile, cols), at(skip)) for cols, _ in outs),
         ),
-        out_shape=tuple(jax.ShapeDtypeStruct((rows, cols), dtype) for cols, dtype in outs),
-        compiler_params=pltpu.CompilerParams(vmem_limit_bytes=32 * MIB),
+        out_shape=tuple(jax.ShapeDtypeStruct((whole or rows, cols), dtype) for cols, dtype in outs),
+        input_output_aliases={first_in + i: i for i in range(len(before))},
+        compiler_params=pltpu.CompilerParams(vmem_limit_bytes=vmem * MIB),
         cost_estimate=COST,
         name="rowwise",
-    )(*flags, *[a for a, _ in ins])
+    )(*flags, *[a for a, _ in ins], *before)
 
 
 def plain_add(a, b):
@@ -219,7 +222,7 @@
     return lambda value, a, b: jnp.where(flag, value, add_low(a, b))
 
 
-def weight_grad(cuts, a, b, last_a=None, last_b=None):
+def weight_grad(cuts, a, b, last_a=None, last_b=None, vmem=20):
     tokens, cols, tile = b.shape[0], b.shape[1], 256
     own = sum(cuts) // tile if last_a is None else a.shape[1] // tile
     skip = 0
@@ -267,7 +270,7 @@
         out_specs=tuple(
             pl.BlockSpec((tile, cols), index(s, e)) for s, e in zip(first[:-1], first[1:], strict=True)
         ),
-        compiler_params=pltpu.CompilerParams(vmem_limit_bytes=40 * MIB),
+        compiler_params=pltpu.CompilerParams(vmem_limit_bytes=vmem * MIB),
         cost_estimate=COST,
         name="weight_grad",
     )(*ins)
@@ -396,7 +399,7 @@
         in_specs=[vmem] * 7,
         out_specs=(vmem,) * 3,
         scratch_shapes=[pltpu.VMEM((slots, rows, HS), F32)] * 2,
-        compiler_params=pltpu.CompilerParams(vmem_limit_bytes=56 * MIB),
+        compiler_params=pltpu.CompilerParams(vmem_limit_bytes=48 * MIB),
         cost_estimate=COST,
         name="attention",
     )(*[a.reshape(slots, rows, a.shape[1]) for a in (q, k, v, g, cos, low, high)])
@@ -466,12 +469,14 @@
         ins + [(w, fixed) for w in weights],
         [((tokens, width), BF, tile, tiled), ((4, width), F32, 4, fixed)],
         col,
+        vmem=58,
         tile=tile,
     )
 
 
-def assemble(name, meta, arrays, steps, out, fill):
+def assemble(name, meta, arrays, steps, out, fill, before=None):
     flat = [a for _, _, part in arrays for a in part]
+    rest = [] if before is None else [before]
     shape, block, index = out
 
     def kernel(meta_ref, *refs):
@@ -490,14 +495,16 @@
         grid_spec=pltpu.PrefetchScalarGridSpec(
             num_scalar_prefetch=1,
             grid=(steps,),
-            in_specs=[pl.BlockSpec(block, index) for block, index, part in arrays for _ in part],
+            in_specs=[pl.BlockSpec(block, index) for block, index, part in arrays for _ in part]
+            + [pl.BlockSpec(memory_space=pl.ANY)] * len(rest),
             out_specs=pl.BlockSpec(block, index),
         ),
         out_shape=jax.ShapeDtypeStruct(shape, F32),
-        compiler_params=pltpu.CompilerParams(vmem_limit_bytes=48 * MIB),
+        input_output_aliases={1 + len(flat): 0} if rest else {},
+        compiler_params=pltpu.CompilerParams(vmem_limit_bytes=58 * MIB),
         cost_estimate=COST,
         name=name,
-    )(meta, *flat)
+    )(meta, *flat, *rest)
 
 
 def rows_of(part, tiles):
@@ -523,22 +530,19 @@
     return assemble("out_grad", meta, arrays, 4 * tiles, ((4 * rows, cols), block, index), fill)
 
 
-def finish_in(meta, parts):
+def finish_in(meta, parts, before=None):
     rows, cols = parts[0][0].shape
     tile, tiles = 256, rows // 256
+    skip = 0 if before is None else tiles
 
     def fill(read, row, out_ref):
-        for k in range(2):
-
-            @pl.when(pl.program_id(0) // tiles == k)
-            def _():
-                mine, other = read(k), read(2 + k)
-                out_ref[:, :cols] = jnp.where(row == 0, mine, other)
-                out_ref[:, cols:] = jnp.where(row == 0, other, mine)
-
-    arrays = [((tile, cols), rows_of(k % 2, tiles), part) for k, part in enumerate(parts)]
-    out = ((2 * rows, 2 * cols), (tile, 2 * cols), tiled)
-    return assemble("in_grad", meta, arrays, 2 * tiles, out, fill)
+        mine, other = read(0), read(1)
+        out_ref[:, :cols] = jnp.where(row == 0, mine, other)
+        out_ref[:, cols:] = jnp.where(row == 0, other, mine)
+
+    arrays = [((tile, cols), tiled, part) for part in parts]
+    out = ((2 * rows, 2 * cols), (tile, 2 * cols), lambda i, *_: (i + skip, 0))
+    return assemble("in_grad", meta, arrays, tiles, out, fill, before)
 
 
 def finish_qkv(meta, parts):
@@ -696,37 +700,39 @@
             src = self.pairs(step - 1)
             return choose(self.on(src[0][1], src[1][1])), inputs
 
+        for name, step in moving:
+            match = [
+                m
+                for m in moving
+                if step >= mid
+                and m[1] == 2 * mid - 2 - step
+                and env[m[0]].shape == env[name].shape
+                and m not in outward
+            ]
+            if match:
+                outward[match[0]] = (name, step)
+        joint = self.add_jointly(beats, moving, outward)
         for name, step in sorted(moving, key=lambda m: (m[1] != mid - 1, m[1] < mid)):
-            fn, inputs = update(name, step)
-            values = [env[i] for i in inputs]
-            if step >= mid:
-                match = [
-                    m
-                    for m in moving
-                    if m[1] == 2 * mid - 2 - step and env[m[0]].shape == env[name].shape and m not in outward
-                ]
-                if match:
-                    inner = match[0]
-                    outward[inner] = (name, step)
-                    continue
-            if step < mid - 1 and (name, step) in outward:
+            if (name, step) in outward or (name, step) in outward.values():
                 continue
-            if step:
-                beats.do((name, "held"), fn, *values)
+            if step and (name, step) not in joint:
+                fn, inputs = update(name, step)
+                beats.do((name, "held"), fn, *[env[i] for i in inputs])
             self.send(beats, self.pairs(step), (name, "held"), [(name, step)])
         for (name, step), (far, far_step) in outward.items():
-            fn, inputs = update(name, step)
-            if step:
-                beats.do((name, "held"), fn, *[env[i] for i in inputs])
-            inputs = update(far, far_step)[1]
-            outer = self.on(step, self.count - 1 - step)
-            if far_step > mid:
-                gets = self.on(*[pair[1] for pair in self.pairs(far_step - 1)])
-                beats.do((far, "held"), choose(gets), *[env[i] for i in inputs])
-                beats.do((far, "held"), choose(outer), env[far, "held"], env[name, "held"])
-            else:
-                add = choose_or_add(outer)
-                beats.do((far, "held"), add, env[name, "held"], *[env[i] for i in inputs])
+            if (far, far_step) not in joint:
+                fn, inputs = update(name, step)
+                if step:
+                    beats.do((name, "held"), fn, *[env[i] for i in inputs])
+                inputs = update(far, far_step)[1]
+                outer = self.on(step, self.count - 1 - step)
+                if far_step > mid:
+                    gets = self.on(*[pair[1] for pair in self.pairs(far_step - 1)])
+                    beats.do((far, "held"), choose(gets), *[env[i] for i in inputs])
+                    beats.do((far, "held"), choose(outer), env[far, "held"], env[name, "held"])
+                else:
+                    add = choose_or_add(outer)
+                    beats.do((far, "held"), add, env[name, "held"], *[env[i] for i in inputs])
             self.send(
                 beats,
                 self.pairs(step) + self.pairs(far_step),
@@ -734,6 +740,30 @@
                 [(name, step), (far, far_step)],
             )
         self.going = moving
+
+    def add_jointly(self, beats, moving, outward):
+        env, mid = beats.env, self.mid
+        for far, far_step in moving:
+            shape = env[far].shape
+            mine = [m for m, step in moving if step == mid - 1 and step and env[m].shape == shape]
+            inner = [m for m, out in outward.items() if out == (far, far_step)]
+            if far_step != mid or not mine or len(shape) != 2 or (inner and inner[0][1]):
+                continue
+            keys = [(mine[0], "held"), (far, "held")]
+            arrays = [env[mine[0], "held"], env[mine[0], mid - 2], env[far, "held"], env[far, mid - 1]]
+            outs, flag = [(shape[1], BF)] * 2, None
+            if inner:
+                arrays.append(env[inner[0][0], "held"])
+                flag = self.on(0, self.count - 1)
+
+            def add(*v):
+                a, b, c, d = v[-5:-1] if inner else v
+                both = plain_add(a, b) + plain_add(c, d)
+                return both[:1] + [jnp.where(v[0], v[-1], both[1])] if inner else both
+
+            beats.do(keys, lambda *v: rowwise(add, shape[0], outs, *v, flag=flag), *arrays)
+            return [(mine[0], mid - 1), (far, far_step)]
+        return []
 
     def send(self, beats, pairs, source, gets):
         value = lax.ppermute(tie(beats.env[source], beats.token), "dp", pairs)
@@ -831,23 +861,23 @@
     in_bias_mine = lax.dynamic_slice_in_dim(in_bias, row * units, units, 0)
     compute(3, [n.active, n.slope], pre_call, n.mx, n.my, n.wx, n.wy0, n.wy1, in_bias_mine)
 
-    def grads(beat, names, cuts, *inputs):
-        compute(beat, names, lambda *a: weight_grad(cuts, *a), *inputs)
+    def grads(beat, names, cuts, *inputs, **keys):
+        compute(beat, names, lambda *a: weight_grad(cuts, *a, **keys), *inputs)
 
     two = [units // 2] * 2
     half_units = [units // 2]
-    grads(3, [n.out_own0], half_units, n.active, n.g)
+    grads(3, [n.out_own0], half_units, n.active, n.g, vmem=58)
     z = 4
     for i in range(2):
         send(z + i, (n.oy, i), swap_row, (n.oy_sent, i))
     oy = [(n.oy, 0), (n.oy, 1)]
-    compute(z, [n.out_own1], lambda a, g: weight_grad(half_units, (a, units // 2), g), n.active, n.g)
+    compute(z, [n.out_own1], lambda a, g: weight_grad(half_units, (a, units // 2), g, vmem=58), n.active, n.g)
     share(z, n.h, gather_col, n.cot_x)
     compute(z, n.x_near, below, n.res, n.res_y)
     compute(z, n.y_near, below, n.res_x, n.res_xy)
     compute(z, n.x_far, below, n.res_c, n.res_yc)
     compute(z, n.y_far, below, n.res_xc, n.res_xyc)
-    grads(z + 1, [n.out_oth0, n.out_oth1], two, n.active, n.h)
+    grads(z + 1, [n.out_oth0, n.out_oth1], two, n.active, n.h, vmem=58)
     compute(z + 2, [n.pre_grad, n.in_bias_sum], pre_grad_call, n.g, n.h, n.ox, *oy, n.slope)
     two = [feats // 2] * 2
     grads(z + 3, [n.in_own0, n.in_own1], two, n.mx, n.pre_grad)
@@ -919,36 +949,55 @@
 
     part_rows = rows // 2
 
-    def near(a, b, *c):
-        def fn(a, b, c0, c1):
-            c = jnp.where(pl.program_id(0) == 0, c0, c1)
-            out = a.astype(F32) + b.astype(F32) + c.astype(F32)
-            return [out[:, feats:].astype(BF), out[:, :feats]]
-
-        return rowwise(fn, rows, [(feats, BF), (feats, F32)], a, b, *[(v, None) for v in c])
+    def near_sum(a, b, c):
+        out = a.astype(F32) + b.astype(F32) + c.astype(F32)
+        return [out[:, feats:].astype(BF), out[:, :feats]]
+
+    outs = [(feats, BF), (feats, F32)]
+
+    def near_part(i, join=False):
+        at = i * part_rows
+
+        def fn(a, b, c, *before):
+            keys = dict(whole=rows, skip=at, before=before) if join else {}
+            return rowwise(near_sum, part_rows, outs, (a, at), (b, at), c, vmem=58, **keys)
+
+        return fn
 
     def far_sum(i):
         at, outs = rows + i * part_rows, [(width, BF)]
-        return lambda a, b: rowwise(plain_add, part_rows, outs, (a, at), (b, at))[0]
-
-    def scatter(beat, name):
+        return lambda a, b: rowwise(plain_add, part_rows, outs, (a, at), (b, at), vmem=58)[0]
+
+    def scatter(beat, name, last=False):
         far, mine, got = [(name, i) for i in (n.far, n.near, n.core)]
-        send(beat, got, swap_core, far)
+        send(beat, got, swap_core, far, 0)
         got_y = [(name, n.near, i) for i in range(2)]
         for i in range(2):
             far_y = (name, n.far, i)
-            compute(beat + 1, far_y, far_sum(i), mine, got, top=i == 0)
+            compute(beat + i, far_y, far_sum(i), mine, got)
             send(beat + 1 + i, got_y[i], swap_y, far_y)
-        compute(beat + 3, [(name, n.sent), (name, n.keep)], near, mine, got, *got_y, top=True)
+        if last:
+            for i in range(2):
+                sent = (name, n.sent, i)
+                compute(beat + 3, [sent, (name, n.keep, i)], near_part(i), mine, got, got_y[i], top=True)
+                send(beat + 3, (name, n.got, i), swap_row, sent)
+            return
+        half_sent, half_keep = [(name, part, 0) for part in (n.sent, n.keep)]
+        compute(beat + 2, [half_sent, half_keep], near_part(0, True), mine, got, got_y[0])
+        last_part = [near_part(1, True), mine, got, got_y[1], half_sent, half_keep]
+        compute(beat + 3, [(name, n.sent), (name, n.keep)], *last_part, top=True)
         send(beat + 3, (name, n.got), swap_row, (name, n.sent))
 
     scatter(z + 8, n.ng)
-    scatter(z + 10, n.mixed)
+    scatter(z + 10, n.mixed, last=True)
     compute(
         z + 14,
         n.block_out,
-        lambda a, xg, res, b, c: (res.astype(F32) + a + xg.astype(F32) + b + c).astype(BF),
-        *[(n.mixed, n.keep), (n.mixed, n.got), n.res, dense_bias, out_bias],
+        lambda a0, a1, x0, x1, res, b, c: (
+            res.astype(F32) + below(a0, a1) + below(x0, x1).astype(F32) + b + c
+        ).astype(BF),
+        *[(n.mixed, part, i) for part in (n.keep, n.got) for i in range(2)],
+        *[n.res, dense_bias, out_bias],
     )
 
     def own_norm(res, res_x):
@@ -964,7 +1013,7 @@
         return jnp.stack([jnp.sum(grad, 1), jnp.sum(grad * normed, 1)])
 
     compute(z + 12, n.tok, token_sums, (n.ng, n.keep), (n.ng, n.got), n.res, n.res_x)
-    send(z + 12, n.tok_x, swap_row, n.tok)
+    send(z + 12, n.tok_x, swap_row, n.tok, 0)
 
     def finish_input(keep, xg, res, res_x, cot, tok, tok_x):
         normed, scale = own_norm(res, res_x)
@@ -974,7 +1023,7 @@
 
     rest = [n.res, n.res_x, n.cot, n.tok, n.tok_x]
     compute(
-        z + 13, n.input_grad, finish_input, (n.ng, n.keep), (n.ng, n.got), *rest
+        z + 12, n.input_grad, finish_input, (n.ng, n.keep), (n.ng, n.got), *rest
     )
 
     def small_all(near, far, cot, qkv_bias_sum, in_bias_sum):
@@ -1014,9 +1063,12 @@
     att = done(n.att_own0, n.att_own1, n.att_oth0_x, n.att_oth1_x)
     finish(z + 13, n.qkv_weight_grad, finish_qkv, *att)
     finish(z + 13, n.dense_weight_grad, finish_dense, att[1], att[3])
-    finish(
-        z + 14, n.in_weight_grad, finish_in, *done(n.in_own0, n.in_own1, n.in_oth0_x, n.in_oth1_x)
-    )
+    finish(z + 11, n.in_grad0, finish_in, *done(n.in_own0, n.in_oth0_x))
+
+    def second(meta, arrays):
+        return finish_in(meta, arrays[:2], arrays[2][0])
+
+    finish(z + 14, n.in_weight_grad, second, *done(n.in_own1, n.in_oth1_x), n.in_grad0)
     plan.run()
     def in_order(mine, got):
         return jnp.where(row == 0, jnp.concatenate([mine, got]), jnp.concatenate([got, mine]))

time: 582 us -> 549 us (0.943); the launches traced: 578 us -> 538 us
  other arithmetic: 79.9 us -> 28.7 us
  Pallas kernels: 196 us -> 245 us
  waiting for transfers between devices: 109 us -> 91.4 us
  local copies, waits for them, and re-layouts: 73.3 us -> 58.5 us
    pallas_call x8 -> x21, Pallas kernels: 15.3 us -> 53.3 us  [rowwise(): pl.pallas_call(kernel, grid_spec=pltpu.PrefetchScalarGridSpec(num_scalar_...]
    convert_element_type x14 -> x2, other arithmetic: 31 us -> 4.26 us  [add_low(): return (a.astype(F32) + b.astype(F32)).astype(a.dtype)]
    select_n x10 -> x0, other arithmetic: 24.3 us -> none  [choose_or_add(): return lambda value, a, b: jnp.where(flag, value, add_low(a, b))]
    unnamed x266 -> x224, local copies, waits for them, and re-layouts: 47.2 us -> 33.5 us
    ppermute x29, waiting for transfers between devices: 44.7 us -> 36.1 us  [send(): value = lax.ppermute(tie(beats.env[source], beats.token), 'dp', pairs)]
    ppermute x29, starting transfers between devices: 68.4 us -> 60.4 us  [send(): value = lax.ppermute(tie(beats.env[source], beats.token), 'dp', pairs)]
    ppermute x20 -> x21, waiting for transfers between devices: 45.8 us -> 38.2 us  [swap_row(): return lax.ppermute(value, 'row', [(0, 1), (1, 0)])]
    pallas_call x4 -> x5, Pallas kernels: 24.6 us -> 30.2 us  [assemble(): pl.pallas_call(kernel, grid_spec=pltpu.PrefetchScalarGridSpec(num_scalar_...]
  transfers between devices with their start and end apart: 65 -> 66, of which waited for: 26 -> 26; matrix products, arithmetic and copies ran while one was open for 11% -> 10% of each run, Pallas kernels for 31% -> 40%
where the time goes in v2:
time: 549 us; the launch traced here: 538 us
  Pallas kernels  245 us (45%)
  starting transfers between devices  96.8 us (18%)
  waiting for transfers between devices  91.4 us (17%)
  local copies, waits for them, and re-layouts  58.5 us (11%)
  other arithmetic  28.7 us (5%)
  between operations  15.6 us (3%)
    pallas_call x7, Pallas kernels, call(): pl.pallas_call(kernel if col is None else lambda _, *refs: kernel(*refs),...  81.1 us
    ppermute x29, starting transfers between devices, send(): value = lax.ppermute(tie(beats.env[source], beats.token), 'dp', pairs)  60.4 us
    pallas_call x21, Pallas kernels, rowwise(): pl.pallas_call(kernel, grid_spec=pltpu.PrefetchScalarGridSpec(num_scalar_...  53.3 us
    pallas_call x7, Pallas kernels, weight_grad(): pl.pallas_call(kernel, grid=(first[-1],), out_shape=tuple((jax.ShapeDtype...  46.6 us
    ppermute x21, waiting for transfers between devices, swap_row(): return lax.ppermute(value, 'row', [(0, 1), (1, 0)])  38.2 us
    ppermute x29, waiting for transfers between devices, send(): value = lax.ppermute(tie(beats.env[source], beats.token), 'dp', pairs)  36.1 us
    unnamed x224, local copies, waits for them, and re-layouts  33.5 us
    pallas_call x5, Pallas kernels, assemble(): pl.pallas_call(kernel, grid_spec=pltpu.PrefetchScalarGridSpec(num_scalar_...  30.2 us
  transfers between devices with their start and end apart: 66, of which 26 were waited for; matrix products, arithmetic and copies ran while one was open for 10% of the time, Pallas kernels for 40%

profile of v2, /device:TPU:0, one launch (start us, length us, event | category | flops | bytes accessed | tf_op | source)
XLA Modules:
  0.0 538.2 jit_solution(6842810584383297758)
XLA Ops:
  28.3 7.8 %collective-permute-done.gy.refs_3_ = f32[4,1024]{1,0:T(4,128)S(1)} collective-permute-done((f32[4,1024]{1,0:T(4,128)S(1)}, f32[4,1024]{1,0:T(4,128)S(1)}, u32[]{:S(2)}, u32[]{:S(2)}) %collective-permute-start) | collective-permute-done | bytes 16416 | tf_op jit(solution)/shard_map/ppermute | solution.py:29
  50.0 12.1 %collective-permute-done.5.y = bf16[512,1024]{1,0:T(8,128)(2,1)} collective-permute-done((bf16[512,1024]{1,0:T(8,128)(2,1)}, bf16[512,1024]{1,0:T(8,128)(2,1)}, u32[]{:S(2)}, u32[]{:S(2)}) %collective-permute-start.5) | collective-permute-done | bytes 1048608 | tf_op jit(solution)/shard_map/ppermute | solution.py:33
  82.0 6.6 %collective-permute-done.9.wy1_ref.refs_10_ = bf16[512,1024]{1,0:T(8,128)(2,1)} collective-permute-done((bf16[512,1024]{1,0:T(8,128)(2,1)}, bf16[512,1024]{1,0:T(8,128)(2,1)}, u32[]{:S(2)}, u32[]{:S(2)}) %collective-permute-start.9) | collective-permute-done | bytes 1048608 | tf_op jit(solution)/shard_map/ppermute | solution.py:29
  90.8 16.3 %pre_act.1 = (bf16[2048,1024]{1,0:T(8,128)(2,1)}, bf16[2048,1024]{1,0:T(8,128)(2,1)}) custom-call(bf16[2048,1024]{1,0:T(8,128)(2,1)} %get-tuple-element.537.x_ref.refs_0_, bf16[2048,1024]{1,0:T(8,128)(2,1)} %get-tuple-element.541.y_ref.refs_0_, bf16[1024,1024]{1,0:T(8,128)(2,1)} %constant_dynamic-slice_fusion.4.wx_ref.refs_8_, ...), custom_call_target="tpu_custom_call" | custom-call | tf_op jit(solution)/shard_map/pre_act/pallas_call | solution.py:93
  107.1 6.0 %weight_grad.7 = bf16[512,1024]{1,0:T(8,128)(2,1)} custom-call(bf16[2048,1024]{1,0:T(8,128)(2,1)} %get-tuple-element.500.refs_0_.refs_1_, bf16[2048,1024]{1,0:T(8,128)(2,1)} %all-gather.3.cloned.1.call-done.refs_1_.gx_ref.refs_3_), custom_call_target="tpu_custom_call" | custom-call | tf_op jit(solution)/shard_map/weight_grad/pallas_call | solution.py:265
  120.1 6.6 %weight_grad.8.refs_1_ = bf16[512,1024]{1,0:T(8,128)(2,1)} custom-call(bf16[2048,1024]{1,0:T(8,128)(2,1)} %get-tuple-element.500.refs_0_.refs_1_, bf16[2048,1024]{1,0:T(8,128)(2,1)} %all-gather.3.cloned.1.call-done.refs_1_.gx_ref.refs_3_), custom_call_target="tpu_custom_call" | custom-call | tf_op jit(solution)/shard_map/weight_grad/pallas_call | solution.py:265
  145.0 7.3 %collective-permute-start.14 = (bf16[512,1024]{1,0:T(8,128)(2,1)}, bf16[512,1024]{1,0:T(8,128)(2,1)}, u32[]{:S(2)}, u32[]{:S(2)}) collective-permute-start(bf16[512,1024]{1,0:T(8,128)(2,1)} %weight_grad.8.refs_1_), channel_id=1, source_target_pairs={{0,8},{24,16},{1,9},{25,17},{2,10},{26,18},{3,11},{27,19},{4,12},{... | collective-permute-start | bytes 3145736 | tf_op jit(solution)/shard_map/ppermute | solution.py:769
  152.3 9.1 %weight_grad.9 = (bf16[512,1024]{1,0:T(8,128)(2,1)}, bf16[512,1024]{1,0:T(8,128)(2,1)}) custom-call(bf16[2048,1024]{1,0:T(8,128)(2,1)} %get-tuple-element.500.refs_0_.refs_1_, bf16[2048,1024]{1,0:T(8,128)(2,1)} %all-gather.5.cloned.1.call-done.refs_1_.gy_ref.refs_3_), custom_call_target="tpu_custom_call" | custom-call | tf_op jit(solution)/shard_map/weight_grad/pallas_call | solution.py:265
  161.4 5.9 %collective-permute-done.15.wy1_ref.refs_6_ = bf16[512,1024]{1,0:T(8,128)(2,1)} collective-permute-done((bf16[512,1024]{1,0:T(8,128)(2,1)}, bf16[512,1024]{1,0:T(8,128)(2,1)}, u32[]{:S(2)}, u32[]{:S(2)}) %collective-permute-start.15) | collective-permute-done | bytes 1048608 | tf_op jit(solution)/shard_map/ppermute | solution.py:29
  185.1 11.3 %pre_grad.1 = (bf16[2048,1024]{1,0:T(8,128)(2,1)S(1)}, f32[1,1024]{1,0:T(1,128)S(1)}) custom-call(bf16[2048,1024]{1,0:T(8,128)(2,1)S(1)} %copy-done.10, bf16[2048,1024]{1,0:T(8,128)(2,1)S(1)} %copy-done.14, bf16[1024,1024]{1,0:T(8,128)(2,1)S(1)} %copy-done.16, bf16[512,1024]{1,0:T(8,128)(2,1)S(1)} %copy-done.22, ...), custom_call_target="tpu_custom_call" | custom-call | tf_op jit(solution)/shard_map/pre_grad/pallas_call | solution.py:93
  208.0 5.9 %weight_grad.10 = (bf16[512,1024]{1,0:T(8,128)(2,1)S(1)}, bf16[512,1024]{1,0:T(8,128)(2,1)S(1)}) custom-call(bf16[2048,1024]{1,0:T(8,128)(2,1)S(1)} %copy-done.8, bf16[2048,1024]{1,0:T(8,128)(2,1)S(1)} %get-tuple-element.538.refs_1_.refs_5_), custom_call_target="tpu_custom_call" | custom-call | tf_op jit(solution)/shard_map/weight_grad/pallas_call | solution.py:265
  214.0 6.7 %weight_grad.11 = (bf16[512,1024]{1,0:T(8,128)(2,1)S(1)}, bf16[512,1024]{1,0:T(8,128)(2,1)}) custom-call(bf16[2048,1024]{1,0:T(8,128)(2,1)S(1)} %copy-done.9, bf16[2048,1024]{1,0:T(8,128)(2,1)S(1)} %get-tuple-element.538.refs_1_.refs_5_), custom_call_target="tpu_custom_call" | custom-call | tf_op jit(solution)/shard_map/weight_grad/pallas_call | solution.py:265
  220.8 6.1 %collective-permute-done.22.refs_3_ = bf16[256,1024]{1,0:T(8,128)(2,1)S(1)} collective-permute-done((bf16[256,1024]{1,0:T(8,128)(2,1)S(1)}, bf16[256,1024]{1,0:T(8,128)(2,1)S(1)}, u32[]{:S(2)}, u32[]{:S(2)}) %collective-permute-start.22) | collective-permute-done | bytes 524320 | tf_op jit(solution)/shard_map/ppermute | solution.py:29
  232.2 7.6 %packed.1 = (bf16[2048,256]{1,0:T(8,128)(2,1)S(1)}, bf16[2048,256]{1,0:T(8,128)(2,1)S(1)}, bf16[2048,256]{1,0:T(8,128)(2,1)S(1)}) custom-call(bf16[2048,1024]{1,0:T(8,128)(2,1)S(1)} %copy-done.4, bf16[2048,1024]{1,0:T(8,128)(2,1)S(1)} %copy-done.6, bf16[1024,768]{1,0:T(8,128)(2,1)S(1)} %dynamic-slice_bitcast_fusion.wx_ref.refs_6_, ...), custom_call_target="tpu_custom_call" | custom-call | tf_op jit(solution)/shard_map/packed/pallas_call | solution.py:93
  256.3 15.2 %attention.1 = (bf16[4,512,256]{2,1,0:T(8,128)(2,1)S(1)}, bf16[4,512,768]{2,1,0:T(8,128)(2,1)}, f32[1,768]{1,0:T(1,128)S(1)}) custom-call(bf16[4,512,256]{2,1,0:T(8,128)(2,1)S(1)} %bitcast.62, bf16[4,512,256]{2,1,0:T(8,128)(2,1)S(1)} %bitcast.63, bf16[4,512,256]{2,1,0:T(8,128)(2,1)S(1)} %bitcast.64, bf16[4,512,256]{2,1,0:T(8,128)(2,1)S(1)} %bitcast.65, ...), custom_call_target="tpu_custom_call" | custom-call | tf_op jit(solution)/shard_map/attention/pallas_call | solution.py:392
  294.1 6.7 %weight_grad.13 = (bf16[512,1024]{1,0:T(8,128)(2,1)}, bf16[512,1024]{1,0:T(8,128)(2,1)}) custom-call(bf16[2048,768]{1,0:T(8,128)(2,1)S(1)} %bitcast.54, bf16[2048,1024]{1,0:T(8,128)(2,1)S(1)} %copy-done.7, bf16[2048,256]{1,0:T(8,128)(2,1)S(1)} %bitcast.56, bf16[2048,1024]{1,0:T(8,128)(2,1)S(1)} %copy-done.15), custom_call_target="tpu_custom_call" | custom-call | tf_op jit(solution)/shard_map/weight_grad/pallas_call | solution.py:265
  311.8 15.3 %norm_grad.2 = (bf16[1024,2048]{1,0:T(8,128)(2,1)}, f32[4,2048]{1,0:T(4,128)}) custom-call(s32[1]{0:T(128)} %bitcast.4._, bf16[1024,1024]{1,0:T(8,128)(2,1)} %copy-done.85, bf16[1024,1024]{1,0:T(8,128)(2,1)} %pad_maximum_fusion.refs_1_, f32[4,1024]{1,0:T(4,128)} %copy-done.98, f32[4,1024]{1,0:T(4,128)} %copy-done.100, bf16[2048,768]{1,0:T(8,128)(2,1)} %bitcast.51, ...), custom_call_target="tpu_custom_call" | custom-call | tf_op jit(solution)/shard_map/norm_grad/pallas_call | solution.py:93
  335.8 15.8 %norm_grad.3 = (bf16[1024,2048]{1,0:T(8,128)(2,1)}, f32[4,2048]{1,0:T(4,128)}) custom-call(s32[1]{0:T(128)} %bitcast.4._, bf16[1024,1024]{1,0:T(8,128)(2,1)} %copy-done.86, bf16[1024,1024]{1,0:T(8,128)(2,1)} %copy-done.87, f32[4,1024]{1,0:T(4,128)} %copy-done.98, f32[4,1024]{1,0:T(4,128)} %copy-done.100, bf16[2048,768]{1,0:T(8,128)(2,1)} %bitcast.52, ...), custom_call_target="tpu_custom_call" | custom-call | tf_op jit(solution)/shard_map/norm_grad/pallas_call | solution.py:93
  375.5 7.4 %mixed.2 = bf16[1024,2048]{1,0:T(8,128)(2,1)S(1)} custom-call(s32[1]{0:T(128)} %bitcast.4._, bf16[2048,256]{1,0:T(8,128)(2,1)S(1)} %bitcast.57, bf16[2048,1024]{1,0:T(8,128)(2,1)S(1)} %copy-done.2, bf16[256,1024]{1,0:T(8,128)(2,1)S(1)} %copy-done.28, bf16[256,1024]{1,0:T(8,128)(2,1)S(1)} %copy-done.59, bf16[1024,1024]{1,0:T(8,128)(2,1)S(1)} %copy-done.17, ...), custom_call_target="tpu_custom_call" | custom-call | tf_op jit(solution)/shard_map/mixed/pallas_call | solution.py:93
  402.4 7.5 %mixed.3.refs_0_ = bf16[1024,2048]{1,0:T(8,128)(2,1)S(1)} custom-call(s32[1]{0:T(128)} %bitcast.4._, bf16[2048,256]{1,0:T(8,128)(2,1)S(1)} %bitcast.58, bf16[2048,1024]{1,0:T(8,128)(2,1)S(1)} %copy-done.2, bf16[256,1024]{1,0:T(8,128)(2,1)S(1)} %copy-done.28, bf16[256,1024]{1,0:T(8,128)(2,1)S(1)} %copy-done.60, bf16[1024,1024]{1,0:T(8,128)(2,1)S(1)} %copy-done.18, ...), custom_call_target="tpu_custom_call" | custom-call | tf_op jit(solution)/shard_map/mixed/pallas_call | solution.py:93
  417.8 6.8 %collective-permute-done.47.refs_2_.refs_0_ = bf16[512,1024]{1,0:T(8,128)(2,1)} collective-permute-done((bf16[512,1024]{1,0:T(8,128)(2,1)}, bf16[512,1024]{1,0:T(8,128)(2,1)}, u32[]{:S(2)}, u32[]{:S(2)}) %collective-permute-start.47) | collective-permute-done | bytes 1048608 | tf_op jit(solution)/shard_map/ppermute | solution.py:769
  449.8 10.6 %collective-permute-done.50 = f32[12032]{0:T(1024)S(1)} collective-permute-done((f32[12032]{0:T(1024)S(1)}, f32[12032]{0:T(1024)S(1)}, u32[]{:S(2)}, u32[]{:S(2)}) %collective-permute-start.50) | collective-permute-done | bytes 48160 | tf_op jit(solution)/shard_map/ppermute | solution.py:769
  477.7 9.4 %out_grad.1 = f32[2048,1024]{1,0:T(8,128)} custom-call(s32[2]{0:T(128)} %pad_add_fusion.1.meta_ref, bf16[512,1024]{1,0:T(8,128)(2,1)} %copy-done.31, bf16[512,1024]{1,0:T(8,128)(2,1)} %copy-done.61, bf16[512,1024]{1,0:T(8,128)(2,1)} %copy-done.32, bf16[512,1024]{1,0:T(8,128)(2,1)} %copy-done.62, bf16[512,1024]{1,0:T(8,128)(2,1)} %collective-permute-done.31.refs_4_, ...), custom_call_target="tpu_custom_call" | custom-call | tf_op jit(solution)/shard_map/out_grad/pallas_call | solution.py:493
  507.2 7.7 %qkv_grad.1 = f32[1024,2,768]{2,1,0:T(2,128)} custom-call(s32[2]{0:T(128)} %pad_add_fusion.2.meta_ref, bf16[512,1024]{1,0:T(8,128)(2,1)} %collective-permute-done.41.refs_2_.refs_0_, bf16[512,1024]{1,0:T(8,128)(2,1)} %get-tuple-element.798.refs_1_, bf16[512,1024]{1,0:T(8,128)(2,1)} %collective-permute-done.47.refs_2_.refs_0_, ...), custom_call_target="tpu_custom_call" | custom-call | tf_op jit(solution)/shard_map/qkv_grad/pallas_call | solution.py:493
  (448 shorter events, 304.9 us)
Async XLA Ops:
  7.2 99.9 %all-gather.3.cloned.1.call-start = ((), (), s32[]{:S(2)}) async-start(), calls=%async_computation | async-start | bytes 5242880 | tf_op jit(solution)/shard_map/all_gather | solution.py:844
  7.2 28.9 %collective-permute-start.3 = (bf16[512,1024]{1,0:T(8,128)(2,1)}, bf16[512,1024]{1,0:T(8,128)(2,1)S(1)}, u32[]{:S(2)}, u32[]{:S(2)}) collective-permute-start(bf16[512,1024]{1,0:T(8,128)(2,1)} %x.2), channel_id=1, source_target_pairs={{0,1},{1,0},{2,3},{3,2},{4,5},{5,4},{6,7},{7,6},{8,9},{9,8},{10,11... | collective-permute-start | bytes 3145736 | tf_op jit(solution)/shard_map/ppermute | solution.py:33
  7.8 28.4 %collective-permute-start.2 = (bf16[512,1024]{1,0:T(8,128)(2,1)}, bf16[512,1024]{1,0:T(8,128)(2,1)}, u32[]{:S(2)}, u32[]{:S(2)}) collective-permute-start(bf16[512,1024]{1,0:T(8,128)(2,1)} %x.2), channel_id=1, source_target_pairs={{0,2},{1,3},{2,0},{3,1},{4,6},{5,7},{6,4},{7,5},{8,10},{9,11},{10,... | collective-permute-start | bytes 3145736 | tf_op jit(solution)/shard_map/ppermute | solution.py:33
  10.4 25.8 %collective-permute-start.1 = (bf16[512,1024]{1,0:T(8,128)(2,1)}, bf16[512,1024]{1,0:T(8,128)(2,1)}, u32[]{:S(2)}, u32[]{:S(2)}) collective-permute-start(bf16[512,1024]{1,0:T(8,128)(2,1)} %x.2), channel_id=1, source_target_pairs={{0,4},{4,0},{1,5},{5,1},{2,6},{6,2},{3,7},{7,3},{8,12},{12,8},{9,1... | collective-permute-start | bytes 3145736 | tf_op jit(solution)/shard_map/ppermute | solution.py:29
  36.3 25.9 %collective-permute-start.5 = (bf16[512,1024]{1,0:T(8,128)(2,1)}, bf16[512,1024]{1,0:T(8,128)(2,1)}, u32[]{:S(2)}, u32[]{:S(2)}) collective-permute-start(bf16[512,1024]{1,0:T(8,128)(2,1)} %collective-permute-done.1.y), channel_id=1, source_target_pairs={{0,2},{1,3},{2,0},{3,1},{4,6},{5,7},{6,4},{7,5},{8,10},{9,11},{10,... | collective-permute-start | bytes 3145736 | tf_op jit(solution)/shard_map/ppermute | solution.py:33
  36.6 25.5 %collective-permute-start.7 = (bf16[512,1024]{1,0:T(8,128)(2,1)}, bf16[512,1024]{1,0:T(8,128)(2,1)}, u32[]{:S(2)}, u32[]{:S(2)}) collective-permute-start(bf16[512,1024]{1,0:T(8,128)(2,1)} %collective-permute-done.2.x), channel_id=1, source_target_pairs={{0,1},{1,0},{2,3},{3,2},{4,5},{5,4},{6,7},{7,6},{8,9},{9,8},{10,11... | collective-permute-start | bytes 3145736 | tf_op jit(solution)/shard_map/ppermute | solution.py:33
  36.8 25.7 %collective-permute-start.4 = (bf16[512,1024]{1,0:T(8,128)(2,1)}, bf16[512,1024]{1,0:T(8,128)(2,1)}, u32[]{:S(2)}, u32[]{:S(2)}) collective-permute-start(bf16[512,1024]{1,0:T(8,128)(2,1)} %constant_dynamic-slice_fusion.5), channel_id=1, source_target_pairs={{0,4},{4,0},{1,5},{5,1},{2,6},{6,2},{3,7},{7,3},{8,12},{12,8},{9,1... | collective-permute-start | bytes 3145736 | tf_op jit(solution)/shard_map/ppermute | solution.py:29
  62.5 89.7 %all-gather.5.cloned.1.call-start = ((), (), s32[]{:S(2)}) async-start(), calls=%async_computation.1 | async-start | bytes 5242880 | tf_op jit(solution)/shard_map/all_gather | solution.py:844
  62.6 25.9 %collective-permute-start.9 = (bf16[512,1024]{1,0:T(8,128)(2,1)}, bf16[512,1024]{1,0:T(8,128)(2,1)}, u32[]{:S(2)}, u32[]{:S(2)}) collective-permute-start(bf16[512,1024]{1,0:T(8,128)(2,1)} %constant_dynamic-slice_fusion.6), channel_id=1, source_target_pairs={{0,4},{4,0},{1,5},{5,1},{2,6},{6,2},{3,7},{7,3},{8,12},{12,8},{9,1... | collective-permute-start | bytes 3145736 | tf_op jit(solution)/shard_map/ppermute | solution.py:29
  88.5 24.8 %collective-permute-start.10 = (bf16[512,1024]{1,0:T(8,128)(2,1)S(1)}, bf16[512,1024]{1,0:T(8,128)(2,1)}, u32[]{:S(2)}, u32[]{:S(2)}) collective-permute-start(bf16[512,1024]{1,0:T(8,128)(2,1)S(1)} %copy-done.82), channel_id=1, source_target_pairs={{0,4},{4,0},{1,5},{5,1},{2,6},{6,2},{3,7},{7,3},{8,12},{12,8},{9,1... | collective-permute-start | bytes 3145736 | tf_op jit(solution)/shard_map/ppermute | solution.py:29
  115.2 24.8 %collective-permute-start.11 = (bf16[512,1024]{1,0:T(8,128)(2,1)}, bf16[512,1024]{1,0:T(8,128)(2,1)}, u32[]{:S(2)}, u32[]{:S(2)}) collective-permute-start(bf16[512,1024]{1,0:T(8,128)(2,1)} %weight_grad.7), channel_id=1, source_target_pairs={{0,8},{24,16},{1,9},{25,17},{2,10},{26,18},{3,11},{27,19},{4,12},{... | collective-permute-start | bytes 3145736 | tf_op jit(solution)/shard_map/ppermute | solution.py:769
  145.0 26.3 %collective-permute-start.14 = (bf16[512,1024]{1,0:T(8,128)(2,1)}, bf16[512,1024]{1,0:T(8,128)(2,1)}, u32[]{:S(2)}, u32[]{:S(2)}) collective-permute-start(bf16[512,1024]{1,0:T(8,128)(2,1)} %weight_grad.8.refs_1_), channel_id=1, source_target_pairs={{0,8},{24,16},{1,9},{25,17},{2,10},{26,18},{3,11},{27,19},{4,12},{... | collective-permute-start | bytes 3145736 | tf_op jit(solution)/shard_map/ppermute | solution.py:769
  175.1 24.6 %collective-permute-start.16 = (bf16[512,1024]{1,0:T(8,128)(2,1)S(1)}, bf16[512,1024]{1,0:T(8,128)(2,1)S(1)}, u32[]{:S(2)}, u32[]{:S(2)}) collective-permute-start(bf16[512,1024]{1,0:T(8,128)(2,1)S(1)} %get-tuple-element.532.refs_3_), channel_id=1, source_target_pairs={{8,16},{16,8},{9,17},{17,9},{10,18},{18,10},{11,19},{19,11},{12,20... | collective-permute-start | bytes 3145736 | tf_op jit(solution)/shard_map/ppermute | solution.py:769
  200.7 26.2 %collective-permute-start.19 = (bf16[512,1024]{1,0:T(8,128)(2,1)S(1)}, bf16[512,1024]{1,0:T(8,128)(2,1)S(1)}, u32[]{:S(2)}, u32[]{:S(2)}) collective-permute-start(bf16[512,1024]{1,0:T(8,128)(2,1)S(1)} %get-tuple-element.553.refs_3_), channel_id=1, source_target_pairs={{8,16},{16,8},{9,17},{17,9},{10,18},{18,10},{11,19},{19,11},{12,20... | collective-permute-start | bytes 3145736 | tf_op jit(solution)/shard_map/ppermute | solution.py:769
  201.5 25.4 %collective-permute-start.20 = (bf16[512,1024]{1,0:T(8,128)(2,1)S(1)}, bf16[512,1024]{1,0:T(8,128)(2,1)S(1)}, u32[]{:S(2)}, u32[]{:S(2)}) collective-permute-start(bf16[512,1024]{1,0:T(8,128)(2,1)S(1)} %get-tuple-element.767.refs_3_), channel_id=1, source_target_pairs={{0,8},{24,16},{8,0},{16,24},{1,9},{25,17},{9,1},{17,25},{2,10},{26... | collective-permute-start | bytes 3145736 | tf_op jit(solution)/shard_map/ppermute | solution.py:769
  332.5 25.0 %collective-permute-start.37 = (bf16[512,1024]{1,0:T(8,128)(2,1)}, bf16[512,1024]{1,0:T(8,128)(2,1)}, u32[]{:S(2)}, u32[]{:S(2)}) collective-permute-start(bf16[512,1024]{1,0:T(8,128)(2,1)} %get-tuple-element.737.refs_3_), channel_id=1, source_target_pairs={{0,8},{24,16},{8,0},{16,24},{1,9},{25,17},{9,1},{17,25},{2,10},{26... | collective-permute-start | bytes 3145736 | tf_op jit(solution)/shard_map/ppermute | solution.py:769
  364.3 25.8 %collective-permute-start.39 = (bf16[512,1024]{1,0:T(8,128)(2,1)}, bf16[512,1024]{1,0:T(8,128)(2,1)}, u32[]{:S(2)}, u32[]{:S(2)}) collective-permute-start(bf16[512,1024]{1,0:T(8,128)(2,1)} %get-tuple-element.692.refs_3_), channel_id=1, source_target_pairs={{8,16},{16,8},{9,17},{17,9},{10,18},{18,10},{11,19},{19,11},{12,20... | collective-permute-start | bytes 3145736 | tf_op jit(solution)/shard_map/ppermute | solution.py:769
  398.7 25.9 %collective-permute-start.47 = (bf16[512,1024]{1,0:T(8,128)(2,1)}, bf16[512,1024]{1,0:T(8,128)(2,1)}, u32[]{:S(2)}, u32[]{:S(2)}) collective-permute-start(bf16[512,1024]{1,0:T(8,128)(2,1)} %get-tuple-element.807.refs_3_.refs_1_), channel_id=1, source_target_pairs={{0,8},{24,16},{8,0},{16,24},{1,9},{25,17},{9,1},{17,25},{2,10},{26... | collective-permute-start | bytes 3145736 | tf_op jit(solution)/shard_map/ppermute | solution.py:769
  400.0 25.3 %collective-permute-start.48 = (bf16[256,2048]{1,0:T(8,128)(2,1)}, bf16[256,2048]{1,0:T(8,128)(2,1)}, u32[]{:S(2)}, u32[]{:S(2)}) collective-permute-start(bf16[256,2048]{1,0:T(8,128)(2,1)} %rowwise.32), channel_id=1, source_target_pairs={{0,2},{1,3},{2,0},{3,1},{4,6},{5,7},{6,4},{7,5},{8,10},{9,11},{10,... | collective-permute-start | bytes 3145736 | tf_op jit(solution)/shard_map/ppermute | solution.py:33
  432.1 28.3 %collective-permute-start.52 = (bf16[512,1024]{1,0:T(8,128)(2,1)}, bf16[512,1024]{1,0:T(8,128)(2,1)}, u32[]{:S(2)}, u32[]{:S(2)}) collective-permute-start(bf16[512,1024]{1,0:T(8,128)(2,1)} %get-tuple-element.741), channel_id=1, source_target_pairs={{0,4},{4,0},{1,5},{5,1},{2,6},{6,2},{3,7},{7,3},{8,12},{12,8},{9,1... | collective-permute-start | bytes 3145736 | tf_op jit(solution)/shard_map/ppermute | solution.py:29
  433.3 27.1 %collective-permute-start.49 = (bf16[512,1024]{1,0:T(8,128)(2,1)S(1)}, bf16[512,1024]{1,0:T(8,128)(2,1)}, u32[]{:S(2)}, u32[]{:S(2)}) collective-permute-start(bf16[512,1024]{1,0:T(8,128)(2,1)S(1)} %get-tuple-element.747.refs_2_), channel_id=1, source_target_pairs={{8,16},{16,8},{9,17},{17,9},{10,18},{18,10},{11,19},{19,11},{12,20... | collective-permute-start | bytes 3145736 | tf_op jit(solution)/shard_map/ppermute | solution.py:769
  435.0 25.4 %collective-permute-start.51 = (bf16[512,1024]{1,0:T(8,128)(2,1)S(1)}, bf16[512,1024]{1,0:T(8,128)(2,1)S(1)}, u32[]{:S(2)}, u32[]{:S(2)}) collective-permute-start(bf16[512,1024]{1,0:T(8,128)(2,1)S(1)} %get-tuple-element.802.refs_5_), channel_id=1, source_target_pairs={{0,8},{24,16},{8,0},{16,24},{1,9},{25,17},{9,1},{17,25},{2,10},{26... | collective-permute-start | bytes 3145736 | tf_op jit(solution)/shard_map/ppermute | solution.py:769
  464.8 25.0 %collective-permute-start.56 = (bf16[512,1024]{1,0:T(8,128)(2,1)S(1)}, bf16[512,1024]{1,0:T(8,128)(2,1)}, u32[]{:S(2)}, u32[]{:S(2)}) collective-permute-start(bf16[512,1024]{1,0:T(8,128)(2,1)S(1)} %get-tuple-element.804.refs_7_.refs_3_), channel_id=1, source_target_pairs={{8,0},{16,24},{9,1},{17,25},{10,2},{18,26},{11,3},{19,27},{12,4},{... | collective-permute-start | bytes 3145736 | tf_op jit(solution)/shard_map/ppermute | solution.py:769
  491.5 30.3 %collective-permute-start.61 = (bf16[512,1024]{1,0:T(8,128)(2,1)S(1)}, bf16[512,1024]{1,0:T(8,128)(2,1)S(1)}, u32[]{:S(2)}, u32[]{:S(2)}) collective-permute-start(bf16[512,1024]{1,0:T(8,128)(2,1)S(1)} %add_convert_fusion.refs_3_), channel_id=1, source_target_pairs={{8,0},{16,24},{9,1},{17,25},{10,2},{18,26},{11,3},{19,27},{12,4},{... | collective-permute-start | bytes 3145736 | tf_op jit(solution)/shard_map/ppermute | solution.py:769
  (151 other events, 1791.6 us)
Sparse Core Ops, SparseCore 0:
  62.6 35.9 all-gather.2
  113.5 35.9 all-gather.4

commit v3 on v2

--- a/solution.py
+++ b/solution.py
@@ -979,7 +979,7 @@
         if last:
             for i in range(2):
                 sent = (name, n.sent, i)
-                compute(beat + 3, [sent, (name, n.keep, i)], near_part(i), mine, got, got_y[i], top=True)
+                compute(beat + 2 + i, [sent, (name, n.keep, i)], near_part(i), mine, got, got_y[i], top=i == 1)
                 send(beat + 3, (name, n.got, i), swap_row, sent)
             return
         half_sent, half_keep = [(name, part, 0) for part in (n.sent, n.keep)]
@@ -989,7 +989,6 @@
         send(beat + 3, (name, n.got), swap_row, (name, n.sent))
 
     scatter(z + 8, n.ng)
-    scatter(z + 10, n.mixed, last=True)
     compute(
         z + 14,
         n.block_out,
@@ -1059,16 +1058,17 @@
     def done(*names):
         return [(v, n.parts) for v in names]
 
-    finish(z + 12, n.out_weight_grad, finish_out, *done(n.out_own0, n.out_own1), n.out_oth0_y, n.out_oth1_y)
+    finish(z + 11, n.out_weight_grad, finish_out, *done(n.out_own0, n.out_own1), n.out_oth0_y, n.out_oth1_y)
     att = done(n.att_own0, n.att_own1, n.att_oth0_x, n.att_oth1_x)
     finish(z + 13, n.qkv_weight_grad, finish_qkv, *att)
     finish(z + 13, n.dense_weight_grad, finish_dense, att[1], att[3])
-    finish(z + 11, n.in_grad0, finish_in, *done(n.in_own0, n.in_oth0_x))
+    finish(z + 12, n.in_grad0, finish_in, *done(n.in_own0, n.in_oth0_x))
 
     def second(meta, arrays):
         return finish_in(meta, arrays[:2], arrays[2][0])
 
     finish(z + 14, n.in_weight_grad, second, *done(n.in_own1, n.in_oth1_x), n.in_grad0)
+    scatter(z + 10, n.mixed, last=True)
     plan.run()
     def in_order(mine, got):
         return jnp.where(row == 0, jnp.concatenate([mine, got]), jnp.concatenate([got, mine]))

time: 549 us -> 545 us (level)
  transfers between devices with their start and end apart: 66 -> 66, of which waited for: 26 -> 26; matrix products, arithmetic and copies ran while one was open for 10% -> 10% of each run, Pallas kernels for 40% -> 41%
where the time goes in v3:
time: 545 us; the launch traced here: 535 us
  Pallas kernels  244 us (45%)
  starting transfers between devices  96.5 us (18%)
  waiting for transfers between devices  88.5 us (16%)
  local copies, waits for them, and re-layouts  58.5 us (11%)
  other arithmetic  28.7 us (5%)
  between operations  15.6 us (3%)
    pallas_call x7, Pallas kernels, call(): pl.pallas_call(kernel if col is None else lambda _, *refs: kernel(*refs),...  81.1 us
    ppermute x29, starting transfers between devices, send(): value = lax.ppermute(tie(beats.env[source], beats.token), 'dp', pairs)  60.3 us
    pallas_call x21, Pallas kernels, rowwise(): pl.pallas_call(kernel, grid_spec=pltpu.PrefetchScalarGridSpec(num_scalar_...  53.3 us
    pallas_call x7, Pallas kernels, weight_grad(): pl.pallas_call(kernel, grid=(first[-1],), out_shape=tuple((jax.ShapeDtype...  46.7 us
    ppermute x21, waiting for transfers between devices, swap_row(): return lax.ppermute(value, 'row', [(0, 1), (1, 0)])  38.3 us
    unnamed x224, local copies, waits for them, and re-layouts  33.5 us
    ppermute x29, waiting for transfers between devices, send(): value = lax.ppermute(tie(beats.env[source], beats.token), 'dp', pairs)  33 us
    pallas_call x5, Pallas kernels, assemble(): pl.pallas_call(kernel, grid_spec=pltpu.PrefetchScalarGridSpec(num_scalar_...  30 us
  transfers between devices with their start and end apart: 66, of which 26 were waited for; matrix products, arithmetic and copies ran while one was open for 10% of the time, Pallas kernels for 41%

profile of v3, /device:TPU:0, one launch (start us, length us, event | category | flops | bytes accessed | tf_op | source)
XLA Modules:
  0.0 535.0 jit_solution(9325965279328907141)
XLA Ops:
  20.3 5.8 %fusion.14 = (f32[2048,128]{1,0:T(8,128)}, f32[2048,128]{1,0:T(8,128)}, f32[2048,128]{1,0:T(8,128)}) fusion(f32[128]{0:T(128)S(1)} %fusion.30, f32[2048]{0:T(1024)S(1)} %fusion.22, pred[128]{0:T(512)(128)(4,1)S(1)} %get-tuple-element.852, pred[128]{0:T(512)(128)(4,1)S(1)} %get-tuple-element.853, pred[128]{0:T(512)(128)(4,1)S(1)} %iota_compare_fusion.3), kind=kLoop, calls=%fused_computation.31 | loop fusion | flops 1310720 | bytes 3154816 | tf_op jit(solution)/shard_map/jit(_where)/select_n | solution.py:62
  28.3 7.8 %collective-permute-done.gy.refs_3_ = f32[4,1024]{1,0:T(4,128)S(1)} collective-permute-done((f32[4,1024]{1,0:T(4,128)S(1)}, f32[4,1024]{1,0:T(4,128)S(1)}, u32[]{:S(2)}, u32[]{:S(2)}) %collective-permute-start) | collective-permute-done | bytes 16416 | tf_op jit(solution)/shard_map/ppermute | solution.py:29
  49.9 12.2 %collective-permute-done.5.y = bf16[512,1024]{1,0:T(8,128)(2,1)} collective-permute-done((bf16[512,1024]{1,0:T(8,128)(2,1)}, bf16[512,1024]{1,0:T(8,128)(2,1)}, u32[]{:S(2)}, u32[]{:S(2)}) %collective-permute-start.5) | collective-permute-done | bytes 1048608 | tf_op jit(solution)/shard_map/ppermute | solution.py:33
  82.0 6.5 %collective-permute-done.9.wy1_ref.refs_10_ = bf16[512,1024]{1,0:T(8,128)(2,1)} collective-permute-done((bf16[512,1024]{1,0:T(8,128)(2,1)}, bf16[512,1024]{1,0:T(8,128)(2,1)}, u32[]{:S(2)}, u32[]{:S(2)}) %collective-permute-start.9) | collective-permute-done | bytes 1048608 | tf_op jit(solution)/shard_map/ppermute | solution.py:29
  90.8 16.3 %pre_act.1 = (bf16[2048,1024]{1,0:T(8,128)(2,1)}, bf16[2048,1024]{1,0:T(8,128)(2,1)}) custom-call(bf16[2048,1024]{1,0:T(8,128)(2,1)} %get-tuple-element.538.x_ref.refs_0_, bf16[2048,1024]{1,0:T(8,128)(2,1)} %get-tuple-element.542.y_ref.refs_0_, bf16[1024,1024]{1,0:T(8,128)(2,1)} %constant_dynamic-slice_fusion.4.wx_ref.refs_8_, ...), custom_call_target="tpu_custom_call" | custom-call | tf_op jit(solution)/shard_map/pre_act/pallas_call | solution.py:93
  107.1 6.0 %weight_grad.7 = bf16[512,1024]{1,0:T(8,128)(2,1)} custom-call(bf16[2048,1024]{1,0:T(8,128)(2,1)} %get-tuple-element.501.refs_0_.refs_1_, bf16[2048,1024]{1,0:T(8,128)(2,1)} %all-gather.3.cloned.1.call-done.refs_1_.gx_ref.refs_3_), custom_call_target="tpu_custom_call" | custom-call | tf_op jit(solution)/shard_map/weight_grad/pallas_call | solution.py:265
  120.1 6.6 %weight_grad.8.refs_1_ = bf16[512,1024]{1,0:T(8,128)(2,1)} custom-call(bf16[2048,1024]{1,0:T(8,128)(2,1)} %get-tuple-element.501.refs_0_.refs_1_, bf16[2048,1024]{1,0:T(8,128)(2,1)} %all-gather.3.cloned.1.call-done.refs_1_.gx_ref.refs_3_), custom_call_target="tpu_custom_call" | custom-call | tf_op jit(solution)/shard_map/weight_grad/pallas_call | solution.py:265
  145.0 7.3 %collective-permute-start.14 = (bf16[512,1024]{1,0:T(8,128)(2,1)}, bf16[512,1024]{1,0:T(8,128)(2,1)}, u32[]{:S(2)}, u32[]{:S(2)}) collective-permute-start(bf16[512,1024]{1,0:T(8,128)(2,1)} %weight_grad.8.refs_1_), channel_id=1, source_target_pairs={{0,8},{24,16},{1,9},{25,17},{2,10},{26,18},{3,11},{27,19},{4,12},{... | collective-permute-start | bytes 3145736 | tf_op jit(solution)/shard_map/ppermute | solution.py:769
  152.3 9.1 %weight_grad.9 = (bf16[512,1024]{1,0:T(8,128)(2,1)}, bf16[512,1024]{1,0:T(8,128)(2,1)}) custom-call(bf16[2048,1024]{1,0:T(8,128)(2,1)} %get-tuple-element.501.refs_0_.refs_1_, bf16[2048,1024]{1,0:T(8,128)(2,1)} %all-gather.5.cloned.1.call-done.refs_1_.gy_ref.refs_3_), custom_call_target="tpu_custom_call" | custom-call | tf_op jit(solution)/shard_map/weight_grad/pallas_call | solution.py:265
  161.4 5.8 %collective-permute-done.15.wy1_ref.refs_6_ = bf16[512,1024]{1,0:T(8,128)(2,1)} collective-permute-done((bf16[512,1024]{1,0:T(8,128)(2,1)}, bf16[512,1024]{1,0:T(8,128)(2,1)}, u32[]{:S(2)}, u32[]{:S(2)}) %collective-permute-start.15) | collective-permute-done | bytes 1048608 | tf_op jit(solution)/shard_map/ppermute | solution.py:29
  185.2 11.3 %pre_grad.1 = (bf16[2048,1024]{1,0:T(8,128)(2,1)S(1)}, f32[1,1024]{1,0:T(1,128)S(1)}) custom-call(bf16[2048,1024]{1,0:T(8,128)(2,1)S(1)} %copy-done.10, bf16[2048,1024]{1,0:T(8,128)(2,1)S(1)} %copy-done.14, bf16[1024,1024]{1,0:T(8,128)(2,1)S(1)} %copy-done.16, bf16[512,1024]{1,0:T(8,128)(2,1)S(1)} %copy-done.22, ...), custom_call_target="tpu_custom_call" | custom-call | tf_op jit(solution)/shard_map/pre_grad/pallas_call | solution.py:93
  208.1 5.9 %weight_grad.10 = (bf16[512,1024]{1,0:T(8,128)(2,1)S(1)}, bf16[512,1024]{1,0:T(8,128)(2,1)S(1)}) custom-call(bf16[2048,1024]{1,0:T(8,128)(2,1)S(1)} %copy-done.8, bf16[2048,1024]{1,0:T(8,128)(2,1)S(1)} %get-tuple-element.539.refs_1_.refs_5_), custom_call_target="tpu_custom_call" | custom-call | tf_op jit(solution)/shard_map/weight_grad/pallas_call | solution.py:265
  214.1 6.7 %weight_grad.11 = (bf16[512,1024]{1,0:T(8,128)(2,1)S(1)}, bf16[512,1024]{1,0:T(8,128)(2,1)}) custom-call(bf16[2048,1024]{1,0:T(8,128)(2,1)S(1)} %copy-done.9, bf16[2048,1024]{1,0:T(8,128)(2,1)S(1)} %get-tuple-element.539.refs_1_.refs_5_), custom_call_target="tpu_custom_call" | custom-call | tf_op jit(solution)/shard_map/weight_grad/pallas_call | solution.py:265
  220.8 6.1 %collective-permute-done.22.refs_3_ = bf16[256,1024]{1,0:T(8,128)(2,1)S(1)} collective-permute-done((bf16[256,1024]{1,0:T(8,128)(2,1)S(1)}, bf16[256,1024]{1,0:T(8,128)(2,1)S(1)}, u32[]{:S(2)}, u32[]{:S(2)}) %collective-permute-start.22) | collective-permute-done | bytes 524320 | tf_op jit(solution)/shard_map/ppermute | solution.py:29
  232.3 7.6 %packed.1 = (bf16[2048,256]{1,0:T(8,128)(2,1)S(1)}, bf16[2048,256]{1,0:T(8,128)(2,1)S(1)}, bf16[2048,256]{1,0:T(8,128)(2,1)S(1)}) custom-call(bf16[2048,1024]{1,0:T(8,128)(2,1)S(1)} %copy-done.4, bf16[2048,1024]{1,0:T(8,128)(2,1)S(1)} %copy-done.6, bf16[1024,768]{1,0:T(8,128)(2,1)S(1)} %dynamic-slice_bitcast_fusion.wx_ref.refs_6_, ...), custom_call_target="tpu_custom_call" | custom-call | tf_op jit(solution)/shard_map/packed/pallas_call | solution.py:93
  256.4 15.2 %attention.1 = (bf16[4,512,256]{2,1,0:T(8,128)(2,1)S(1)}, bf16[4,512,768]{2,1,0:T(8,128)(2,1)}, f32[1,768]{1,0:T(1,128)S(1)}) custom-call(bf16[4,512,256]{2,1,0:T(8,128)(2,1)S(1)} %bitcast.62, bf16[4,512,256]{2,1,0:T(8,128)(2,1)S(1)} %bitcast.63, bf16[4,512,256]{2,1,0:T(8,128)(2,1)S(1)} %bitcast.64, bf16[4,512,256]{2,1,0:T(8,128)(2,1)S(1)} %bitcast.65, ...), custom_call_target="tpu_custom_call" | custom-call | tf_op jit(solution)/shard_map/attention/pallas_call | solution.py:392
  294.2 6.7 %weight_grad.13 = (bf16[512,1024]{1,0:T(8,128)(2,1)}, bf16[512,1024]{1,0:T(8,128)(2,1)}) custom-call(bf16[2048,768]{1,0:T(8,128)(2,1)S(1)} %bitcast.54, bf16[2048,1024]{1,0:T(8,128)(2,1)S(1)} %copy-done.7, bf16[2048,256]{1,0:T(8,128)(2,1)S(1)} %bitcast.56, bf16[2048,1024]{1,0:T(8,128)(2,1)S(1)} %copy-done.15), custom_call_target="tpu_custom_call" | custom-call | tf_op jit(solution)/shard_map/weight_grad/pallas_call | solution.py:265
  311.8 15.3 %norm_grad.2 = (bf16[1024,2048]{1,0:T(8,128)(2,1)}, f32[4,2048]{1,0:T(4,128)}) custom-call(s32[1]{0:T(128)} %bitcast.4._, bf16[1024,1024]{1,0:T(8,128)(2,1)} %copy-done.85, bf16[1024,1024]{1,0:T(8,128)(2,1)} %pad_maximum_fusion.refs_1_, f32[4,1024]{1,0:T(4,128)} %copy-done.98, f32[4,1024]{1,0:T(4,128)} %copy-done.100, bf16[2048,768]{1,0:T(8,128)(2,1)} %bitcast.51, ...), custom_call_target="tpu_custom_call" | custom-call | tf_op jit(solution)/shard_map/norm_grad/pallas_call | solution.py:93
  335.9 15.8 %norm_grad.3 = (bf16[1024,2048]{1,0:T(8,128)(2,1)}, f32[4,2048]{1,0:T(4,128)}) custom-call(s32[1]{0:T(128)} %bitcast.4._, bf16[1024,1024]{1,0:T(8,128)(2,1)} %copy-done.86, bf16[1024,1024]{1,0:T(8,128)(2,1)} %copy-done.87, f32[4,1024]{1,0:T(4,128)} %copy-done.98, f32[4,1024]{1,0:T(4,128)} %copy-done.100, bf16[2048,768]{1,0:T(8,128)(2,1)} %bitcast.52, ...), custom_call_target="tpu_custom_call" | custom-call | tf_op jit(solution)/shard_map/norm_grad/pallas_call | solution.py:93
  375.7 7.4 %mixed.2 = bf16[1024,2048]{1,0:T(8,128)(2,1)S(1)} custom-call(s32[1]{0:T(128)} %bitcast.4._, bf16[2048,256]{1,0:T(8,128)(2,1)S(1)} %bitcast.57, bf16[2048,1024]{1,0:T(8,128)(2,1)S(1)} %copy-done.2, bf16[256,1024]{1,0:T(8,128)(2,1)S(1)} %copy-done.28, bf16[256,1024]{1,0:T(8,128)(2,1)S(1)} %copy-done.59, bf16[1024,1024]{1,0:T(8,128)(2,1)S(1)} %copy-done.17, ...), custom_call_target="tpu_custom_call" | custom-call | tf_op jit(solution)/shard_map/mixed/pallas_call | solution.py:93
  402.4 7.5 %mixed.3.refs_0_ = bf16[1024,2048]{1,0:T(8,128)(2,1)S(1)} custom-call(s32[1]{0:T(128)} %bitcast.4._, bf16[2048,256]{1,0:T(8,128)(2,1)S(1)} %bitcast.58, bf16[2048,1024]{1,0:T(8,128)(2,1)S(1)} %copy-done.2, bf16[256,1024]{1,0:T(8,128)(2,1)S(1)} %copy-done.28, bf16[256,1024]{1,0:T(8,128)(2,1)S(1)} %copy-done.60, bf16[1024,1024]{1,0:T(8,128)(2,1)S(1)} %copy-done.18, ...), custom_call_target="tpu_custom_call" | custom-call | tf_op jit(solution)/shard_map/mixed/pallas_call | solution.py:93
  417.8 6.8 %collective-permute-done.47.refs_2_.refs_0_ = bf16[512,1024]{1,0:T(8,128)(2,1)} collective-permute-done((bf16[512,1024]{1,0:T(8,128)(2,1)}, bf16[512,1024]{1,0:T(8,128)(2,1)}, u32[]{:S(2)}, u32[]{:S(2)}) %collective-permute-start.47) | collective-permute-done | bytes 1048608 | tf_op jit(solution)/shard_map/ppermute | solution.py:769
  442.5 9.4 %out_grad.1 = f32[2048,1024]{1,0:T(8,128)} custom-call(s32[2]{0:T(128)} %pad_add_fusion.meta_ref, bf16[512,1024]{1,0:T(8,128)(2,1)} %copy-done.31, bf16[512,1024]{1,0:T(8,128)(2,1)} %copy-done.61, bf16[512,1024]{1,0:T(8,128)(2,1)} %copy-done.33, bf16[512,1024]{1,0:T(8,128)(2,1)} %copy-done.62, bf16[512,1024]{1,0:T(8,128)(2,1)} %collective-permute-done.31.refs_4_, ...), custom_call_target="tpu_custom_call" | custom-call | tf_op jit(solution)/shard_map/out_grad/pallas_call | solution.py:493
  504.0 7.7 %qkv_grad.1 = f32[1024,2,768]{2,1,0:T(2,128)} custom-call(s32[2]{0:T(128)} %pad_add_fusion.2.meta_ref, bf16[512,1024]{1,0:T(8,128)(2,1)} %collective-permute-done.41.refs_2_.refs_0_, bf16[512,1024]{1,0:T(8,128)(2,1)} %get-tuple-element.799.refs_1_, bf16[512,1024]{1,0:T(8,128)(2,1)} %collective-permute-done.47.refs_2_.refs_0_, ...), custom_call_target="tpu_custom_call" | custom-call | tf_op jit(solution)/shard_map/qkv_grad/pallas_call | solution.py:493
  (448 shorter events, 306.4 us)
Async XLA Ops:
  7.2 99.9 %all-gather.3.cloned.1.call-start = ((), (), s32[]{:S(2)}) async-start(), calls=%async_computation | async-start | bytes 5242880 | tf_op jit(solution)/shard_map/all_gather | solution.py:844
  7.2 28.9 %collective-permute-start.3 = (bf16[512,1024]{1,0:T(8,128)(2,1)}, bf16[512,1024]{1,0:T(8,128)(2,1)S(1)}, u32[]{:S(2)}, u32[]{:S(2)}) collective-permute-start(bf16[512,1024]{1,0:T(8,128)(2,1)} %x.2), channel_id=1, source_target_pairs={{0,1},{1,0},{2,3},{3,2},{4,5},{5,4},{6,7},{7,6},{8,9},{9,8},{10,11... | collective-permute-start | bytes 3145736 | tf_op jit(solution)/shard_map/ppermute | solution.py:33
  7.8 28.4 %collective-permute-start.2 = (bf16[512,1024]{1,0:T(8,128)(2,1)}, bf16[512,1024]{1,0:T(8,128)(2,1)}, u32[]{:S(2)}, u32[]{:S(2)}) collective-permute-start(bf16[512,1024]{1,0:T(8,128)(2,1)} %x.2), channel_id=1, source_target_pairs={{0,2},{1,3},{2,0},{3,1},{4,6},{5,7},{6,4},{7,5},{8,10},{9,11},{10,... | collective-permute-start | bytes 3145736 | tf_op jit(solution)/shard_map/ppermute | solution.py:33
  10.4 25.8 %collective-permute-start.1 = (bf16[512,1024]{1,0:T(8,128)(2,1)}, bf16[512,1024]{1,0:T(8,128)(2,1)}, u32[]{:S(2)}, u32[]{:S(2)}) collective-permute-start(bf16[512,1024]{1,0:T(8,128)(2,1)} %x.2), channel_id=1, source_target_pairs={{0,4},{4,0},{1,5},{5,1},{2,6},{6,2},{3,7},{7,3},{8,12},{12,8},{9,1... | collective-permute-start | bytes 3145736 | tf_op jit(solution)/shard_map/ppermute | solution.py:29
  36.3 25.9 %collective-permute-start.5 = (bf16[512,1024]{1,0:T(8,128)(2,1)}, bf16[512,1024]{1,0:T(8,128)(2,1)}, u32[]{:S(2)}, u32[]{:S(2)}) collective-permute-start(bf16[512,1024]{1,0:T(8,128)(2,1)} %collective-permute-done.1.y), channel_id=1, source_target_pairs={{0,2},{1,3},{2,0},{3,1},{4,6},{5,7},{6,4},{7,5},{8,10},{9,11},{10,... | collective-permute-start | bytes 3145736 | tf_op jit(solution)/shard_map/ppermute | solution.py:33
  36.6 25.5 %collective-permute-start.7 = (bf16[512,1024]{1,0:T(8,128)(2,1)}, bf16[512,1024]{1,0:T(8,128)(2,1)}, u32[]{:S(2)}, u32[]{:S(2)}) collective-permute-start(bf16[512,1024]{1,0:T(8,128)(2,1)} %collective-permute-done.2.x), channel_id=1, source_target_pairs={{0,1},{1,0},{2,3},{3,2},{4,5},{5,4},{6,7},{7,6},{8,9},{9,8},{10,11... | collective-permute-start | bytes 3145736 | tf_op jit(solution)/shard_map/ppermute | solution.py:33
  36.8 25.7 %collective-permute-start.4 = (bf16[512,1024]{1,0:T(8,128)(2,1)}, bf16[512,1024]{1,0:T(8,128)(2,1)}, u32[]{:S(2)}, u32[]{:S(2)}) collective-permute-start(bf16[512,1024]{1,0:T(8,128)(2,1)} %constant_dynamic-slice_fusion.5), channel_id=1, source_target_pairs={{0,4},{4,0},{1,5},{5,1},{2,6},{6,2},{3,7},{7,3},{8,12},{12,8},{9,1... | collective-permute-start | bytes 3145736 | tf_op jit(solution)/shard_map/ppermute | solution.py:29
  62.5 89.8 %all-gather.5.cloned.1.call-start = ((), (), s32[]{:S(2)}) async-start(), calls=%async_computation.1 | async-start | bytes 5242880 | tf_op jit(solution)/shard_map/all_gather | solution.py:844
  62.6 25.9 %collective-permute-start.9 = (bf16[512,1024]{1,0:T(8,128)(2,1)}, bf16[512,1024]{1,0:T(8,128)(2,1)}, u32[]{:S(2)}, u32[]{:S(2)}) collective-permute-start(bf16[512,1024]{1,0:T(8,128)(2,1)} %constant_dynamic-slice_fusion.6), channel_id=1, source_target_pairs={{0,4},{4,0},{1,5},{5,1},{2,6},{6,2},{3,7},{7,3},{8,12},{12,8},{9,1... | collective-permute-start | bytes 3145736 | tf_op jit(solution)/shard_map/ppermute | solution.py:29
  88.5 24.8 %collective-permute-start.10 = (bf16[512,1024]{1,0:T(8,128)(2,1)S(1)}, bf16[512,1024]{1,0:T(8,128)(2,1)}, u32[]{:S(2)}, u32[]{:S(2)}) collective-permute-start(bf16[512,1024]{1,0:T(8,128)(2,1)S(1)} %copy-done.82), channel_id=1, source_target_pairs={{0,4},{4,0},{1,5},{5,1},{2,6},{6,2},{3,7},{7,3},{8,12},{12,8},{9,1... | collective-permute-start | bytes 3145736 | tf_op jit(solution)/shard_map/ppermute | solution.py:29
  115.2 24.8 %collective-permute-start.11 = (bf16[512,1024]{1,0:T(8,128)(2,1)}, bf16[512,1024]{1,0:T(8,128)(2,1)}, u32[]{:S(2)}, u32[]{:S(2)}) collective-permute-start(bf16[512,1024]{1,0:T(8,128)(2,1)} %weight_grad.7), channel_id=1, source_target_pairs={{0,8},{24,16},{1,9},{25,17},{2,10},{26,18},{3,11},{27,19},{4,12},{... | collective-permute-start | bytes 3145736 | tf_op jit(solution)/shard_map/ppermute | solution.py:769
  145.0 26.4 %collective-permute-start.14 = (bf16[512,1024]{1,0:T(8,128)(2,1)}, bf16[512,1024]{1,0:T(8,128)(2,1)}, u32[]{:S(2)}, u32[]{:S(2)}) collective-permute-start(bf16[512,1024]{1,0:T(8,128)(2,1)} %weight_grad.8.refs_1_), channel_id=1, source_target_pairs={{0,8},{24,16},{1,9},{25,17},{2,10},{26,18},{3,11},{27,19},{4,12},{... | collective-permute-start | bytes 3145736 | tf_op jit(solution)/shard_map/ppermute | solution.py:769
  175.2 24.6 %collective-permute-start.16 = (bf16[512,1024]{1,0:T(8,128)(2,1)S(1)}, bf16[512,1024]{1,0:T(8,128)(2,1)S(1)}, u32[]{:S(2)}, u32[]{:S(2)}) collective-permute-start(bf16[512,1024]{1,0:T(8,128)(2,1)S(1)} %get-tuple-element.533.refs_3_), channel_id=1, source_target_pairs={{8,16},{16,8},{9,17},{17,9},{10,18},{18,10},{11,19},{19,11},{12,20... | collective-permute-start | bytes 3145736 | tf_op jit(solution)/shard_map/ppermute | solution.py:769
  200.8 26.2 %collective-permute-start.19 = (bf16[512,1024]{1,0:T(8,128)(2,1)S(1)}, bf16[512,1024]{1,0:T(8,128)(2,1)S(1)}, u32[]{:S(2)}, u32[]{:S(2)}) collective-permute-start(bf16[512,1024]{1,0:T(8,128)(2,1)S(1)} %get-tuple-element.554.refs_3_), channel_id=1, source_target_pairs={{8,16},{16,8},{9,17},{17,9},{10,18},{18,10},{11,19},{19,11},{12,20... | collective-permute-start | bytes 3145736 | tf_op jit(solution)/shard_map/ppermute | solution.py:769
  201.6 25.4 %collective-permute-start.20 = (bf16[512,1024]{1,0:T(8,128)(2,1)S(1)}, bf16[512,1024]{1,0:T(8,128)(2,1)S(1)}, u32[]{:S(2)}, u32[]{:S(2)}) collective-permute-start(bf16[512,1024]{1,0:T(8,128)(2,1)S(1)} %get-tuple-element.736.refs_3_), channel_id=1, source_target_pairs={{0,8},{24,16},{8,0},{16,24},{1,9},{25,17},{9,1},{17,25},{2,10},{26... | collective-permute-start | bytes 3145736 | tf_op jit(solution)/shard_map/ppermute | solution.py:769
  332.6 25.1 %collective-permute-start.37 = (bf16[512,1024]{1,0:T(8,128)(2,1)}, bf16[512,1024]{1,0:T(8,128)(2,1)}, u32[]{:S(2)}, u32[]{:S(2)}) collective-permute-start(bf16[512,1024]{1,0:T(8,128)(2,1)} %get-tuple-element.770.refs_3_), channel_id=1, source_target_pairs={{0,8},{24,16},{8,0},{16,24},{1,9},{25,17},{9,1},{17,25},{2,10},{26... | collective-permute-start | bytes 3145736 | tf_op jit(solution)/shard_map/ppermute | solution.py:769
  364.4 25.8 %collective-permute-start.39 = (bf16[512,1024]{1,0:T(8,128)(2,1)}, bf16[512,1024]{1,0:T(8,128)(2,1)}, u32[]{:S(2)}, u32[]{:S(2)}) collective-permute-start(bf16[512,1024]{1,0:T(8,128)(2,1)} %get-tuple-element.693.refs_3_), channel_id=1, source_target_pairs={{8,16},{16,8},{9,17},{17,9},{10,18},{18,10},{11,19},{19,11},{12,20... | collective-permute-start | bytes 3145736 | tf_op jit(solution)/shard_map/ppermute | solution.py:769
  398.8 25.9 %collective-permute-start.47 = (bf16[512,1024]{1,0:T(8,128)(2,1)}, bf16[512,1024]{1,0:T(8,128)(2,1)}, u32[]{:S(2)}, u32[]{:S(2)}) collective-permute-start(bf16[512,1024]{1,0:T(8,128)(2,1)} %get-tuple-element.808.refs_3_.refs_1_), channel_id=1, source_target_pairs={{0,8},{24,16},{8,0},{16,24},{1,9},{25,17},{9,1},{17,25},{2,10},{26... | collective-permute-start | bytes 3145736 | tf_op jit(solution)/shard_map/ppermute | solution.py:769
  400.1 25.3 %collective-permute-start.48 = (bf16[256,2048]{1,0:T(8,128)(2,1)}, bf16[256,2048]{1,0:T(8,128)(2,1)}, u32[]{:S(2)}, u32[]{:S(2)}) collective-permute-start(bf16[256,2048]{1,0:T(8,128)(2,1)} %rowwise.32), channel_id=1, source_target_pairs={{0,2},{1,3},{2,0},{3,1},{4,6},{5,7},{6,4},{7,5},{8,10},{9,11},{10,... | collective-permute-start | bytes 3145736 | tf_op jit(solution)/shard_map/ppermute | solution.py:33
  432.2 28.3 %collective-permute-start.52 = (bf16[512,1024]{1,0:T(8,128)(2,1)}, bf16[512,1024]{1,0:T(8,128)(2,1)}, u32[]{:S(2)}, u32[]{:S(2)}) collective-permute-start(bf16[512,1024]{1,0:T(8,128)(2,1)} %get-tuple-element.744), channel_id=1, source_target_pairs={{0,4},{4,0},{1,5},{5,1},{2,6},{6,2},{3,7},{7,3},{8,12},{12,8},{9,1... | collective-permute-start | bytes 3145736 | tf_op jit(solution)/shard_map/ppermute | solution.py:29
  433.4 27.1 %collective-permute-start.49 = (bf16[512,1024]{1,0:T(8,128)(2,1)S(1)}, bf16[512,1024]{1,0:T(8,128)(2,1)}, u32[]{:S(2)}, u32[]{:S(2)}) collective-permute-start(bf16[512,1024]{1,0:T(8,128)(2,1)S(1)} %get-tuple-element.750.refs_2_), channel_id=1, source_target_pairs={{8,16},{16,8},{9,17},{17,9},{10,18},{18,10},{11,19},{19,11},{12,20... | collective-permute-start | bytes 3145736 | tf_op jit(solution)/shard_map/ppermute | solution.py:769
  435.0 25.5 %collective-permute-start.51 = (bf16[512,1024]{1,0:T(8,128)(2,1)S(1)}, bf16[512,1024]{1,0:T(8,128)(2,1)S(1)}, u32[]{:S(2)}, u32[]{:S(2)}) collective-permute-start(bf16[512,1024]{1,0:T(8,128)(2,1)S(1)} %get-tuple-element.803.refs_5_), channel_id=1, source_target_pairs={{0,8},{24,16},{8,0},{16,24},{1,9},{25,17},{9,1},{17,25},{2,10},{26... | collective-permute-start | bytes 3145736 | tf_op jit(solution)/shard_map/ppermute | solution.py:769
  464.8 25.1 %collective-permute-start.56 = (bf16[512,1024]{1,0:T(8,128)(2,1)S(1)}, bf16[512,1024]{1,0:T(8,128)(2,1)}, u32[]{:S(2)}, u32[]{:S(2)}) collective-permute-start(bf16[512,1024]{1,0:T(8,128)(2,1)S(1)} %get-tuple-element.805.refs_7_.refs_3_), channel_id=1, source_target_pairs={{8,0},{16,24},{9,1},{17,25},{10,2},{18,26},{11,3},{19,27},{12,4},{... | collective-permute-start | bytes 3145736 | tf_op jit(solution)/shard_map/ppermute | solution.py:769
  491.5 27.1 %collective-permute-start.61 = (bf16[512,1024]{1,0:T(8,128)(2,1)S(1)}, bf16[512,1024]{1,0:T(8,128)(2,1)S(1)}, u32[]{:S(2)}, u32[]{:S(2)}) collective-permute-start(bf16[512,1024]{1,0:T(8,128)(2,1)S(1)} %add_convert_fusion.refs_3_), channel_id=1, source_target_pairs={{8,0},{16,24},{9,1},{17,25},{10,2},{18,26},{11,3},{19,27},{12,4},{... | collective-permute-start | bytes 3145736 | tf_op jit(solution)/shard_map/ppermute | solution.py:769
  (151 other events, 1780.6 us)
Sparse Core Ops, SparseCore 0:
  62.6 35.9 all-gather.2
  113.5 35.9 all-gather.4

commit v4 on v3

--- a/solution.py
+++ b/solution.py
@@ -925,7 +925,7 @@
         return choose(parts[0])(parts[2], parts[1])
 
     compute(z + 5, n.out_oth0_s, choose_part, (n.out_oth0, n.parts))
-    compute(z + 6, n.out_oth1_s, choose_part, (n.out_oth1, n.parts))
+    compute(z + 7, n.out_oth1_s, choose_part, (n.out_oth1, n.parts))
     send(z + 6, n.out_oth0_y, swap_row, n.out_oth0_s)
     send(z + 9, n.out_oth1_y, swap_row, n.out_oth1_s)
 

time: 545 us -> 543 us (level)
    unnamed x224 -> x220, local copies, waits for them, and re-layouts: 33.5 us -> 30 us
  transfers between devices with their start and end apart: 66 -> 66, of which waited for: 26 -> 28; matrix products, arithmetic and copies ran while one was open for 10% -> 10% of each run, Pallas kernels for 41% -> 41%
where the time goes in v4:
time: 543 us; the launch traced here: 533 us
  Pallas kernels  241 us (44%)
  starting transfers between devices  97.9 us (18%)
  waiting for transfers between devices  91.3 us (17%)
  local copies, waits for them, and re-layouts  54.9 us (10%)
  other arithmetic  28.7 us (5%)
  between operations  15.6 us (3%)
    pallas_call x7, Pallas kernels, call(): pl.pallas_call(kernel if col is None else lambda _, *refs: kernel(*refs),...  81.2 us
    ppermute x29, starting transfers between devices, send(): value = lax.ppermute(tie(beats.env[source], beats.token), 'dp', pairs)  62.4 us
    pallas_call x21, Pallas kernels, rowwise(): pl.pallas_call(kernel, grid_spec=pltpu.PrefetchScalarGridSpec(num_scalar_...  50.2 us
    pallas_call x7, Pallas kernels, weight_grad(): pl.pallas_call(kernel, grid=(first[-1],), out_shape=tuple((jax.ShapeDtype...  46.7 us
    ppermute x21, waiting for transfers between devices, swap_row(): return lax.ppermute(value, 'row', [(0, 1), (1, 0)])  39.3 us
    ppermute x29, waiting for transfers between devices, send(): value = lax.ppermute(tie(beats.env[source], beats.token), 'dp', pairs)  34.9 us
    pallas_call x5, Pallas kernels, assemble(): pl.pallas_call(kernel, grid_spec=pltpu.PrefetchScalarGridSpec(num_scalar_...  30 us
    unnamed x220, local copies, waits for them, and re-layouts  30 us
  transfers between devices with their start and end apart: 66, of which 28 were waited for; matrix products, arithmetic and copies ran while one was open for 10% of the time, Pallas kernels for 41%

profile of v4, /device:TPU:0, one launch (start us, length us, event | category | flops | bytes accessed | tf_op | source)
XLA Modules:
  0.0 532.6 jit_solution(9915515091480087493)
XLA Ops:
  28.3 7.8 %collective-permute-done.gy.refs_3_ = f32[4,1024]{1,0:T(4,128)S(1)} collective-permute-done((f32[4,1024]{1,0:T(4,128)S(1)}, f32[4,1024]{1,0:T(4,128)S(1)}, u32[]{:S(2)}, u32[]{:S(2)}) %collective-permute-start) | collective-permute-done | bytes 16416 | tf_op jit(solution)/shard_map/ppermute | solution.py:29
  49.9 12.2 %collective-permute-done.5.y = bf16[512,1024]{1,0:T(8,128)(2,1)} collective-permute-done((bf16[512,1024]{1,0:T(8,128)(2,1)}, bf16[512,1024]{1,0:T(8,128)(2,1)}, u32[]{:S(2)}, u32[]{:S(2)}) %collective-permute-start.5) | collective-permute-done | bytes 1048608 | tf_op jit(solution)/shard_map/ppermute | solution.py:33
  82.0 6.5 %collective-permute-done.9.wy1_ref.refs_10_ = bf16[512,1024]{1,0:T(8,128)(2,1)} collective-permute-done((bf16[512,1024]{1,0:T(8,128)(2,1)}, bf16[512,1024]{1,0:T(8,128)(2,1)}, u32[]{:S(2)}, u32[]{:S(2)}) %collective-permute-start.9) | collective-permute-done | bytes 1048608 | tf_op jit(solution)/shard_map/ppermute | solution.py:29
  90.8 16.2 %pre_act.1 = (bf16[2048,1024]{1,0:T(8,128)(2,1)}, bf16[2048,1024]{1,0:T(8,128)(2,1)}) custom-call(bf16[2048,1024]{1,0:T(8,128)(2,1)} %get-tuple-element.538.x_ref.refs_0_, bf16[2048,1024]{1,0:T(8,128)(2,1)} %get-tuple-element.542.y_ref.refs_0_, bf16[1024,1024]{1,0:T(8,128)(2,1)} %constant_dynamic-slice_fusion.4.wx_ref.refs_8_, ...), custom_call_target="tpu_custom_call" | custom-call | tf_op jit(solution)/shard_map/pre_act/pallas_call | solution.py:93
  107.1 6.0 %weight_grad.7 = bf16[512,1024]{1,0:T(8,128)(2,1)} custom-call(bf16[2048,1024]{1,0:T(8,128)(2,1)} %get-tuple-element.501.refs_0_.refs_1_, bf16[2048,1024]{1,0:T(8,128)(2,1)} %all-gather.3.cloned.1.call-done.refs_1_.gx_ref.refs_3_), custom_call_target="tpu_custom_call" | custom-call | tf_op jit(solution)/shard_map/weight_grad/pallas_call | solution.py:265
  120.1 6.6 %weight_grad.8.refs_1_ = bf16[512,1024]{1,0:T(8,128)(2,1)} custom-call(bf16[2048,1024]{1,0:T(8,128)(2,1)} %get-tuple-element.501.refs_0_.refs_1_, bf16[2048,1024]{1,0:T(8,128)(2,1)} %all-gather.3.cloned.1.call-done.refs_1_.gx_ref.refs_3_), custom_call_target="tpu_custom_call" | custom-call | tf_op jit(solution)/shard_map/weight_grad/pallas_call | solution.py:265
  145.0 7.3 %collective-permute-start.14 = (bf16[512,1024]{1,0:T(8,128)(2,1)}, bf16[512,1024]{1,0:T(8,128)(2,1)}, u32[]{:S(2)}, u32[]{:S(2)}) collective-permute-start(bf16[512,1024]{1,0:T(8,128)(2,1)} %weight_grad.8.refs_1_), channel_id=1, source_target_pairs={{0,8},{24,16},{1,9},{25,17},{2,10},{26,18},{3,11},{27,19},{4,12},{... | collective-permute-start | bytes 3145736 | tf_op jit(solution)/shard_map/ppermute | solution.py:769
  152.3 9.1 %weight_grad.9 = (bf16[512,1024]{1,0:T(8,128)(2,1)}, bf16[512,1024]{1,0:T(8,128)(2,1)}) custom-call(bf16[2048,1024]{1,0:T(8,128)(2,1)} %get-tuple-element.501.refs_0_.refs_1_, bf16[2048,1024]{1,0:T(8,128)(2,1)} %all-gather.5.cloned.1.call-done.refs_1_.gy_ref.refs_3_), custom_call_target="tpu_custom_call" | custom-call | tf_op jit(solution)/shard_map/weight_grad/pallas_call | solution.py:265
  161.4 5.8 %collective-permute-done.15.wy1_ref.refs_6_ = bf16[512,1024]{1,0:T(8,128)(2,1)} collective-permute-done((bf16[512,1024]{1,0:T(8,128)(2,1)}, bf16[512,1024]{1,0:T(8,128)(2,1)}, u32[]{:S(2)}, u32[]{:S(2)}) %collective-permute-start.15) | collective-permute-done | bytes 1048608 | tf_op jit(solution)/shard_map/ppermute | solution.py:29
  185.2 11.3 %pre_grad.1 = (bf16[2048,1024]{1,0:T(8,128)(2,1)S(1)}, f32[1,1024]{1,0:T(1,128)S(1)}) custom-call(bf16[2048,1024]{1,0:T(8,128)(2,1)S(1)} %copy-done.10, bf16[2048,1024]{1,0:T(8,128)(2,1)S(1)} %copy-done.14, bf16[1024,1024]{1,0:T(8,128)(2,1)S(1)} %copy-done.16, bf16[512,1024]{1,0:T(8,128)(2,1)S(1)} %copy-done.22, ...), custom_call_target="tpu_custom_call" | custom-call | tf_op jit(solution)/shard_map/pre_grad/pallas_call | solution.py:93
  208.1 5.9 %weight_grad.10 = (bf16[512,1024]{1,0:T(8,128)(2,1)S(1)}, bf16[512,1024]{1,0:T(8,128)(2,1)S(1)}) custom-call(bf16[2048,1024]{1,0:T(8,128)(2,1)S(1)} %copy-done.8, bf16[2048,1024]{1,0:T(8,128)(2,1)S(1)} %get-tuple-element.539.refs_1_.refs_5_), custom_call_target="tpu_custom_call" | custom-call | tf_op jit(solution)/shard_map/weight_grad/pallas_call | solution.py:265
  214.1 6.8 %weight_grad.11 = (bf16[512,1024]{1,0:T(8,128)(2,1)S(1)}, bf16[512,1024]{1,0:T(8,128)(2,1)}) custom-call(bf16[2048,1024]{1,0:T(8,128)(2,1)S(1)} %copy-done.9, bf16[2048,1024]{1,0:T(8,128)(2,1)S(1)} %get-tuple-element.539.refs_1_.refs_5_), custom_call_target="tpu_custom_call" | custom-call | tf_op jit(solution)/shard_map/weight_grad/pallas_call | solution.py:265
  220.8 6.1 %collective-permute-done.22.refs_3_ = bf16[256,1024]{1,0:T(8,128)(2,1)S(1)} collective-permute-done((bf16[256,1024]{1,0:T(8,128)(2,1)S(1)}, bf16[256,1024]{1,0:T(8,128)(2,1)S(1)}, u32[]{:S(2)}, u32[]{:S(2)}) %collective-permute-start.22) | collective-permute-done | bytes 524320 | tf_op jit(solution)/shard_map/ppermute | solution.py:29
  232.3 7.6 %packed.1 = (bf16[2048,256]{1,0:T(8,128)(2,1)S(1)}, bf16[2048,256]{1,0:T(8,128)(2,1)S(1)}, bf16[2048,256]{1,0:T(8,128)(2,1)S(1)}) custom-call(bf16[2048,1024]{1,0:T(8,128)(2,1)S(1)} %copy-done.4, bf16[2048,1024]{1,0:T(8,128)(2,1)S(1)} %copy-done.6, bf16[1024,768]{1,0:T(8,128)(2,1)S(1)} %dynamic-slice_bitcast_fusion.wx_ref.refs_6_, ...), custom_call_target="tpu_custom_call" | custom-call | tf_op jit(solution)/shard_map/packed/pallas_call | solution.py:93
  256.4 15.3 %attention.1 = (bf16[4,512,256]{2,1,0:T(8,128)(2,1)S(1)}, bf16[4,512,768]{2,1,0:T(8,128)(2,1)}, f32[1,768]{1,0:T(1,128)S(1)}) custom-call(bf16[4,512,256]{2,1,0:T(8,128)(2,1)S(1)} %bitcast.62, bf16[4,512,256]{2,1,0:T(8,128)(2,1)S(1)} %bitcast.63, bf16[4,512,256]{2,1,0:T(8,128)(2,1)S(1)} %bitcast.64, bf16[4,512,256]{2,1,0:T(8,128)(2,1)S(1)} %bitcast.65, ...), custom_call_target="tpu_custom_call" | custom-call | tf_op jit(solution)/shard_map/attention/pallas_call | solution.py:392
  291.4 6.7 %weight_grad.13 = (bf16[512,1024]{1,0:T(8,128)(2,1)}, bf16[512,1024]{1,0:T(8,128)(2,1)}) custom-call(bf16[2048,768]{1,0:T(8,128)(2,1)S(1)} %bitcast.54, bf16[2048,1024]{1,0:T(8,128)(2,1)S(1)} %copy-done.7, bf16[2048,256]{1,0:T(8,128)(2,1)S(1)} %bitcast.56, bf16[2048,1024]{1,0:T(8,128)(2,1)S(1)} %copy-done.15), custom_call_target="tpu_custom_call" | custom-call | tf_op jit(solution)/shard_map/weight_grad/pallas_call | solution.py:265
  311.3 15.4 %norm_grad.2 = (bf16[1024,2048]{1,0:T(8,128)(2,1)}, f32[4,2048]{1,0:T(4,128)}) custom-call(s32[1]{0:T(128)} %bitcast.4._, bf16[1024,1024]{1,0:T(8,128)(2,1)} %copy-done.82, bf16[1024,1024]{1,0:T(8,128)(2,1)} %pad_maximum_fusion.refs_1_, f32[4,1024]{1,0:T(4,128)} %copy-done.96, f32[4,1024]{1,0:T(4,128)} %copy-done.98, bf16[2048,768]{1,0:T(8,128)(2,1)} %bitcast.51, ...), custom_call_target="tpu_custom_call" | custom-call | tf_op jit(solution)/shard_map/norm_grad/pallas_call | solution.py:93
  334.1 15.8 %norm_grad.3 = (bf16[1024,2048]{1,0:T(8,128)(2,1)}, f32[4,2048]{1,0:T(4,128)}) custom-call(s32[1]{0:T(128)} %bitcast.4._, bf16[1024,1024]{1,0:T(8,128)(2,1)} %copy-done.83, bf16[1024,1024]{1,0:T(8,128)(2,1)} %copy-done.84, f32[4,1024]{1,0:T(4,128)} %copy-done.96, f32[4,1024]{1,0:T(4,128)} %copy-done.98, bf16[2048,768]{1,0:T(8,128)(2,1)} %bitcast.52, ...), custom_call_target="tpu_custom_call" | custom-call | tf_op jit(solution)/shard_map/norm_grad/pallas_call | solution.py:93
  373.2 7.4 %mixed.2 = bf16[1024,2048]{1,0:T(8,128)(2,1)S(1)} custom-call(s32[1]{0:T(128)} %bitcast.4._, bf16[2048,256]{1,0:T(8,128)(2,1)S(1)} %bitcast.57, bf16[2048,1024]{1,0:T(8,128)(2,1)S(1)} %copy-done.2, bf16[256,1024]{1,0:T(8,128)(2,1)S(1)} %copy-done.28, bf16[256,1024]{1,0:T(8,128)(2,1)S(1)} %copy-done.55, bf16[1024,1024]{1,0:T(8,128)(2,1)S(1)} %copy-done.17, ...), custom_call_target="tpu_custom_call" | custom-call | tf_op jit(solution)/shard_map/mixed/pallas_call | solution.py:93
  400.3 7.5 %mixed.3.refs_0_ = bf16[1024,2048]{1,0:T(8,128)(2,1)S(1)} custom-call(s32[1]{0:T(128)} %bitcast.4._, bf16[2048,256]{1,0:T(8,128)(2,1)S(1)} %bitcast.58, bf16[2048,1024]{1,0:T(8,128)(2,1)S(1)} %copy-done.2, bf16[256,1024]{1,0:T(8,128)(2,1)S(1)} %copy-done.28, bf16[256,1024]{1,0:T(8,128)(2,1)S(1)} %copy-done.56, bf16[1024,1024]{1,0:T(8,128)(2,1)S(1)} %copy-done.18, ...), custom_call_target="tpu_custom_call" | custom-call | tf_op jit(solution)/shard_map/mixed/pallas_call | solution.py:93
  415.7 6.2 %collective-permute-done.47.refs_2_.refs_0_ = bf16[512,1024]{1,0:T(8,128)(2,1)} collective-permute-done((bf16[512,1024]{1,0:T(8,128)(2,1)}, bf16[512,1024]{1,0:T(8,128)(2,1)}, u32[]{:S(2)}, u32[]{:S(2)}) %collective-permute-start.47) | collective-permute-done | bytes 1048608 | tf_op jit(solution)/shard_map/ppermute | solution.py:769
  439.9 9.4 %out_grad.1 = f32[2048,1024]{1,0:T(8,128)} custom-call(s32[2]{0:T(128)} %pad_add_fusion.meta_ref, bf16[512,1024]{1,0:T(8,128)(2,1)} %copy-done.32, bf16[512,1024]{1,0:T(8,128)(2,1)} %copy-done.57, bf16[512,1024]{1,0:T(8,128)(2,1)} %copy-done.33, bf16[512,1024]{1,0:T(8,128)(2,1)} %copy-done.58, bf16[512,1024]{1,0:T(8,128)(2,1)} %copy-done.92, ...), custom_call_target="tpu_custom_call" | custom-call | tf_op jit(solution)/shard_map/out_grad/pallas_call | solution.py:493
  452.2 5.8 %collective-permute-done.50 = f32[12032]{0:T(1024)S(1)} collective-permute-done((f32[12032]{0:T(1024)S(1)}, f32[12032]{0:T(1024)S(1)}, u32[]{:S(2)}, u32[]{:S(2)}) %collective-permute-start.50) | collective-permute-done | bytes 48160 | tf_op jit(solution)/shard_map/ppermute | solution.py:769
  501.6 7.7 %qkv_grad.1 = f32[1024,2,768]{2,1,0:T(2,128)} custom-call(s32[2]{0:T(128)} %pad_add_fusion.2.meta_ref, bf16[512,1024]{1,0:T(8,128)(2,1)} %collective-permute-done.41.refs_2_.refs_0_, bf16[512,1024]{1,0:T(8,128)(2,1)} %get-tuple-element.799.refs_1_, bf16[512,1024]{1,0:T(8,128)(2,1)} %collective-permute-done.47.refs_2_.refs_0_, ...), custom_call_target="tpu_custom_call" | custom-call | tf_op jit(solution)/shard_map/qkv_grad/pallas_call | solution.py:493
  (444 shorter events, 304.6 us)
Async XLA Ops:
  7.2 99.9 %all-gather.3.cloned.1.call-start = ((), (), s32[]{:S(2)}) async-start(), calls=%async_computation | async-start | bytes 5242880 | tf_op jit(solution)/shard_map/all_gather | solution.py:844
  7.2 28.9 %collective-permute-start.3 = (bf16[512,1024]{1,0:T(8,128)(2,1)}, bf16[512,1024]{1,0:T(8,128)(2,1)S(1)}, u32[]{:S(2)}, u32[]{:S(2)}) collective-permute-start(bf16[512,1024]{1,0:T(8,128)(2,1)} %x.2), channel_id=1, source_target_pairs={{0,1},{1,0},{2,3},{3,2},{4,5},{5,4},{6,7},{7,6},{8,9},{9,8},{10,11... | collective-permute-start | bytes 3145736 | tf_op jit(solution)/shard_map/ppermute | solution.py:33
  7.8 28.4 %collective-permute-start.2 = (bf16[512,1024]{1,0:T(8,128)(2,1)}, bf16[512,1024]{1,0:T(8,128)(2,1)}, u32[]{:S(2)}, u32[]{:S(2)}) collective-permute-start(bf16[512,1024]{1,0:T(8,128)(2,1)} %x.2), channel_id=1, source_target_pairs={{0,2},{1,3},{2,0},{3,1},{4,6},{5,7},{6,4},{7,5},{8,10},{9,11},{10,... | collective-permute-start | bytes 3145736 | tf_op jit(solution)/shard_map/ppermute | solution.py:33
  10.4 25.8 %collective-permute-start.1 = (bf16[512,1024]{1,0:T(8,128)(2,1)}, bf16[512,1024]{1,0:T(8,128)(2,1)}, u32[]{:S(2)}, u32[]{:S(2)}) collective-permute-start(bf16[512,1024]{1,0:T(8,128)(2,1)} %x.2), channel_id=1, source_target_pairs={{0,4},{4,0},{1,5},{5,1},{2,6},{6,2},{3,7},{7,3},{8,12},{12,8},{9,1... | collective-permute-start | bytes 3145736 | tf_op jit(solution)/shard_map/ppermute | solution.py:29
  36.3 25.9 %collective-permute-start.5 = (bf16[512,1024]{1,0:T(8,128)(2,1)}, bf16[512,1024]{1,0:T(8,128)(2,1)}, u32[]{:S(2)}, u32[]{:S(2)}) collective-permute-start(bf16[512,1024]{1,0:T(8,128)(2,1)} %collective-permute-done.1.y), channel_id=1, source_target_pairs={{0,2},{1,3},{2,0},{3,1},{4,6},{5,7},{6,4},{7,5},{8,10},{9,11},{10,... | collective-permute-start | bytes 3145736 | tf_op jit(solution)/shard_map/ppermute | solution.py:33
  36.6 25.5 %collective-permute-start.7 = (bf16[512,1024]{1,0:T(8,128)(2,1)}, bf16[512,1024]{1,0:T(8,128)(2,1)}, u32[]{:S(2)}, u32[]{:S(2)}) collective-permute-start(bf16[512,1024]{1,0:T(8,128)(2,1)} %collective-permute-done.2.x), channel_id=1, source_target_pairs={{0,1},{1,0},{2,3},{3,2},{4,5},{5,4},{6,7},{7,6},{8,9},{9,8},{10,11... | collective-permute-start | bytes 3145736 | tf_op jit(solution)/shard_map/ppermute | solution.py:33
  36.8 25.7 %collective-permute-start.4 = (bf16[512,1024]{1,0:T(8,128)(2,1)}, bf16[512,1024]{1,0:T(8,128)(2,1)}, u32[]{:S(2)}, u32[]{:S(2)}) collective-permute-start(bf16[512,1024]{1,0:T(8,128)(2,1)} %constant_dynamic-slice_fusion.5), channel_id=1, source_target_pairs={{0,4},{4,0},{1,5},{5,1},{2,6},{6,2},{3,7},{7,3},{8,12},{12,8},{9,1... | collective-permute-start | bytes 3145736 | tf_op jit(solution)/shard_map/ppermute | solution.py:29
  62.5 89.7 %all-gather.5.cloned.1.call-start = ((), (), s32[]{:S(2)}) async-start(), calls=%async_computation.1 | async-start | bytes 5242880 | tf_op jit(solution)/shard_map/all_gather | solution.py:844
  62.6 25.9 %collective-permute-start.9 = (bf16[512,1024]{1,0:T(8,128)(2,1)}, bf16[512,1024]{1,0:T(8,128)(2,1)}, u32[]{:S(2)}, u32[]{:S(2)}) collective-permute-start(bf16[512,1024]{1,0:T(8,128)(2,1)} %constant_dynamic-slice_fusion.6), channel_id=1, source_target_pairs={{0,4},{4,0},{1,5},{5,1},{2,6},{6,2},{3,7},{7,3},{8,12},{12,8},{9,1... | collective-permute-start | bytes 3145736 | tf_op jit(solution)/shard_map/ppermute | solution.py:29
  115.2 24.8 %collective-permute-start.11 = (bf16[512,1024]{1,0:T(8,128)(2,1)}, bf16[512,1024]{1,0:T(8,128)(2,1)}, u32[]{:S(2)}, u32[]{:S(2)}) collective-permute-start(bf16[512,1024]{1,0:T(8,128)(2,1)} %weight_grad.7), channel_id=1, source_target_pairs={{0,8},{24,16},{1,9},{25,17},{2,10},{26,18},{3,11},{27,19},{4,12},{... | collective-permute-start | bytes 3145736 | tf_op jit(solution)/shard_map/ppermute | solution.py:769
  145.0 26.4 %collective-permute-start.14 = (bf16[512,1024]{1,0:T(8,128)(2,1)}, bf16[512,1024]{1,0:T(8,128)(2,1)}, u32[]{:S(2)}, u32[]{:S(2)}) collective-permute-start(bf16[512,1024]{1,0:T(8,128)(2,1)} %weight_grad.8.refs_1_), channel_id=1, source_target_pairs={{0,8},{24,16},{1,9},{25,17},{2,10},{26,18},{3,11},{27,19},{4,12},{... | collective-permute-start | bytes 3145736 | tf_op jit(solution)/shard_map/ppermute | solution.py:769
  200.7 26.2 %collective-permute-start.19 = (bf16[512,1024]{1,0:T(8,128)(2,1)S(1)}, bf16[512,1024]{1,0:T(8,128)(2,1)S(1)}, u32[]{:S(2)}, u32[]{:S(2)}) collective-permute-start(bf16[512,1024]{1,0:T(8,128)(2,1)S(1)} %get-tuple-element.554.refs_3_), channel_id=1, source_target_pairs={{8,16},{16,8},{9,17},{17,9},{10,18},{18,10},{11,19},{19,11},{12,20... | collective-permute-start | bytes 3145736 | tf_op jit(solution)/shard_map/ppermute | solution.py:769
  201.6 25.4 %collective-permute-start.20 = (bf16[512,1024]{1,0:T(8,128)(2,1)S(1)}, bf16[512,1024]{1,0:T(8,128)(2,1)S(1)}, u32[]{:S(2)}, u32[]{:S(2)}) collective-permute-start(bf16[512,1024]{1,0:T(8,128)(2,1)S(1)} %get-tuple-element.736.refs_3_), channel_id=1, source_target_pairs={{0,8},{24,16},{8,0},{16,24},{1,9},{25,17},{9,1},{17,25},{2,10},{26... | collective-permute-start | bytes 3145736 | tf_op jit(solution)/shard_map/ppermute | solution.py:769
  301.7 25.1 %collective-permute-start.32 = (bf16[512,1024]{1,0:T(8,128)(2,1)}, bf16[512,1024]{1,0:T(8,128)(2,1)}, u32[]{:S(2)}, u32[]{:S(2)}) collective-permute-start(bf16[512,1024]{1,0:T(8,128)(2,1)} %get-tuple-element.650.refs_3_), channel_id=1, source_target_pairs={{8,16},{16,8},{9,17},{17,9},{10,18},{18,10},{11,19},{19,11},{12,20... | collective-permute-start | bytes 3145736 | tf_op jit(solution)/shard_map/ppermute | solution.py:769
  331.7 25.4 %collective-permute-start.37 = (bf16[512,1024]{1,0:T(8,128)(2,1)}, bf16[512,1024]{1,0:T(8,128)(2,1)}, u32[]{:S(2)}, u32[]{:S(2)}) collective-permute-start(bf16[512,1024]{1,0:T(8,128)(2,1)} %get-tuple-element.770.refs_3_), channel_id=1, source_target_pairs={{0,8},{24,16},{8,0},{16,24},{1,9},{25,17},{9,1},{17,25},{2,10},{26... | collective-permute-start | bytes 3145736 | tf_op jit(solution)/shard_map/ppermute | solution.py:769
  333.2 24.8 %collective-permute-start.38 = (bf16[512,1024]{1,0:T(8,128)(2,1)}, bf16[512,1024]{1,0:T(8,128)(2,1)}, u32[]{:S(2)}, u32[]{:S(2)}) collective-permute-start(bf16[512,1024]{1,0:T(8,128)(2,1)} %get-tuple-element.670), channel_id=1, source_target_pairs={{0,4},{4,0},{1,5},{5,1},{2,6},{6,2},{3,7},{7,3},{8,12},{12,8},{9,1... | collective-permute-start | bytes 3145736 | tf_op jit(solution)/shard_map/ppermute | solution.py:29
  362.6 25.7 %collective-permute-start.39 = (bf16[512,1024]{1,0:T(8,128)(2,1)}, bf16[512,1024]{1,0:T(8,128)(2,1)}, u32[]{:S(2)}, u32[]{:S(2)}) collective-permute-start(bf16[512,1024]{1,0:T(8,128)(2,1)} %get-tuple-element.693.refs_3_), channel_id=1, source_target_pairs={{8,16},{16,8},{9,17},{17,9},{10,18},{18,10},{11,19},{19,11},{12,20... | collective-permute-start | bytes 3145736 | tf_op jit(solution)/shard_map/ppermute | solution.py:769
  395.3 26.6 %collective-permute-start.47 = (bf16[512,1024]{1,0:T(8,128)(2,1)}, bf16[512,1024]{1,0:T(8,128)(2,1)}, u32[]{:S(2)}, u32[]{:S(2)}) collective-permute-start(bf16[512,1024]{1,0:T(8,128)(2,1)} %get-tuple-element.808.refs_3_.refs_1_), channel_id=1, source_target_pairs={{0,8},{24,16},{8,0},{16,24},{1,9},{25,17},{9,1},{17,25},{2,10},{26... | collective-permute-start | bytes 3145736 | tf_op jit(solution)/shard_map/ppermute | solution.py:769
  398.1 25.3 %collective-permute-start.48 = (bf16[256,2048]{1,0:T(8,128)(2,1)}, bf16[256,2048]{1,0:T(8,128)(2,1)}, u32[]{:S(2)}, u32[]{:S(2)}) collective-permute-start(bf16[256,2048]{1,0:T(8,128)(2,1)} %rowwise.32), channel_id=1, source_target_pairs={{0,2},{1,3},{2,0},{3,1},{4,6},{5,7},{6,4},{7,5},{8,10},{9,11},{10,... | collective-permute-start | bytes 3145736 | tf_op jit(solution)/shard_map/ppermute | solution.py:33
  430.1 27.9 %collective-permute-start.52 = (bf16[512,1024]{1,0:T(8,128)(2,1)}, bf16[512,1024]{1,0:T(8,128)(2,1)}, u32[]{:S(2)}, u32[]{:S(2)}) collective-permute-start(bf16[512,1024]{1,0:T(8,128)(2,1)} %get-tuple-element.744), channel_id=1, source_target_pairs={{0,4},{4,0},{1,5},{5,1},{2,6},{6,2},{3,7},{7,3},{8,12},{12,8},{9,1... | collective-permute-start | bytes 3145736 | tf_op jit(solution)/shard_map/ppermute | solution.py:29
  430.9 27.1 %collective-permute-start.49 = (bf16[512,1024]{1,0:T(8,128)(2,1)S(1)}, bf16[512,1024]{1,0:T(8,128)(2,1)}, u32[]{:S(2)}, u32[]{:S(2)}) collective-permute-start(bf16[512,1024]{1,0:T(8,128)(2,1)S(1)} %get-tuple-element.750.refs_2_), channel_id=1, source_target_pairs={{8,16},{16,8},{9,17},{17,9},{10,18},{18,10},{11,19},{19,11},{12,20... | collective-permute-start | bytes 3145736 | tf_op jit(solution)/shard_map/ppermute | solution.py:769
  432.6 25.4 %collective-permute-start.51 = (bf16[512,1024]{1,0:T(8,128)(2,1)S(1)}, bf16[512,1024]{1,0:T(8,128)(2,1)S(1)}, u32[]{:S(2)}, u32[]{:S(2)}) collective-permute-start(bf16[512,1024]{1,0:T(8,128)(2,1)S(1)} %get-tuple-element.803.refs_5_), channel_id=1, source_target_pairs={{0,8},{24,16},{8,0},{16,24},{1,9},{25,17},{9,1},{17,25},{2,10},{26... | collective-permute-start | bytes 3145736 | tf_op jit(solution)/shard_map/ppermute | solution.py:769
  462.4 25.1 %collective-permute-start.56 = (bf16[512,1024]{1,0:T(8,128)(2,1)S(1)}, bf16[512,1024]{1,0:T(8,128)(2,1)}, u32[]{:S(2)}, u32[]{:S(2)}) collective-permute-start(bf16[512,1024]{1,0:T(8,128)(2,1)S(1)} %get-tuple-element.805.refs_7_.refs_3_), channel_id=1, source_target_pairs={{8,0},{16,24},{9,1},{17,25},{10,2},{18,26},{11,3},{19,27},{12,4},{... | collective-permute-start | bytes 3145736 | tf_op jit(solution)/shard_map/ppermute | solution.py:769
  489.1 27.1 %collective-permute-start.61 = (bf16[512,1024]{1,0:T(8,128)(2,1)S(1)}, bf16[512,1024]{1,0:T(8,128)(2,1)S(1)}, u32[]{:S(2)}, u32[]{:S(2)}) collective-permute-start(bf16[512,1024]{1,0:T(8,128)(2,1)S(1)} %add_convert_fusion.refs_3_), channel_id=1, source_target_pairs={{8,0},{16,24},{9,1},{17,25},{10,2},{18,26},{11,3},{19,27},{12,4},{... | collective-permute-start | bytes 3145736 | tf_op jit(solution)/shard_map/ppermute | solution.py:769
  (149 other events, 1793.8 us)
Sparse Core Ops, SparseCore 0:
  62.6 35.9 all-gather.2
  113.5 35.9 all-gather.4
